TPU v7x, 32 devices: a whole 2x2x4 slice. The times are simulated.
32 devices in a mesh: pole: 2 (over y), prow: 1, pcol: 16 (over z, x, core).
Axes of the slice: x: 2, y: 2, z: 4, core: 2. Of those that a mesh axis runs over, the one named last changes fastest.
Arguments:
- anc_inverse: float32 [12288, 6144], P(('pole', 'prow'), 'pcol'), parts along dimension 0, may hold values from -8 to 8
- anc_factor: float32 [12288, 768], P(('pole', 'pcol')), parts along dimension 0, may hold values from -0.078125 to 0.078125
- win_factor: float32 [1536, 768], P('pole'), parts along dimension 0, may hold values from -0.375 to 0.375
- pivot_inverse: float32 [6, 256, 256], P('pole'), parts along dimension 0, may hold values from -6 to 6
- structure: int32 [3, 24], replicated, may hold values 0 or 1
Outputs:
- anc_columns: float32 [12288, 768], P(('pole', 'prow', 'pcol')), parts along dimension 0
- win_inverse: float32 [1536, 768], P('pole'), parts along dimension 0
There are 2 independent parts, one for each index of `pole`. A program takes and returns all parts, laid end to end along the dimension named above; an argument that names none is the same for every part. Nothing has to cross between parts.
All inputs are finite; a program needn't handle non-finite values.
Results may differ from a plain program's by a relative error of at most 0.0001.
Values sent between devices are 32-bit elements; how exact they have to be, the bound alone decides.
No kernel may reach another device: no remote copies, remote signals or barrier semaphores. Data moves between devices by JAX's collectives and lax.ppermute only.
A program may use at most 128 MiB of HBM per device.

v0:
```python
import jax
import jax.numpy as jnp
from jax import lax
from jax.sharding import PartitionSpec as P

precise = lax.Precision.HIGHEST


def product(left, right):
    return jnp.dot(left, right, precision=precise, preferred_element_type=jnp.float32)


def on_device(anc_inverse, anc_factor, win_factor, pivot_inverse, structure):
    row_count = lax.axis_size("prow")
    col_count = lax.axis_size("pcol")
    row_index = lax.axis_index("prow")
    col_index = lax.axis_index("pcol")
    block_rows = anc_inverse.shape[0]
    block_cols = anc_inverse.shape[1]
    steps_total = pivot_inverse.shape[0]
    width = pivot_inverse.shape[1]
    all_cols = anc_factor.shape[1]
    block_count = structure.shape[1]
    ratio_cols = col_count // row_count
    share_rows = block_rows // col_count
    structure_cols = structure.T.astype(jnp.float32)
    global_rows = col_index * block_cols + lax.iota(jnp.int32, block_cols)
    onehot_rows = (
        (global_rows // width)[:, None] == lax.iota(jnp.int32, block_count)[None, :]
    ).astype(jnp.float32)
    kept_rows = product(onehot_rows, structure_cols)
    share_offset = col_index * share_rows
    share_global = (row_index * col_count + col_index) * share_rows + lax.iota(
        jnp.int32, share_rows
    )
    onehot_share = (
        (share_global // width)[:, None] == lax.iota(jnp.int32, block_count)[None, :]
    ).astype(jnp.float32)
    kept_share = product(onehot_share, structure_cols)
    slot_ids = lax.iota(jnp.int32, col_count)
    source_flag = (slot_ids // row_count == col_index - row_index * ratio_cols).astype(jnp.float32)
    pieces = jnp.tile(anc_factor.reshape(row_count, share_rows, all_cols), (ratio_cols, 1, 1))
    outgoing = pieces * source_flag[:, None, None]
    incoming = lax.all_to_all(outgoing, "pcol", split_axis=0, concat_axis=0, tiled=True)
    factor_share = jnp.sum(incoming, axis=0)
    column_store = {}
    share_store = {}
    window_blocks = {}
    for k in range(steps_total - 1, -1, -1):
        first_col = k * width
        factor_now = anc_factor[:, first_col : first_col + width] * kept_rows[:, k : k + 1]
        share_factor = factor_share[:, first_col : first_col + width] * kept_share[:, k : k + 1]
        finished = list(range(k + 1, steps_total))
        if finished:
            stacked = jnp.concatenate([column_store[j] for j in finished], axis=1)
            factor_win = win_factor[first_col + width :, first_col : first_col + width]

        def term_rows(start, count, factor_now=factor_now):
            return product(anc_inverse, factor_now)

        share_image = lax.psum_scatter(
            term_rows(jnp.int32(0), share_rows * lax.axis_size("pcol")),
            "pcol",
            scatter_dimension=0,
            tiled=True,
        )
        if finished:
            share_image = share_image + product(
                lax.dynamic_slice_in_dim(stacked, share_offset, share_rows, 0), factor_win
            )
        share_column = -share_image
        column_now = lax.all_gather(share_column, "pcol", axis=0, tiled=True)
        crossings = [product(share_store[j].T, share_factor) for j in finished]
        pivot_part = product(share_factor.T, share_column)
        cross_sums = []
        if finished:
            cross_total = lax.psum(jnp.stack(crossings), ("prow", "pcol"))
            cross_sums = [cross_total[position] for position in range(len(finished))]
        pivot_sum = lax.psum(pivot_part, ("prow", "pcol"))
        for position, j in enumerate(finished):
            running = cross_sums[position]
            for i in finished:
                running = running + product(
                    window_blocks[j, i],
                    win_factor[i * width : (i + 1) * width, first_col : first_col + width],
                )
            window_blocks[j, k] = -running
            window_blocks[k, j] = -running.T
        pivot_block = pivot_inverse[k] - pivot_sum
        for j in finished:
            pivot_block = pivot_block - product(
                win_factor[j * width : (j + 1) * width, first_col : first_col + width].T,
                window_blocks[j, k],
            )
        window_blocks[k, k] = pivot_block
        column_store[k] = column_now
        share_store[k] = share_column
    anc_columns = jnp.concatenate([share_store[k] for k in range(steps_total)], axis=1)
    win_inverse = jnp.concatenate(
        [
            jnp.concatenate([window_blocks[i, k] for k in range(steps_total)], axis=1)
            for i in range(steps_total)
        ],
        axis=0,
    )
    return (anc_columns, win_inverse)


def solution(mesh):
    in_specs = (
        P(("pole", "prow"), "pcol"),
        P(("pole", "pcol"), None),
        P("pole", None),
        P("pole", None, None),
        P(),
    )
    out_specs = (P(("pole", "prow", "pcol"), None), P("pole", None))
    return jax.shard_map(
        on_device, mesh=mesh, in_specs=in_specs, out_specs=out_specs, check_vma=False
    )
```

profile of v0, /device:TPU:0, one launch (start us, length us, event | category | flops | bytes accessed | tf_op | source)
XLA Modules:
  0.0 905.3 jit_solution(14524148858973868540)
XLA Ops:
  7.2 1.0 fusion.40
  8.2 19.4 %convolution_bitcast_fusion = f32[6144,256]{0,1:T(8,128)} fusion(f32[6144,384]{1,0:T(8,128)} %param.5, f32[384,768]{1,0:T(8,128)} %param.6, f32[384]{0:T(512)S(1)} %get-tuple-element.7), kind=kOutput, calls=%fused_computation.3 | convolution fusion | flops 7247855616 | bytes 16123392 | tf_op jit(solution)/shard_map/dot_general | solution.py:10
  27.9 1.0 copy-done.2
  28.9 19.2 %convolution_bitcast_fusion.1 = f32[6144,256]{0,1:T(8,128)} fusion(f32[6144,384]{1,0:T(8,128)} %param.5, f32[384,768]{1,0:T(8,128)S(1)} %copy-done.2, f32[384]{0:T(512)S(1)} %get-tuple-element.8), kind=kOutput, calls=%fused_computation.4 | convolution fusion | flops 7247855616 | bytes 16123904 | tf_op jit(solution)/shard_map/dot_general | solution.py:10
  48.1 8.4 broadcast_multiply_fusion
  56.5 7.4 all-to-all-start
  63.9 346.9 %reduce-scatter.8.cloned.1.call-done = f32[384,256]{0,1:T(8,128)} async-done(((f32[6144,256]{0,1:T(8,128)}), f32[384,256]{0,1:T(8,128)}) %reduce-scatter.8.cloned.1.call-update) | async-done | bytes 393232 | tf_op jit(solution)/shard_map/reduce_scatter | solution.py:61
  410.8 1.8 neg.30
  412.9 19.2 %convolution_bitcast_fusion.2 = f32[6144,256]{0,1:T(8,128)} fusion(f32[6144,384]{1,0:T(8,128)} %param.5, f32[384,768]{1,0:T(8,128)S(1)} %copy-done.2, f32[384]{0:T(512)S(1)} %get-tuple-element.6), kind=kOutput, calls=%fused_computation.5 | convolution fusion | flops 7247855616 | bytes 16123904 | tf_op jit(solution)/shard_map/dot_general | solution.py:10
  432.2 121.9 %reduce-scatter.6.cloned.1.call-done = f32[384,256]{0,1:T(8,128)} async-done(((f32[6144,256]{0,1:T(8,128)}), f32[384,256]{0,1:T(8,128)}) %reduce-scatter.6.cloned.1.call-update) | async-done | bytes 393232 | tf_op jit(solution)/shard_map/reduce_scatter | solution.py:61
  554.1 64.0 %all-gather.3.cloned.1.call-done = f32[6144,256]{0,1:T(8,128)} async-done(((f32[384,256]{0,1:T(8,128)}), f32[6144,256]{0,1:T(8,128)}) %all-gather.3.cloned.1.call-update) | async-done | bytes 6291472 | tf_op jit(solution)/shard_map/all_gather | solution.py:72
  618.1 2.6 fusion.1
  621.0 84.6 %reduce-scatter.4.cloned.1.call-done = f32[384,256]{0,1:T(8,128)} async-done(((f32[6144,256]{0,1:T(8,128)}), f32[384,256]{0,1:T(8,128)}) %reduce-scatter.4.cloned.1.call-update) | async-done | bytes 393232 | tf_op jit(solution)/shard_map/reduce_scatter | solution.py:61
  705.7 64.0 %all-gather.5.cloned.1.call-done = f32[6144,256]{0,1:T(8,128)} async-done(((f32[384,256]{0,1:T(8,128)}), f32[6144,256]{0,1:T(8,128)}) %all-gather.5.cloned.1.call-update) | async-done | bytes 6291472 | tf_op jit(solution)/shard_map/all_gather | solution.py:72
  769.7 2.4 fusion
  772.1 7.7 reduce_sum.9
  779.8 0.9 convolution_bitcast_fusion.7
  780.7 1.4 fusion.20
  782.1 1.6 fusion.21
  783.7 0.9 convolution_bitcast_fusion.6
  785.4 1.4 fusion.19
  786.8 1.6 fusion.11
  788.4 0.8 copy.42
  789.3 1.4 copy.32
  790.7 93.1 %all-reduce.3.cloned.1.call-done = (f32[256,256]{1,0:T(8,128)}, f32[256,256]{1,0:T(8,128)}, f32[2,256,256]{1,2,0:T(8,128)}, f32[256,256]{0,1:T(8,128)}, f32[256,256]{1,0:T(8,128)}) async-done(((f32[256,256]{1,0:T(8,128)}, f32[256,256]{1,0:T(8,128)}, f32[2,256,256]{1,2,0:T(8,128)}, f32[256,256]{0,1:T(8,128)}, f32[256,256]{1,0:T(8,128)}), (f32[256,256]{1,0:T(8,128)}, f32[256,256]{1,0:T(8,128)}, ...) | async-done | bytes 1572880 | tf_op jit(solution)/shard_map/psum | solution.py:79
  883.8 1.1 bitcast_subtract_fusion
  884.9 1.4 fusion.7
  886.3 1.6 convolution_add_fusion.3
  888.0 1.5 fusion.6
  892.9 1.7 fusion.4
  894.6 1.3 fusion.2
  896.9 1.6 maximum_maximum_fusion
  (47 shorter events, 6.4 us)
Async XLA Ops:
  7.2 403.7 %reduce-scatter.8.cloned.1.call-start = ((), (), s32[]{:S(2)}) async-start(), calls=%async_computation.6 | async-start | bytes 6684672 | tf_op jit(solution)/shard_map/reduce_scatter | solution.py:61
  27.6 1.3 copy-start.2
  27.6 526.5 %reduce-scatter.6.cloned.1.call-start = ((), (), s32[]{:S(2)}) async-start(), calls=%async_computation.5 | async-start | bytes 6684672 | tf_op jit(solution)/shard_map/reduce_scatter | solution.py:61
  56.5 715.6 %all-to-all-start = ((f32[16,384,768]{2,1,0:T(8,128)}), f32[16,384,768]{2,1,0:T(8,128)}, u32[]{:S(2)}, u32[]{:S(2)}) async-start(f32[16,384,768]{2,1,0:T(8,128)} %broadcast_multiply_fusion), calls=%async_computation.3 | async-start | bytes 37748736 | tf_op jit(solution)/shard_map/all_to_all | solution.py:44
  63.9 554.3 %all-gather.3.cloned.1.call-start = ((), (), s32[]{:S(2)}) async-start(), calls=%async_computation.7 | async-start | bytes 6684672 | tf_op jit(solution)/shard_map/all_gather | solution.py:72
  412.6 293.1 %reduce-scatter.4.cloned.1.call-start = ((), (), s32[]{:S(2)}) async-start(), calls=%async_computation.4 | async-start | bytes 6684672 | tf_op jit(solution)/shard_map/reduce_scatter | solution.py:61
  432.1 337.5 %all-gather.5.cloned.1.call-start = ((), (), s32[]{:S(2)}) async-start(), calls=%async_computation.8 | async-start | bytes 6684672 | tf_op jit(solution)/shard_map/all_gather | solution.py:72
  620.7 263.0 %all-reduce.3.cloned.1.call-start = ((), (), s32[]{:S(2)}) async-start(), calls=%async_computation.9 | async-start | bytes 3145728 | tf_op jit(solution)/shard_map/psum | solution.py:79
  772.1 7.7 copy-start
  779.8 3.9 copy-start.1
  785.4 3.0 slice-start
  785.4 3.8 copy-start.3
  790.7 97.3 %copy-start.4 = (f32[768,768]{1,0:T(8,128)S(1)}, f32[768,768]{1,0:T(8,128)}, u32[]{:S(2)}) copy-start(f32[768,768]{1,0:T(8,128)} %param.7) | copy-start | bytes 7077892
  790.7 97.3 %copy-start.7 = (f32[1,256,256]{1,2,0:T(8,128)S(1)}, f32[1,256,256]{1,2,0:T(8,128)}, u32[]{:S(2)}) copy-start(f32[1,256,256]{1,2,0:T(8,128)} %copy.42) | copy-start | bytes 786436
  883.8 6.5 copy-start.10
  889.5 0.7 copy-start.5
  892.9 3.0 copy-start.6
  895.9 0.9 copy-start.8
  895.9 1.0 copy-start.9
Sparse Core Ops, SparseCore 0:
  27.8 383.0 reduce-scatter.7
  415.3 138.7 reduce-scatter.5
  557.0 61.1 all-gather.2
  621.9 83.6 reduce-scatter.3
  708.7 60.9 all-gather.4
  788.5 95.2 all-reduce.2
where the time goes:
time: 906 us; the launch traced here: 905 us
  waiting for transfers between devices  775 us (86%)
  matrix products  80.8 us (9%)
  other arithmetic  21.5 us (2%)
  between operations  14.3 us (2%)
    reduce_scatter x3, waiting for transfers between devices, on_device(): lax.psum_scatter(term_rows(jnp.int32(0), share_rows * lax.axis_size('pcol...  553 us
    all_gather x2, waiting for transfers between devices, on_device(): column_now = lax.all_gather(share_column, 'pcol', axis=0, tiled=True)  128 us
    psum x1, waiting for transfers between devices, on_device(): pivot_sum = lax.psum(pivot_part, ('prow', 'pcol'))  93.1 us
    dot_general x20, matrix products, product(): jnp.dot(left, right, precision=precise, preferred_element_type=jnp.float32)  80.8 us
  transfers between devices with their start and end apart: 7, of which 6 were waited for; matrix products, arithmetic and copies ran while one was open for 6% of the time, Pallas kernels for 0%

commit v1 on v0

--- a/solution.py
+++ b/solution.py
@@ -1,6 +1,11 @@
+import functools
+import math
+
 import jax
 import jax.numpy as jnp
 from jax import lax
+from jax.experimental import pallas as pl
+from jax.experimental.pallas import tpu as pltpu
 from jax.sharding import PartitionSpec as P
 
 precise = lax.Precision.HIGHEST
@@ -106,6 +111,435 @@
     return (anc_columns, win_inverse)
 
 
+vmem_bytes = 60 * 1024 * 1024
+tile = 128
+little = pl.CostEstimate(flops=1, bytes_accessed=1, transcendentals=0)
+
+
+def halves_of(value):
+    high = value.astype(jnp.bfloat16)
+    return high, (value - high.astype(jnp.float32)).astype(jnp.bfloat16)
+
+
+def product_of(left, right, turned=False):
+    dims = ((0,), (0,)) if turned else ((1,), (0,))
+
+    def dot(a, b):
+        return lax.dot_general(a, b, (dims, ((), ())), preferred_element_type=jnp.float32)
+
+    return dot(left[0], right[0]) + dot(left[0], right[1]) + dot(left[1], right[0])
+
+
+def times(left, right, turned=False):
+    return product_of(halves_of(left), halves_of(right), turned)
+
+
+def chip_at(place, levels):
+    return jnp.where(place < levels, 2 * place, 2 * (2 * levels - 1 - place) + 1)
+
+
+def ring_place(index, levels):
+    z = index // 4
+    return jnp.where((index // 2) % 2 == 0, z, 2 * levels - 1 - z)
+
+
+def source_device(step, index, levels):
+    away = jnp.where(step % 2 == 1, -((step + 1) // 2), step // 2)
+    spot = lax.rem(ring_place(index, levels) + away + 2 * levels, 2 * levels)
+    return 2 * chip_at(spot, levels) + index % 2
+
+
+def head_kernel(width, cuts, index_ref, structure_ref, factor_ref, masked_ref, *turned_refs):
+    rows, all_cols = factor_ref.shape
+    share = math.gcd(rows, width)
+    for t in range(rows // share):
+        block = (index_ref[0] * rows + t * share) // width
+        at = slice(t * share, (t + 1) * share)
+        for k in range(all_cols // width):
+            kept = structure_ref[k, block].astype(jnp.float32)
+            cols = slice(k * width, (k + 1) * width)
+            masked_ref[at, cols] = factor_ref[at, cols] * kept
+    for (first, last), ref in zip(cuts, turned_refs):
+        ref[...] = masked_ref[:, first:last].T
+
+
+def head(index, structure, anc_factor, width, cuts):
+    rows, all_cols = anc_factor.shape
+    smem = pl.BlockSpec(memory_space=pltpu.SMEM)
+    vmem = pl.BlockSpec(memory_space=pltpu.VMEM)
+    return pl.pallas_call(
+        functools.partial(head_kernel, width, cuts),
+        in_specs=[smem, smem, vmem],
+        out_specs=[vmem] * (1 + len(cuts)),
+        out_shape=[jax.ShapeDtypeStruct((rows, all_cols), jnp.float32)]
+        + [jax.ShapeDtypeStruct((last - first, rows), jnp.float32) for first, last in cuts],
+        compiler_params=pltpu.CompilerParams(vmem_limit_bytes=vmem_bytes),
+        cost_estimate=little,
+    )(index, structure, anc_factor)
+
+
+def multiply_kernel(layout, has_start, rows_at, index_ref, own_ref, twin_ref, *refs):
+    refs = list(refs)
+    piece_count = sum(len(block) for block in layout)
+    pieces = [refs.pop(0) for _ in range(piece_count)]
+    starts = [refs.pop(0) for _ in range(2)] if has_start else None
+    factors = [refs.pop(0) for _ in range(2)] if rows_at else None
+    outs = [refs.pop(0) for _ in range(2)]
+    inner_ref = refs.pop(0) if rows_at else None
+    held = refs.pop(0)
+    step = pl.program_id(0)
+    at = 0
+    for b, block in enumerate(layout):
+        chosen = pieces[at : at + len(block)]
+        at += len(block)
+
+        @pl.when(step == b)
+        def _(chosen=chosen, block=block):
+            for ref, (top, height) in zip(chosen, block):
+                held[top : top + height, :] = ref[...]
+
+    @pl.when(step == 0)
+    def _():
+        for i in range(2):
+            outs[i][...] = starts[i][...] if has_start else jnp.zeros_like(outs[i])
+
+    rows = halves_of(held[...])
+    for ref, out in ((own_ref, outs[0]), (twin_ref, outs[1])):
+        out[...] += product_of(rows, halves_of(ref[...]))
+    if rows_at:
+
+        @pl.when(step == len(layout) - 1)
+        def _():
+            images = [halves_of(out[...]) for out in outs]
+            sides = [halves_of(ref[...]) for ref in factors]
+            spot = 0
+            for top, first in rows_at:
+                value = 0.0
+                for image, side in zip(images, sides):
+                    value = value + product_of(
+                        tuple(half[top : top + tile] for half in image),
+                        tuple(half[:, : first + tile] for half in side),
+                    )
+                for i in range(first // tile + 1):
+                    inner_ref[spot * tile : (spot + 1) * tile, :] = value[
+                        :, i * tile : (i + 1) * tile
+                    ]
+                    spot += 1
+
+
+def multiply(index, inverse, twin, first, blocks, start=None, rows_at=(), factors=()):
+    rows = inverse.shape[1]
+    levels = inverse.shape[0] // rows // 4
+    layout, flat = [], []
+    for block in blocks:
+        top, places = 0, []
+        for piece in block:
+            places.append((top, piece.shape[0]))
+            top += piece.shape[0]
+            flat.append(piece)
+        layout.append(tuple(places))
+    height = top
+
+    def whole(shape):
+        return pl.BlockSpec(shape, lambda i, at: (0, 0))
+
+    def source(i, at):
+        return source_device(i + first, at[0], levels), 0
+
+    image = jax.ShapeDtypeStruct((height, rows), jnp.float32)
+    out_shape = [image, image]
+    if rows_at:
+        count = sum(first // tile + 1 for _, first in rows_at)
+        out_shape.append(jax.ShapeDtypeStruct((count * tile, tile), jnp.float32))
+    operands = flat + list(start or ()) + list(factors)
+    return pl.pallas_call(
+        functools.partial(multiply_kernel, tuple(layout), start is not None, rows_at),
+        grid_spec=pltpu.PrefetchScalarGridSpec(
+            num_scalar_prefetch=1,
+            grid=(len(blocks),),
+            in_specs=[pl.BlockSpec((rows, rows), source), pl.BlockSpec((rows, rows), source)]
+            + [whole(v.shape) for v in operands],
+            out_specs=[whole(v.shape) for v in out_shape],
+            scratch_shapes=[pltpu.VMEM((height, rows), jnp.float32)],
+        ),
+        out_shape=out_shape,
+        compiler_params=pltpu.CompilerParams(vmem_limit_bytes=vmem_bytes),
+        cost_estimate=little,
+    )(index, inverse, twin, *operands)
+
+
+def columns_kernel(width, steps, tops, *refs):
+    images, adds = refs[: len(tops)], refs[len(tops) : 2 * len(tops)]
+    factor_ref, out_ref, image = refs[2 * len(tops) :]
+    for top, ref, add_ref in zip(tops, images, adds):
+        image[top : top + ref.shape[0], :] = ref[...] + add_ref[...]
+    solved = {}
+    for k in range(steps - 1, -1, -1):
+        value = image[k * width : (k + 1) * width, :]
+        for j in range(k + 1, steps):
+            side = factor_ref[j * width : (j + 1) * width, k * width : (k + 1) * width]
+            value = value + times(side, solved[j], True)
+        solved[k] = -value
+        out_ref[:, k * width : (k + 1) * width] = solved[k].T
+
+
+def solve_columns(width, steps, tops, images, adds, win_factor):
+    rows = images[0].shape[1]
+    return pl.pallas_call(
+        functools.partial(columns_kernel, width, steps, tops),
+        out_shape=jax.ShapeDtypeStruct((rows, steps * width), jnp.float32),
+        scratch_shapes=[pltpu.VMEM((steps * width, rows), jnp.float32)],
+        compiler_params=pltpu.CompilerParams(vmem_limit_bytes=vmem_bytes),
+        cost_estimate=little,
+    )(*images, *adds, win_factor)
+
+
+def fill_inner(inner, top, one, two, first_half):
+    whole = jnp.concatenate(
+        [jnp.where(first_half, one, two), jnp.where(first_half, two, one)], axis=0
+    )
+    spot, row = 0, top
+    while spot * tile < whole.shape[0]:
+        for i in range(row // tile + 1):
+            block = whole[spot * tile : (spot + 1) * tile]
+            spot += 1
+            inner[row : row + tile, i * tile : (i + 1) * tile] = block
+            if i * tile < row:
+                inner[i * tile : (i + 1) * tile, row : row + tile] = block.T
+        row += tile
+
+
+def add_kernel(core_ref, mine_ref, other_ref, base_ref, out_ref, inner):
+    fill_inner(inner, 0, mine_ref[...], other_ref[...], core_ref[0] % 2 == 0)
+    out_ref[...] = base_ref[...] + inner[...]
+
+
+def add_last(index, mine, other, base, width):
+    block = pl.BlockSpec((width, width), lambda i: (0, 0))
+    part = pl.BlockSpec(mine.shape, lambda i: (0, 0))
+    return pl.pallas_call(
+        add_kernel,
+        grid=(1,),
+        in_specs=[pl.BlockSpec(memory_space=pltpu.SMEM), part, part, block],
+        out_specs=block,
+        out_shape=jax.ShapeDtypeStruct(base.shape, jnp.float32),
+        input_output_aliases={3: 0},
+        scratch_shapes=[pltpu.VMEM((width, width), jnp.float32)],
+        compiler_params=pltpu.CompilerParams(vmem_limit_bytes=vmem_bytes),
+        cost_estimate=little,
+    )(index, mine, other, base)
+
+
+def window_kernel(width, steps, tops, core_ref, *refs):
+    mine, other = refs[: len(tops)], refs[len(tops) : 2 * len(tops)]
+    factor_ref, pivot_ref, out_ref, inner = refs[2 * len(tops) :]
+    low = min(tops)
+    if low:
+        inner[:low, :low] = jnp.zeros((low, low), jnp.float32)
+    for top, mine_ref, other_ref in zip(tops, mine, other):
+        fill_inner(inner, top, mine_ref[...], other_ref[...], core_ref[0] % 2 == 0)
+
+    def at(k):
+        return slice(k * width, (k + 1) * width)
+
+    cross = {}
+    for k in range(steps - 1, -1, -1):
+        later = range(k + 1, steps)
+        for i in range(k + 1):
+            value = inner[at(k), at(i)]
+            for j in later:
+                value = value + times(factor_ref[at(j), at(k)], cross[j, i], True)
+            cross[k, i] = -value
+        for j in later:
+            value = cross[j, k]
+            for i in later:
+                value = value + times(out_ref[at(j), at(i)], factor_ref[at(i), at(k)])
+            out_ref[at(j), at(k)] = -value
+            out_ref[at(k), at(j)] = -value.T
+        value = pivot_ref[k] - cross[k, k].T
+        for j in later:
+            value = value - times(factor_ref[at(j), at(k)], out_ref[at(j), at(k)], True)
+        out_ref[at(k), at(k)] = value
+
+
+def window_blocks_of(width, steps, tops, index, mine, other, win_factor, pivot_inverse):
+    order = steps * width
+    vmem = pl.BlockSpec(memory_space=pltpu.VMEM)
+    count = 2 * len(tops) + 2
+    return pl.pallas_call(
+        functools.partial(window_kernel, width, steps, tops),
+        in_specs=[pl.BlockSpec(memory_space=pltpu.SMEM)] + [vmem] * count,
+        out_specs=vmem,
+        out_shape=jax.ShapeDtypeStruct((order, order), jnp.float32),
+        scratch_shapes=[pltpu.VMEM((order, order), jnp.float32)],
+        compiler_params=pltpu.CompilerParams(vmem_limit_bytes=vmem_bytes),
+        cost_estimate=little,
+    )(index, *mine, *other, win_factor, pivot_inverse)
+
+
+def fast(anc_inverse, anc_factor, win_factor, pivot_inverse, structure):
+    n = lax.axis_size("pcol")
+    index = lax.axis_index("pcol")
+    levels = n // 4
+    chips = n // 2
+    half_way = chips // 2
+    core = index % 2
+    x = (index // 2) % 2
+    z = index // 4
+    rows = anc_inverse.shape[1]
+    steps_total, width = pivot_inverse.shape[:2]
+    all_cols = anc_factor.shape[1]
+    order = [2 * s if s < levels else 2 * (chips - 1 - s) + 1 for s in range(chips)]
+    forward = [
+        (2 * order[s] + c, 2 * order[(s + 1) % chips] + c) for s in range(chips) for c in range(2)
+    ]
+    backward = [(to, start) for start, to in forward]
+
+    def flip(bits):
+        return [(p, p ^ bits) for p in range(n)]
+
+    def send(value, pairs):
+        return lax.ppermute(value, "pcol", pairs)
+
+    def pick(value, at):
+        return lax.dynamic_index_in_dim(value, at, 0, keepdims=False)
+
+    def swap_halves(value, bit):
+        halves = value.reshape((2, value.shape[0] // 2) + value.shape[1:])
+        return pick(halves, bit), pick(halves, 1 - bit)
+
+    def join(bit, mine, other):
+        return jnp.concatenate(
+            [jnp.where(bit == 0, mine, other), jnp.where(bit == 0, other, mine)], axis=0
+        )
+
+    def sum_small(value):
+        mine, other = swap_halves(value, core)
+        got = yield [send(other, flip(1))]
+        mine = mine + got[0]
+        got = yield [send(mine, flip(2))]
+        mine = mine + got[0]
+        got = yield [send(mine, flip(4 * d)) for d in range(1, levels)]
+        for value in got:
+            mine = mine + value
+        got = yield [send(mine, flip(1))]
+        yield mine, got[0]
+
+    def sum_large(value):
+        mine, other = swap_halves(value, core)
+        got = yield [send(other, flip(1))]
+        mine, other = swap_halves(mine + got[0], x)
+        got = yield [send(other, flip(2))]
+        mine = mine + got[0]
+        parts = mine.reshape((levels, mine.shape[0] // levels) + mine.shape[1:])
+        got = yield [send(pick(parts, z ^ d), flip(4 * d)) for d in range(1, levels)]
+        total = pick(parts, z)
+        for value in got:
+            total = total + value
+        got = yield [send(total, flip(4 * d)) for d in range(1, levels)]
+        pieces = [total] + got
+        bit = 1
+        while bit < levels:
+            pieces = [
+                join((z // bit) % 2, pieces[i], pieces[i + 1]) for i in range(0, len(pieces), 2)
+            ]
+            bit *= 2
+        mine = pieces[0]
+        got = yield [send(mine, flip(2))]
+        mine = join(x, mine, got[0])
+        got = yield [send(mine, flip(1))]
+        yield mine, got[0]
+
+    def ends(up, down):
+        middle = up.shape[0] // 2
+        return [send(up[:middle], forward), send(down[middle:], backward)]
+
+    at = index.astype(jnp.int32).reshape(1)
+    plan = (((width, 2 * width), (2 * width, all_cols)), ((0, width),))
+    cuts = tuple(cut for streams in plan for cut in streams)
+    factor, *turned = head(at, structure, anc_factor, width, cuts)
+    twin = send(anc_inverse, flip(1))
+    factor_twin = send(factor, flip(1))
+    factors = (factor, factor_twin)
+
+    def ring(pieces):
+        ups = downs = list(pieces)
+        yield ups, ups
+        for s in range(1, half_way):
+            ups = [send(v, forward) for v in ups]
+            downs = [send(v, backward) for v in downs]
+            ups, downs = yield ups, downs
+        if len(ups) == 2:
+            yield [send(ups[0], forward), send(downs[1], backward)]
+        else:
+            yield ends(ups[0], downs[0])
+
+    def strips(streams):
+        first, last = streams[0][0], streams[-1][1]
+        return tuple((i - first, i) for i in range(first, last, tile))
+
+    def product(start, blocks, total=None, rows_at=()):
+        return multiply(
+            at, anc_inverse, twin, start, blocks, total, rows_at, factors if rows_at else ()
+        )
+
+    hold = lax.optimization_barrier
+    ring_a = ring(turned[: len(plan[0])])
+    pieces_b = turned[len(plan[0]) :]
+    ups, _ = next(ring_a)
+    a = [ups]
+    ups, downs = next(ring_a)
+    for s in range(2, half_way):
+        a += [ups, downs]
+        ups, downs = ring_a.send((ups, downs))
+    near = product(0, a)
+    (ups, downs), near = hold(((ups, downs), near))
+    pieces_b, downs = hold((pieces_b, downs))
+    far = ring_a.send((ups, downs))
+    ring_b = ring(pieces_b)
+    b = [next(ring_b)[0]]
+    ups_b, downs_b = next(ring_b)
+    mid = product(5, [ups, downs], near)
+    mine_a, theirs_a, local = product(7, [far], mid, strips(plan[0]))
+    (ups_b, downs_b), local = hold(((ups_b, downs_b), local))
+    sum_a = sum_large(local)
+    got = next(sum_a)
+    b += [ups_b, downs_b]
+    ups_b, downs_b = ring_b.send((ups_b, downs_b))
+    (ups_b, downs_b), got = hold(((ups_b, downs_b), got))
+    got = sum_a.send(got)
+    adds_a = send(theirs_a, flip(1))
+    b += [ups_b, downs_b]
+    near = product(0, b)
+    ups_b, downs_b = ring_b.send((ups_b, downs_b))
+    (ups_b, downs_b), got, near = hold(((ups_b, downs_b), got, near))
+    got = sum_a.send(got)
+    far = ring_b.send((ups_b, downs_b))
+    mid = product(5, [ups_b, downs_b], near)
+    got = sum_a.send(got)
+    mine_b, theirs_b, local = product(7, [far], mid, strips(plan[1]))
+    sum_b = sum_small(local)
+    got_b = next(sum_b)
+    got_b, got = hold((got_b, got))
+    got = sum_a.send(got)
+    got_b = sum_b.send(got_b)
+    adds_b = send(theirs_b, flip(1))
+    got_b, got = hold((got_b, got))
+    got = sum_a.send(got)
+    got_b = sum_b.send(got_b)
+    tops = [plan[0][0][0], plan[1][0][0]]
+    images, adds = [mine_a, mine_b], [adds_a, adds_b]
+    anc_columns = solve_columns(width, steps_total, tops, images, adds, win_factor)
+    got_b, got, anc_columns = hold((got_b, got, anc_columns))
+    got_b = sum_b.send(got_b)
+    mine, other = sum_a.send(got)
+    base = window_blocks_of(
+        width, steps_total, tops[:1], at, [mine], [other], win_factor, pivot_inverse
+    )
+    win_inverse = add_last(at, *sum_b.send(got_b), base, width)
+    return (anc_columns, win_inverse)
+
+
 def solution(mesh):
     in_specs = (
         P(("pole", "prow"), "pcol"),
@@ -115,6 +549,9 @@
         P(),
     )
     out_specs = (P(("pole", "prow", "pcol"), None), P("pole", None))
+    levels = mesh.shape["pcol"] // 4
+    ringed = mesh.shape["prow"] == 1 and mesh.shape["pcol"] % 4 == 0
+    ringed = ringed and levels > 1 and levels & (levels - 1) == 0
     return jax.shard_map(
-        on_device, mesh=mesh, in_specs=in_specs, out_specs=out_specs, check_vma=False
+        fast if ringed else on_device, mesh=mesh, in_specs=in_specs, out_specs=out_specs, check_vma=False
     )

time: 906 us -> 176 us (0.19)
  waiting for transfers between devices: 775 us -> 67.4 us
  matrix products: 80.8 us -> 0 us
  Pallas kernels: 0 us -> 58.7 us
  starting transfers between devices: 8.28 us -> 42.8 us
  other arithmetic: 21.5 us -> 0.32 us
  between operations: 14.3 us -> 0.99 us
    reduce_scatter x3 -> x0, waiting for transfers between devices: 553 us -> none  [on_device(): lax.psum_scatter(term_rows(jnp.int32(0), share_rows * lax.axis_size('pcol...]
    all_gather x2 -> x0, waiting for transfers between devices: 128 us -> none  [on_device(): column_now = lax.all_gather(share_column, 'pcol', axis=0, tiled=True)]
    psum x1 -> x0, waiting for transfers between devices: 93.1 us -> none  [on_device(): pivot_sum = lax.psum(pivot_part, ('prow', 'pcol'))]
    dot_general x20 -> x0, matrix products: 80.8 us -> none  [product(): jnp.dot(left, right, precision=precise, preferred_element_type=jnp.float32)]
    ppermute x0 -> x42, waiting for transfers between devices: none -> 67.4 us  [send(): return lax.ppermute(value, 'pcol', pairs)]
    pallas_call x0 -> x10, Pallas kernels: none -> 58.7 us  [the longest x6 43.7 us: multiply(): pl.pallas_call(functools.partial(multiply_kernel, tuple(layout), start is...]
    ppermute x0 -> x42, starting transfers between devices: none -> 42.8 us  [send(): return lax.ppermute(value, 'pcol', pairs)]
  transfers between devices with their start and end apart: 7 -> 42, of which waited for: 6 -> 15; matrix products, arithmetic and copies ran while one was open for 6% -> 1% of each run, Pallas kernels for 0% -> 32%
where the time goes in v1:
time: 176 us
  waiting for transfers between devices  67.4 us (38%)
  Pallas kernels  58.7 us (33%)
  starting transfers between devices  42.8 us (24%)
  local copies, waits for them, and re-layouts  5.38 us (3%)
    ppermute x42, waiting for transfers between devices, send(): return lax.ppermute(value, 'pcol', pairs)  67.4 us
    pallas_call x6, Pallas kernels, multiply(): pl.pallas_call(functools.partial(multiply_kernel, tuple(layout), start is...  43.7 us
    ppermute x42, starting transfers between devices, send(): return lax.ppermute(value, 'pcol', pairs)  42.8 us
    pallas_call x1, Pallas kernels, window_blocks_of(): pl.pallas_call(functools.partial(window_kernel, width, steps, tops), in_s...  5.67 us
    pallas_call x1, Pallas kernels, solve_columns(): pl.pallas_call(functools.partial(columns_kernel, width, steps, tops), out...  4.54 us
  transfers between devices with their start and end apart: 42, of which 15 were waited for; matrix products, arithmetic and copies ran while one was open for 1% of the time, Pallas kernels for 32%

profile of v1, /device:TPU:0, one launch (start us, length us, event | category | flops | bytes accessed | tf_op | source)
XLA Modules:
  0.0 175.6 jit_solution(5005626810450249235)
XLA Ops:
  1.1 2.9 %shard_map.68 = (f32[384,768]{1,0:T(8,128)}, f32[256,384]{1,0:T(8,128)}, f32[256,384]{1,0:T(8,128)}, f32[256,384]{1,0:T(8,128)}) custom-call(s32[1]{0:T(128)} %bitcast.index_ref.core_ref, s32[3,24]{1,0:T(4,128)} %structure_ref.1, f32[384,768]{1,0:T(8,128)} %factor_ref.1), custom_call_target="tpu_custom_call" | custom-call | flops 1 | bytes 1 | tf_op jit(solution)/shard_map/pallas_call | solution.py:170
  4.0 2.5 %collective-permute-start.10 = (f32[256,384]{1,0:T(8,128)}, f32[256,384]{1,0:T(8,128)S(1)}, u32[]{:S(2)}, u32[]{:S(2)}) collective-permute-start(f32[256,384]{1,0:T(8,128)} %get-tuple-element.53.refs_1_), channel_id=1, source_target_pairs={{4,0},{5,1},{8,4},{9,5},{12,8},{13,9},{14,12},{15,13},{10,14},{11,... | collective-permute-start | bytes 1179656 | tf_op jit(solution)/shard_map/ppermute | solution.py:402
  6.6 2.0 %collective-permute-start.4 = (f32[256,384]{1,0:T(8,128)}, f32[256,384]{1,0:T(8,128)S(1)}, u32[]{:S(2)}, u32[]{:S(2)}) collective-permute-start(f32[256,384]{1,0:T(8,128)} %get-tuple-element.53.refs_1_), channel_id=1, source_target_pairs={{0,4},{1,5},{4,8},{5,9},{8,12},{9,13},{12,14},{13,15},{14,10},{15,... | collective-permute-start | bytes 1179656 | tf_op jit(solution)/shard_map/ppermute | solution.py:402
  8.6 8.1 %collective-permute-done.10.refs_5_ = f32[256,384]{1,0:T(8,128)S(1)} collective-permute-done((f32[256,384]{1,0:T(8,128)}, f32[256,384]{1,0:T(8,128)S(1)}, u32[]{:S(2)}, u32[]{:S(2)}) %collective-permute-start.10) | collective-permute-done | bytes 393248 | tf_op jit(solution)/shard_map/ppermute | solution.py:402
  16.8 1.9 %collective-permute-start.11 = (f32[256,384]{1,0:T(8,128)S(1)}, f32[256,384]{1,0:T(8,128)}, u32[]{:S(2)}, u32[]{:S(2)}) collective-permute-start(f32[256,384]{1,0:T(8,128)S(1)} %collective-permute-done.10.refs_5_), channel_id=1, source_target_pairs={{4,0},{5,1},{8,4},{9,5},{12,8},{13,9},{14,12},{15,13},{10,14},{11,... | collective-permute-start | bytes 1179656 | tf_op jit(solution)/shard_map/ppermute | solution.py:402
  18.8 8.3 %collective-permute-done.4.refs_3_ = f32[256,384]{1,0:T(8,128)S(1)} collective-permute-done((f32[256,384]{1,0:T(8,128)}, f32[256,384]{1,0:T(8,128)S(1)}, u32[]{:S(2)}, u32[]{:S(2)}) %collective-permute-start.4) | collective-permute-done | bytes 393248 | tf_op jit(solution)/shard_map/ppermute | solution.py:402
  27.2 2.0 %collective-permute-start.8 = (f32[256,384]{1,0:T(8,128)S(1)}, f32[256,384]{1,0:T(8,128)}, u32[]{:S(2)}, u32[]{:S(2)}) collective-permute-start(f32[256,384]{1,0:T(8,128)S(1)} %collective-permute-done.7.refs_4_), channel_id=1, source_target_pairs={{4,0},{5,1},{8,4},{9,5},{12,8},{13,9},{14,12},{15,13},{10,14},{11,... | collective-permute-start | bytes 1179656 | tf_op jit(solution)/shard_map/ppermute | solution.py:402
  29.2 4.6 %collective-permute-done.11.refs_9_ = f32[256,384]{1,0:T(8,128)} collective-permute-done((f32[256,384]{1,0:T(8,128)S(1)}, f32[256,384]{1,0:T(8,128)}, u32[]{:S(2)}, u32[]{:S(2)}) %collective-permute-start.11) | collective-permute-done | bytes 393248 | tf_op jit(solution)/shard_map/ppermute | solution.py:402
  33.8 1.9 %collective-permute-done.2.refs_6_ = f32[256,384]{1,0:T(8,128)} collective-permute-done((f32[256,384]{1,0:T(8,128)S(1)}, f32[256,384]{1,0:T(8,128)}, u32[]{:S(2)}, u32[]{:S(2)}) %collective-permute-start.2) | collective-permute-done | bytes 393248 | tf_op jit(solution)/shard_map/ppermute | solution.py:402
  37.2 6.1 %collective-permute-done.5.refs_7_ = f32[256,384]{1,0:T(8,128)} collective-permute-done((f32[256,384]{1,0:T(8,128)S(1)}, f32[256,384]{1,0:T(8,128)}, u32[]{:S(2)}, u32[]{:S(2)}) %collective-permute-start.5) | collective-permute-done | bytes 393248 | tf_op jit(solution)/shard_map/ppermute | solution.py:402
  43.7 1.8 %collective-permute-start.6 = (f32[256,384]{1,0:T(8,128)}, f32[256,384]{1,0:T(8,128)S(1)}, u32[]{:S(2)}, u32[]{:S(2)}) collective-permute-start(f32[256,384]{1,0:T(8,128)} %collective-permute-done.5.refs_7_), channel_id=1, source_target_pairs={{0,4},{1,5},{4,8},{5,9},{8,12},{9,13},{12,14},{13,15},{14,10},{15,... | collective-permute-start | bytes 1179656 | tf_op jit(solution)/shard_map/ppermute | solution.py:402
  45.8 12.5 %shard_map.69 = (f32[512,384]{1,0:T(8,128)}, f32[512,384]{1,0:T(8,128)}) custom-call(s32[1]{0:T(128)} %bitcast.index_ref.core_ref, f32[6144,384]{1,0:T(8,128)} %own_ref.11, f32[6144,384]{1,0:T(8,128)} %collective-permute-done.twin_ref, f32[256,384]{1,0:T(8,128)} %get-tuple-element.52.refs_0_, f32[256,384]{1,0:T(8,128)} %get-tuple-element.53.refs_1_, ...), custom_call_target="tpu_custom_call" | custom-call | flops 1 | bytes 1 | tf_op jit(solution)/shard_map/pallas_call | solution.py:255
  58.3 4.1 %collective-permute-done.6.refs_1_ = f32[256,384]{1,0:T(8,128)S(1)} collective-permute-done((f32[256,384]{1,0:T(8,128)}, f32[256,384]{1,0:T(8,128)S(1)}, u32[]{:S(2)}, u32[]{:S(2)}) %collective-permute-start.6) | collective-permute-done | bytes 393248 | tf_op jit(solution)/shard_map/ppermute | solution.py:402
  66.5 6.7 %shard_map.70 = (f32[512,384]{1,0:T(8,128)}, f32[512,384]{1,0:T(8,128)}) custom-call(s32[1]{0:T(128)} %bitcast.index_ref.core_ref, f32[6144,384]{1,0:T(8,128)} %own_ref.11, f32[6144,384]{1,0:T(8,128)} %collective-permute-done.twin_ref, f32[256,384]{1,0:T(8,128)} %copy-done.14, f32[256,384]{1,0:T(8,128)} %copy-done.16, ...), custom_call_target="tpu_custom_call" | custom-call | flops 1 | bytes 1 | tf_op jit(solution)/shard_map/pallas_call | solution.py:255
  76.1 7.5 %shard_map.71 = (f32[512,384]{1,0:T(8,128)}, f32[512,384]{1,0:T(8,128)}, f32[2304,128]{1,0:T(8,128)}) custom-call(s32[1]{0:T(128)} %bitcast.index_ref.core_ref, f32[6144,384]{1,0:T(8,128)} %own_ref.11, f32[6144,384]{1,0:T(8,128)} %collective-permute-done.twin_ref, f32[256,384]{1,0:T(8,128)} %collective-permute-done.15.refs_0_, ...), custom_call_target="tpu_custom_call" | custom-call | flops 1 | bytes 1 | tf_op jit(solution)/shard_map/pallas_call | solution.py:255
  87.3 9.4 %collective-permute-done.18.refs_3_ = f32[256,384]{1,0:T(8,128)S(1)} collective-permute-done((f32[256,384]{1,0:T(8,128)S(1)}, f32[256,384]{1,0:T(8,128)S(1)}, u32[]{:S(2)}, u32[]{:S(2)}) %collective-permute-start.18) | collective-permute-done | bytes 393248 | tf_op jit(solution)/shard_map/ppermute | solution.py:402
  99.2 1.6 collective-permute-start.23
  100.8 8.1 %shard_map.72 = (f32[256,384]{1,0:T(8,128)}, f32[256,384]{1,0:T(8,128)}) custom-call(s32[1]{0:T(128)} %bitcast.index_ref.core_ref, f32[6144,384]{1,0:T(8,128)} %own_ref.11, f32[6144,384]{1,0:T(8,128)} %collective-permute-done.twin_ref, f32[256,384]{1,0:T(8,128)} %get-tuple-element.58.refs_0_, f32[256,384]{1,0:T(8,128)} %copy-done.10, f32[256,384]{1,0:T(8,128)} %copy-done.11, ...), custom_call_target="tpu_custom_call" | custom-call | flops 1 | bytes 1 | tf_op jit(solution)/shard_map/pallas_call | solution.py:255
  108.9 5.0 %collective-permute-done.23 = f32[576,128]{1,0:T(8,128)S(1)} collective-permute-done((f32[576,128]{1,0:T(8,128)S(1)}, f32[576,128]{1,0:T(8,128)S(1)}, u32[]{:S(2)}, u32[]{:S(2)}) %collective-permute-start.23) | collective-permute-done | bytes 294944 | tf_op jit(solution)/shard_map/ppermute | solution.py:402
  114.0 2.2 %collective-permute-start.25 = (f32[128,384]{1,0:T(8,128)S(1)}, f32[128,384]{1,0:T(8,128)S(1)}, u32[]{:S(2)}, u32[]{:S(2)}) collective-permute-start(f32[128,384]{1,0:T(8,128)S(1)} %slice.7), channel_id=1, source_target_pairs={{4,0},{5,1},{8,4},{9,5},{12,8},{13,9},{14,12},{15,13},{10,14},{11,... | collective-permute-start | bytes 589832 | tf_op jit(solution)/shard_map/ppermute | solution.py:402
  116.4 4.7 %collective-permute-start.28 = (f32[144,128]{1,0:T(8,128)S(1)}, f32[144,128]{1,0:T(8,128)S(1)}, u32[]{:S(2)}, u32[]{:S(2)}) collective-permute-start(f32[144,128]{1,0:T(8,128)S(1)} %get-tuple-element.106), channel_id=1, source_target_pairs={{0,8},{1,9},{2,10},{3,11},{4,12},{5,13},{6,14},{7,15},{8,0},{9,1},... | collective-permute-start | bytes 221192 | tf_op jit(solution)/shard_map/ppermute | solution.py:402
  121.1 4.5 %shard_map.73 = (f32[256,384]{1,0:T(8,128)}, f32[256,384]{1,0:T(8,128)}) custom-call(s32[1]{0:T(128)} %bitcast.index_ref.core_ref, f32[6144,384]{1,0:T(8,128)} %own_ref.11, f32[6144,384]{1,0:T(8,128)} %collective-permute-done.twin_ref, f32[256,384]{1,0:T(8,128)} %copy-done.3, f32[256,384]{1,0:T(8,128)} %copy-done.4, f32[256,384]{1,0:T(8,128)} %get-tuple-element.79.refs_2_, ...), custom_call_target="tpu_custom_call" | custom-call | flops 1 | bytes 1 | tf_op jit(solution)/shard_map/pallas_call | solution.py:255
  126.4 4.4 %shard_map.74 = (f32[256,384]{1,0:T(8,128)}, f32[256,384]{1,0:T(8,128)}, f32[384,128]{1,0:T(8,128)}) custom-call(s32[1]{0:T(128)} %bitcast.index_ref.core_ref, f32[6144,384]{1,0:T(8,128)} %own_ref.11, f32[6144,384]{1,0:T(8,128)} %collective-permute-done.twin_ref, f32[128,384]{1,0:T(8,128)} %copy-done.20, f32[128,384]{1,0:T(8,128)} %copy-done.21, ...), custom_call_target="tpu_custom_call" | custom-call | flops 1 | bytes 1 | tf_op jit(solution)/shard_map/pallas_call | solution.py:255
  132.5 3.8 %collective-permute-start.31 = (f32[144,128]{1,0:T(8,128)S(1)}, f32[144,128]{1,0:T(8,128)S(1)}, u32[]{:S(2)}, u32[]{:S(2)}) collective-permute-start(f32[144,128]{1,0:T(8,128)S(1)} %fusion.3), channel_id=1, source_target_pairs={{0,8},{1,9},{2,10},{3,11},{4,12},{5,13},{6,14},{7,15},{8,0},{9,1},... | collective-permute-start | bytes 221192 | tf_op jit(solution)/shard_map/ppermute | solution.py:402
  136.6 5.9 %collective-permute-done.31 = f32[144,128]{1,0:T(8,128)S(1)} collective-permute-done((f32[144,128]{1,0:T(8,128)S(1)}, f32[144,128]{1,0:T(8,128)S(1)}, u32[]{:S(2)}, u32[]{:S(2)}) %collective-permute-start.31) | collective-permute-done | bytes 73760 | tf_op jit(solution)/shard_map/ppermute | solution.py:402
  143.1 1.8 %collective-permute-start.33 = (f32[192,128]{1,0:T(8,128)S(1)}, f32[192,128]{1,0:T(8,128)S(1)}, u32[]{:S(2)}, u32[]{:S(2)}) collective-permute-start(f32[192,128]{1,0:T(8,128)S(1)} %bitcast_add_fusion.2), channel_id=1, source_target_pairs={{0,2},{1,3},{2,0},{3,1},{4,6},{5,7},{6,4},{7,5},{8,10},{9,11},{10,... | collective-permute-start | bytes 294920 | tf_op jit(solution)/shard_map/ppermute | solution.py:402
  144.9 7.6 %collective-permute-done.33 = f32[192,128]{1,0:T(8,128)S(1)} collective-permute-done((f32[192,128]{1,0:T(8,128)S(1)}, f32[192,128]{1,0:T(8,128)S(1)}, u32[]{:S(2)}, u32[]{:S(2)}) %collective-permute-start.33) | collective-permute-done | bytes 98336 | tf_op jit(solution)/shard_map/ppermute | solution.py:402
  153.2 2.7 %collective-permute-start.35 = (f32[192,128]{1,0:T(8,128)S(1)}, f32[192,128]{1,0:T(8,128)S(1)}, u32[]{:S(2)}, u32[]{:S(2)}) collective-permute-start(f32[192,128]{1,0:T(8,128)S(1)} %add.98), channel_id=1, source_target_pairs={{0,4},{1,5},{2,6},{3,7},{4,0},{5,1},{6,2},{7,3},{8,12},{9,13},{10,... | collective-permute-start | bytes 294920 | tf_op jit(solution)/shard_map/ppermute | solution.py:402
  159.3 4.5 %shard_map.75 = f32[384,768]{1,0:T(8,128)} custom-call(f32[512,384]{1,0:T(8,128)} %get-tuple-element.91.refs_0_, f32[256,384]{1,0:T(8,128)} %get-tuple-element.92.refs_1_, f32[512,384]{1,0:T(8,128)} %copy-done.5, f32[256,384]{1,0:T(8,128)} %copy-done.7, f32[768,768]{1,0:T(8,128)} %refs_2_.1), custom_call_target="tpu_custom_call" | custom-call | flops 1 | bytes 1 | tf_op jit(solution)/shard_map/pallas_call | solution.py:288
  163.8 2.8 %collective-permute-done.36 = f32[192,128]{1,0:T(8,128)S(1)} collective-permute-done((f32[192,128]{1,0:T(8,128)S(1)}, f32[192,128]{1,0:T(8,128)S(1)}, u32[]{:S(2)}, u32[]{:S(2)}) %collective-permute-start.36) | collective-permute-done | bytes 98336 | tf_op jit(solution)/shard_map/ppermute | solution.py:402
  167.4 5.7 %shard_map.76.base_ref = f32[768,768]{1,0:T(8,128)} custom-call(s32[1]{0:T(128)} %bitcast.index_ref.core_ref, f32[1152,128]{1,0:T(8,128)} %copy-done.1, f32[1152,128]{1,0:T(8,128)} %copy-done.6, f32[768,768]{1,0:T(8,128)} %refs_2_.1, f32[3,256,256]{2,1,0:T(8,128)} %refs_3_.1), custom_call_target="tpu_custom_call" | custom-call | flops 1 | bytes 1 | tf_op jit(solution)/shard_map/pallas_call | solution.py:369
  173.7 1.9 %shard_map.77 = f32[768,768]{1,0:T(8,128)} custom-call(s32[1]{0:T(128)} %bitcast.index_ref.core_ref, f32[192,128]{1,0:T(8,128)} %copy-done.8, f32[192,128]{1,0:T(8,128)} %copy-done.23, f32[768,768]{1,0:T(8,128)} %shard_map.76.base_ref), custom_call_target="tpu_custom_call", output_to_operand_aliasing={{}: (3, {})} | custom-call | flops 1 | bytes 1 | tf_op jit(solution)/shard_map/pallas_call | solution.py:320
  (131 shorter events, 25.0 us)
Async XLA Ops:
  0.6 44.9 %collective-permute-start = (f32[6144,384]{1,0:T(8,128)}, f32[6144,384]{1,0:T(8,128)}, u32[]{:S(2)}, u32[]{:S(2)}) collective-permute-start(f32[6144,384]{1,0:T(8,128)} %own_ref.11), channel_id=1, source_target_pairs={{0,1},{1,0},{2,3},{3,2},{4,5},{5,4},{6,7},{7,6},{8,9},{9,8},{10,11... | collective-permute-start | bytes 28311560 | tf_op jit(solution)/shard_map/ppermute | solution.py:402
  4.0 12.8 %collective-permute-start.10 = (f32[256,384]{1,0:T(8,128)}, f32[256,384]{1,0:T(8,128)S(1)}, u32[]{:S(2)}, u32[]{:S(2)}) collective-permute-start(f32[256,384]{1,0:T(8,128)} %get-tuple-element.53.refs_1_), channel_id=1, source_target_pairs={{4,0},{5,1},{8,4},{9,5},{12,8},{13,9},{14,12},{15,13},{10,14},{11,... | collective-permute-start | bytes 1179656 | tf_op jit(solution)/shard_map/ppermute | solution.py:402
  6.5 12.2 %collective-permute-start.1 = (f32[256,384]{1,0:T(8,128)}, f32[256,384]{1,0:T(8,128)S(1)}, u32[]{:S(2)}, u32[]{:S(2)}) collective-permute-start(f32[256,384]{1,0:T(8,128)} %get-tuple-element.52.refs_0_), channel_id=1, source_target_pairs={{0,4},{1,5},{4,8},{5,9},{8,12},{9,13},{12,14},{13,15},{14,10},{15,... | collective-permute-start | bytes 1179656 | tf_op jit(solution)/shard_map/ppermute | solution.py:402
  6.6 20.5 %collective-permute-start.4 = (f32[256,384]{1,0:T(8,128)}, f32[256,384]{1,0:T(8,128)S(1)}, u32[]{:S(2)}, u32[]{:S(2)}) collective-permute-start(f32[256,384]{1,0:T(8,128)} %get-tuple-element.53.refs_1_), channel_id=1, source_target_pairs={{0,4},{1,5},{4,8},{5,9},{8,12},{9,13},{12,14},{13,15},{14,10},{15,... | collective-permute-start | bytes 1179656 | tf_op jit(solution)/shard_map/ppermute | solution.py:402
  8.6 18.5 %collective-permute-start.7 = (f32[256,384]{1,0:T(8,128)}, f32[256,384]{1,0:T(8,128)S(1)}, u32[]{:S(2)}, u32[]{:S(2)}) collective-permute-start(f32[256,384]{1,0:T(8,128)} %get-tuple-element.52.refs_0_), channel_id=1, source_target_pairs={{4,0},{5,1},{8,4},{9,5},{12,8},{13,9},{14,12},{15,13},{10,14},{11,... | collective-permute-start | bytes 1179656 | tf_op jit(solution)/shard_map/ppermute | solution.py:402
  16.8 17.0 %collective-permute-start.11 = (f32[256,384]{1,0:T(8,128)S(1)}, f32[256,384]{1,0:T(8,128)}, u32[]{:S(2)}, u32[]{:S(2)}) collective-permute-start(f32[256,384]{1,0:T(8,128)S(1)} %collective-permute-done.10.refs_5_), channel_id=1, source_target_pairs={{4,0},{5,1},{8,4},{9,5},{12,8},{13,9},{14,12},{15,13},{10,14},{11,... | collective-permute-start | bytes 1179656 | tf_op jit(solution)/shard_map/ppermute | solution.py:402
  18.7 17.0 %collective-permute-start.2 = (f32[256,384]{1,0:T(8,128)S(1)}, f32[256,384]{1,0:T(8,128)}, u32[]{:S(2)}, u32[]{:S(2)}) collective-permute-start(f32[256,384]{1,0:T(8,128)S(1)} %collective-permute-done.1.refs_2_), channel_id=1, source_target_pairs={{0,4},{1,5},{4,8},{5,9},{8,12},{9,13},{12,14},{13,15},{14,10},{15,... | collective-permute-start | bytes 1179656 | tf_op jit(solution)/shard_map/ppermute | solution.py:402
  27.1 16.2 %collective-permute-start.5 = (f32[256,384]{1,0:T(8,128)S(1)}, f32[256,384]{1,0:T(8,128)}, u32[]{:S(2)}, u32[]{:S(2)}) collective-permute-start(f32[256,384]{1,0:T(8,128)S(1)} %collective-permute-done.4.refs_3_), channel_id=1, source_target_pairs={{0,4},{1,5},{4,8},{5,9},{8,12},{9,13},{12,14},{13,15},{14,10},{15,... | collective-permute-start | bytes 1179656 | tf_op jit(solution)/shard_map/ppermute | solution.py:402
  27.2 16.6 %collective-permute-start.8 = (f32[256,384]{1,0:T(8,128)S(1)}, f32[256,384]{1,0:T(8,128)}, u32[]{:S(2)}, u32[]{:S(2)}) collective-permute-start(f32[256,384]{1,0:T(8,128)S(1)} %collective-permute-done.7.refs_4_), channel_id=1, source_target_pairs={{4,0},{5,1},{8,4},{9,5},{12,8},{13,9},{14,12},{15,13},{10,14},{11,... | collective-permute-start | bytes 1179656 | tf_op jit(solution)/shard_map/ppermute | solution.py:402
  33.7 39.4 %collective-permute-start.17 = (f32[384,768]{1,0:T(8,128)}, f32[384,768]{1,0:T(8,128)S(1)}, u32[]{:S(2)}, u32[]{:S(2)}) collective-permute-start(f32[384,768]{1,0:T(8,128)} %get-tuple-element.67.refs_4_), channel_id=1, source_target_pairs={{0,1},{1,0},{2,3},{3,2},{4,5},{5,4},{6,7},{7,6},{8,9},{9,8},{10,11... | collective-permute-start | bytes 3538952 | tf_op jit(solution)/shard_map/ppermute | solution.py:402
  35.7 22.6 %collective-permute-start.12 = (f32[256,384]{1,0:T(8,128)}, f32[256,384]{1,0:T(8,128)S(1)}, u32[]{:S(2)}, u32[]{:S(2)}) collective-permute-start(f32[256,384]{1,0:T(8,128)} %collective-permute-done.11.refs_9_), channel_id=1, source_target_pairs={{4,0},{5,1},{8,4},{9,5},{12,8},{13,9},{14,12},{15,13},{10,14},{11,... | collective-permute-start | bytes 1179656 | tf_op jit(solution)/shard_map/ppermute | solution.py:402
  43.3 14.9 %collective-permute-start.3 = (f32[256,384]{1,0:T(8,128)}, f32[256,384]{1,0:T(8,128)S(1)}, u32[]{:S(2)}, u32[]{:S(2)}) collective-permute-start(f32[256,384]{1,0:T(8,128)} %collective-permute-done.2.refs_6_), channel_id=1, source_target_pairs={{0,4},{1,5},{4,8},{5,9},{8,12},{9,13},{12,14},{13,15},{14,10},{15,... | collective-permute-start | bytes 1179656 | tf_op jit(solution)/shard_map/ppermute | solution.py:402
  43.7 18.7 %collective-permute-start.6 = (f32[256,384]{1,0:T(8,128)}, f32[256,384]{1,0:T(8,128)S(1)}, u32[]{:S(2)}, u32[]{:S(2)}) collective-permute-start(f32[256,384]{1,0:T(8,128)} %collective-permute-done.5.refs_7_), channel_id=1, source_target_pairs={{0,4},{1,5},{4,8},{5,9},{8,12},{9,13},{12,14},{13,15},{14,10},{15,... | collective-permute-start | bytes 1179656 | tf_op jit(solution)/shard_map/ppermute | solution.py:402
  45.5 16.9 %collective-permute-start.9 = (f32[256,384]{1,0:T(8,128)}, f32[256,384]{1,0:T(8,128)}, u32[]{:S(2)}, u32[]{:S(2)}) collective-permute-start(f32[256,384]{1,0:T(8,128)} %collective-permute-done.8.refs_8_), channel_id=1, source_target_pairs={{4,0},{5,1},{8,4},{9,5},{12,8},{13,9},{14,12},{15,13},{10,14},{11,... | collective-permute-start | bytes 1179656 | tf_op jit(solution)/shard_map/ppermute | solution.py:402
  62.4 12.2 %collective-permute-start.16 = (f32[256,384]{1,0:T(8,128)S(1)}, f32[256,384]{1,0:T(8,128)}, u32[]{:S(2)}, u32[]{:S(2)}) collective-permute-start(f32[256,384]{1,0:T(8,128)S(1)} %collective-permute-done.12.refs_3_), channel_id=1, source_target_pairs={{4,0},{5,1},{8,4},{9,5},{12,8},{13,9},{14,12},{15,13},{10,14},{11,... | collective-permute-start | bytes 1179656 | tf_op jit(solution)/shard_map/ppermute | solution.py:402
  64.0 12.2 %collective-permute-start.15 = (f32[256,384]{1,0:T(8,128)S(1)}, f32[256,384]{1,0:T(8,128)}, u32[]{:S(2)}, u32[]{:S(2)}) collective-permute-start(f32[256,384]{1,0:T(8,128)S(1)} %collective-permute-done.3.refs_0_), channel_id=1, source_target_pairs={{0,4},{1,5},{4,8},{5,9},{8,12},{9,13},{12,14},{13,15},{14,10},{15,... | collective-permute-start | bytes 1179656 | tf_op jit(solution)/shard_map/ppermute | solution.py:402
  64.4 19.2 %collective-permute-start.13 = (f32[256,384]{1,0:T(8,128)S(1)}, f32[256,384]{1,0:T(8,128)S(1)}, u32[]{:S(2)}, u32[]{:S(2)}) collective-permute-start(f32[256,384]{1,0:T(8,128)S(1)} %copy-done.9), channel_id=1, source_target_pairs={{0,4},{1,5},{4,8},{5,9},{8,12},{9,13},{12,14},{13,15},{14,10},{15,... | collective-permute-start | bytes 1179656 | tf_op jit(solution)/shard_map/ppermute | solution.py:402
  65.3 18.4 %collective-permute-start.14 = (f32[256,384]{1,0:T(8,128)S(1)}, f32[256,384]{1,0:T(8,128)S(1)}, u32[]{:S(2)}, u32[]{:S(2)}) collective-permute-start(f32[256,384]{1,0:T(8,128)S(1)} %copy-done.9), channel_id=1, source_target_pairs={{4,0},{5,1},{8,4},{9,5},{12,8},{13,9},{14,12},{15,13},{10,14},{11,... | collective-permute-start | bytes 1179656 | tf_op jit(solution)/shard_map/ppermute | solution.py:402
  85.1 11.9 %collective-permute-start.20 = (f32[1152,128]{1,0:T(8,128)S(1)}, f32[1152,128]{1,0:T(8,128)S(1)}, u32[]{:S(2)}, u32[]{:S(2)}) collective-permute-start(f32[1152,128]{1,0:T(8,128)S(1)} %dynamic-slice_bitcast_fusion), channel_id=1, source_target_pairs={{0,1},{1,0},{2,3},{3,2},{4,5},{5,4},{6,7},{7,6},{8,9},{9,8},{10,11... | collective-permute-start | bytes 1769480 | tf_op jit(solution)/shard_map/ppermute | solution.py:402
  85.2 11.5 %collective-permute-start.18 = (f32[256,384]{1,0:T(8,128)S(1)}, f32[256,384]{1,0:T(8,128)S(1)}, u32[]{:S(2)}, u32[]{:S(2)}) collective-permute-start(f32[256,384]{1,0:T(8,128)S(1)} %collective-permute-done.13.refs_1_), channel_id=1, source_target_pairs={{0,4},{1,5},{4,8},{5,9},{8,12},{9,13},{12,14},{13,15},{14,10},{15,... | collective-permute-start | bytes 1179656 | tf_op jit(solution)/shard_map/ppermute | solution.py:402
  85.7 11.3 %collective-permute-start.19 = (f32[256,384]{1,0:T(8,128)S(1)}, f32[256,384]{1,0:T(8,128)}, u32[]{:S(2)}, u32[]{:S(2)}) collective-permute-start(f32[256,384]{1,0:T(8,128)S(1)} %collective-permute-done.14.refs_2_), channel_id=1, source_target_pairs={{4,0},{5,1},{8,4},{9,5},{12,8},{13,9},{14,12},{15,13},{10,14},{11,... | collective-permute-start | bytes 1179656 | tf_op jit(solution)/shard_map/ppermute | solution.py:402
  97.0 16.9 %collective-permute-start.21 = (f32[256,384]{1,0:T(8,128)S(1)}, f32[256,384]{1,0:T(8,128)S(1)}, u32[]{:S(2)}, u32[]{:S(2)}) collective-permute-start(f32[256,384]{1,0:T(8,128)S(1)} %collective-permute-done.18.refs_3_), channel_id=1, source_target_pairs={{0,4},{1,5},{4,8},{5,9},{8,12},{9,13},{12,14},{13,15},{14,10},{15,... | collective-permute-start | bytes 1179656 | tf_op jit(solution)/shard_map/ppermute | solution.py:402
  97.9 16.0 %collective-permute-start.22 = (f32[256,384]{1,0:T(8,128)}, f32[256,384]{1,0:T(8,128)S(1)}, u32[]{:S(2)}, u32[]{:S(2)}) collective-permute-start(f32[256,384]{1,0:T(8,128)} %collective-permute-done.19.refs_4_), channel_id=1, source_target_pairs={{4,0},{5,1},{8,4},{9,5},{12,8},{13,9},{14,12},{15,13},{10,14},{11,... | collective-permute-start | bytes 1179656 | tf_op jit(solution)/shard_map/ppermute | solution.py:402
  99.2 14.7 %collective-permute-start.23 = (f32[576,128]{1,0:T(8,128)S(1)}, f32[576,128]{1,0:T(8,128)S(1)}, u32[]{:S(2)}, u32[]{:S(2)}) collective-permute-start(f32[576,128]{1,0:T(8,128)S(1)} %dynamic-slice_bitcast_fusion.1), channel_id=1, source_target_pairs={{0,2},{1,3},{2,0},{3,1},{4,6},{5,7},{6,4},{7,5},{8,10},{9,11},{10,... | collective-permute-start | bytes 884744 | tf_op jit(solution)/shard_map/ppermute | solution.py:402
  113.9 11.7 %collective-permute-start.24 = (f32[128,384]{1,0:T(8,128)S(1)}, f32[128,384]{1,0:T(8,128)S(1)}, u32[]{:S(2)}, u32[]{:S(2)}) collective-permute-start(f32[128,384]{1,0:T(8,128)S(1)} %slice.6), channel_id=1, source_target_pairs={{0,4},{1,5},{4,8},{5,9},{8,12},{9,13},{12,14},{13,15},{14,10},{15,... | collective-permute-start | bytes 589832 | tf_op jit(solution)/shard_map/ppermute | solution.py:402
  114.0 11.6 %collective-permute-start.25 = (f32[128,384]{1,0:T(8,128)S(1)}, f32[128,384]{1,0:T(8,128)S(1)}, u32[]{:S(2)}, u32[]{:S(2)}) collective-permute-start(f32[128,384]{1,0:T(8,128)S(1)} %slice.7), channel_id=1, source_target_pairs={{4,0},{5,1},{8,4},{9,5},{12,8},{13,9},{14,12},{15,13},{10,14},{11,... | collective-permute-start | bytes 589832 | tf_op jit(solution)/shard_map/ppermute | solution.py:402
  116.3 15.5 %collective-permute-start.27 = (f32[144,128]{1,0:T(8,128)S(1)}, f32[144,128]{1,0:T(8,128)S(1)}, u32[]{:S(2)}, u32[]{:S(2)}) collective-permute-start(f32[144,128]{1,0:T(8,128)S(1)} %get-tuple-element.104), channel_id=1, source_target_pairs={{0,4},{1,5},{2,6},{3,7},{4,0},{5,1},{6,2},{7,3},{8,12},{9,13},{10,... | collective-permute-start | bytes 221192 | tf_op jit(solution)/shard_map/ppermute | solution.py:402
  116.4 15.5 %collective-permute-start.28 = (f32[144,128]{1,0:T(8,128)S(1)}, f32[144,128]{1,0:T(8,128)S(1)}, u32[]{:S(2)}, u32[]{:S(2)}) collective-permute-start(f32[144,128]{1,0:T(8,128)S(1)} %get-tuple-element.106), channel_id=1, source_target_pairs={{0,8},{1,9},{2,10},{3,11},{4,12},{5,13},{6,14},{7,15},{8,0},{9,1},... | collective-permute-start | bytes 221192 | tf_op jit(solution)/shard_map/ppermute | solution.py:402
  121.1 10.8 %collective-permute-start.29 = (f32[144,128]{1,0:T(8,128)S(1)}, f32[144,128]{1,0:T(8,128)S(1)}, u32[]{:S(2)}, u32[]{:S(2)}) collective-permute-start(f32[144,128]{1,0:T(8,128)S(1)} %get-tuple-element.105), channel_id=1, source_target_pairs={{0,12},{1,13},{2,14},{3,15},{4,8},{5,9},{6,10},{7,11},{8,4},{9,5},... | collective-permute-start | bytes 221192 | tf_op jit(solution)/shard_map/ppermute | solution.py:402
  131.8 10.8 %collective-permute-start.26 = (f32[192,128]{1,0:T(8,128)S(1)}, f32[192,128]{1,0:T(8,128)S(1)}, u32[]{:S(2)}, u32[]{:S(2)}) collective-permute-start(f32[192,128]{1,0:T(8,128)S(1)} %dynamic-slice_bitcast_fusion.2), channel_id=1, source_target_pairs={{0,1},{1,0},{2,3},{3,2},{4,5},{5,4},{6,7},{7,6},{8,9},{9,8},{10,11... | collective-permute-start | bytes 294920 | tf_op jit(solution)/shard_map/ppermute | solution.py:402
  144.9 12.2 %collective-permute-start.39 = (f32[512,384]{1,0:T(8,128)S(1)}, f32[512,384]{1,0:T(8,128)S(1)}, u32[]{:S(2)}, u32[]{:S(2)}) collective-permute-start(f32[512,384]{1,0:T(8,128)S(1)} %copy-done.24), channel_id=1, source_target_pairs={{0,1},{1,0},{2,3},{3,2},{4,5},{5,4},{6,7},{7,6},{8,9},{9,8},{10,11... | collective-permute-start | bytes 2359304 | tf_op jit(solution)/shard_map/ppermute | solution.py:402
  152.6 14.0 %collective-permute-start.38 = (f32[1152,128]{1,0:T(8,128)S(1)}, f32[1152,128]{1,0:T(8,128)S(1)}, u32[]{:S(2)}, u32[]{:S(2)}) collective-permute-start(f32[1152,128]{1,0:T(8,128)S(1)} %pad_maximum_fusion.refs_0_), channel_id=1, source_target_pairs={{0,1},{1,0},{2,3},{3,2},{4,5},{5,4},{6,7},{7,6},{8,9},{9,8},{10,11... | collective-permute-start | bytes 1769480 | tf_op jit(solution)/shard_map/ppermute | solution.py:402
  (36 other events, 339.0 us)

commit v2 on v1

--- a/solution.py
+++ b/solution.py
@@ -178,8 +178,9 @@
     )(index, structure, anc_factor)
 
 
-def multiply_kernel(layout, has_start, rows_at, index_ref, own_ref, twin_ref, *refs):
+def multiply_kernel(layout, has_start, rows_at, index_ref, *refs):
     refs = list(refs)
+    sources = [refs.pop(0) for _ in range(4)]
     piece_count = sum(len(block) for block in layout)
     pieces = [refs.pop(0) for _ in range(piece_count)]
     starts = [refs.pop(0) for _ in range(2)] if has_start else None
@@ -187,39 +188,46 @@
     outs = [refs.pop(0) for _ in range(2)]
     inner_ref = refs.pop(0) if rows_at else None
     held = refs.pop(0)
+    rows = sources[0].shape[1]
     step = pl.program_id(0)
     at = 0
     for b, block in enumerate(layout):
         chosen = pieces[at : at + len(block)]
         at += len(block)
-
-        @pl.when(step == b)
-        def _(chosen=chosen, block=block):
+        left = (b % 2) * rows
+
+        @pl.when(step == b // 2)
+        def _(chosen=chosen, block=block, left=left):
             for ref, (top, height) in zip(chosen, block):
-                held[top : top + height, :] = ref[...]
+                held[top : top + height, left : left + rows] = ref[...]
 
     @pl.when(step == 0)
     def _():
         for i in range(2):
             outs[i][...] = starts[i][...] if has_start else jnp.zeros_like(outs[i])
 
-    rows = halves_of(held[...])
-    for ref, out in ((own_ref, outs[0]), (twin_ref, outs[1])):
-        out[...] += product_of(rows, halves_of(ref[...]))
+    inverse = jnp.concatenate(
+        [
+            jnp.concatenate([own[...], twin[...]], axis=1)
+            for own, twin in (sources[:2], sources[2:])
+        ],
+        axis=0,
+    )
+    value = product_of(halves_of(held[...]), halves_of(inverse))
+    for i in range(2):
+        outs[i][...] += value[:, i * rows : (i + 1) * rows]
     if rows_at:
 
-        @pl.when(step == len(layout) - 1)
+        @pl.when(step == len(layout) // 2 - 1)
         def _():
-            images = [halves_of(out[...]) for out in outs]
-            sides = [halves_of(ref[...]) for ref in factors]
+            image = halves_of(jnp.concatenate([out[...] for out in outs], axis=1))
+            side = halves_of(jnp.concatenate([ref[...] for ref in factors], axis=0))
             spot = 0
             for top, first in rows_at:
-                value = 0.0
-                for image, side in zip(images, sides):
-                    value = value + product_of(
-                        tuple(half[top : top + tile] for half in image),
-                        tuple(half[:, : first + tile] for half in side),
-                    )
+                value = product_of(
+                    tuple(half[top : top + tile] for half in image),
+                    tuple(half[:, : first + tile] for half in side),
+                )
                 for i in range(first // tile + 1):
                     inner_ref[spot * tile : (spot + 1) * tile, :] = value[
                         :, i * tile : (i + 1) * tile
@@ -243,8 +251,10 @@
     def whole(shape):
         return pl.BlockSpec(shape, lambda i, at: (0, 0))
 
-    def source(i, at):
-        return source_device(i + first, at[0], levels), 0
+    def source(side):
+        return pl.BlockSpec(
+            (rows, rows), lambda i, at: (source_device(first + 2 * i + side, at[0], levels), 0)
+        )
 
     image = jax.ShapeDtypeStruct((height, rows), jnp.float32)
     out_shape = [image, image]
@@ -256,26 +266,26 @@
         functools.partial(multiply_kernel, tuple(layout), start is not None, rows_at),
         grid_spec=pltpu.PrefetchScalarGridSpec(
             num_scalar_prefetch=1,
-            grid=(len(blocks),),
-            in_specs=[pl.BlockSpec((rows, rows), source), pl.BlockSpec((rows, rows), source)]
+            grid=(len(blocks) // 2,),
+            in_specs=[source(0), source(0), source(1), source(1)]
             + [whole(v.shape) for v in operands],
             out_specs=[whole(v.shape) for v in out_shape],
-            scratch_shapes=[pltpu.VMEM((height, rows), jnp.float32)],
+            scratch_shapes=[pltpu.VMEM((height, 2 * rows), jnp.float32)],
         ),
         out_shape=out_shape,
         compiler_params=pltpu.CompilerParams(vmem_limit_bytes=vmem_bytes),
         cost_estimate=little,
-    )(index, inverse, twin, *operands)
-
-
-def columns_kernel(width, steps, tops, *refs):
-    images, adds = refs[: len(tops)], refs[len(tops) : 2 * len(tops)]
-    factor_ref, out_ref, image = refs[2 * len(tops) :]
-    for top, ref, add_ref in zip(tops, images, adds):
-        image[top : top + ref.shape[0], :] = ref[...] + add_ref[...]
+    )(index, inverse, twin, inverse, twin, *operands)
+
+
+def columns_kernel(width, steps, image_ref, add_ref, factor_ref, out_ref):
     solved = {}
     for k in range(steps - 1, -1, -1):
-        value = image[k * width : (k + 1) * width, :]
+        if k:
+            at = slice((k - 1) * width, k * width)
+            value = image_ref[at, :] + add_ref[at, :]
+        else:
+            value = jnp.zeros((width, image_ref.shape[1]), jnp.float32)
         for j in range(k + 1, steps):
             side = factor_ref[j * width : (j + 1) * width, k * width : (k + 1) * width]
             value = value + times(side, solved[j], True)
@@ -283,15 +293,14 @@
         out_ref[:, k * width : (k + 1) * width] = solved[k].T
 
 
-def solve_columns(width, steps, tops, images, adds, win_factor):
-    rows = images[0].shape[1]
+def solve_columns(width, steps, image, add, win_factor):
+    rows = image.shape[1]
     return pl.pallas_call(
-        functools.partial(columns_kernel, width, steps, tops),
+        functools.partial(columns_kernel, width, steps),
         out_shape=jax.ShapeDtypeStruct((rows, steps * width), jnp.float32),
-        scratch_shapes=[pltpu.VMEM((steps * width, rows), jnp.float32)],
         compiler_params=pltpu.CompilerParams(vmem_limit_bytes=vmem_bytes),
         cost_estimate=little,
-    )(*images, *adds, win_factor)
+    )(image, add, win_factor)
 
 
 def fill_inner(inner, top, one, two, first_half):
@@ -309,25 +318,36 @@
         row += tile
 
 
-def add_kernel(core_ref, mine_ref, other_ref, base_ref, out_ref, inner):
+def last_kernel(
+    core_ref, mine_ref, other_ref, image_ref, add_ref, columns_ref, base_ref, *refs
+):
+    columns_out, window_out, inner = refs
+    columns_out[...] = columns_ref[...] - (image_ref[...] + add_ref[...]).T
     fill_inner(inner, 0, mine_ref[...], other_ref[...], core_ref[0] % 2 == 0)
-    out_ref[...] = base_ref[...] + inner[...]
-
-
-def add_last(index, mine, other, base, width):
-    block = pl.BlockSpec((width, width), lambda i: (0, 0))
+    window_out[...] = base_ref[...] + inner[...]
+
+
+def add_last(index, mine, other, image, add, columns, base):
+    width, rows = image.shape
+    column_block = pl.BlockSpec((rows, width), lambda i: (0, 0))
+    window_block = pl.BlockSpec((width, width), lambda i: (0, 0))
     part = pl.BlockSpec(mine.shape, lambda i: (0, 0))
+    whole = pl.BlockSpec(image.shape, lambda i: (0, 0))
     return pl.pallas_call(
-        add_kernel,
+        last_kernel,
         grid=(1,),
-        in_specs=[pl.BlockSpec(memory_space=pltpu.SMEM), part, part, block],
-        out_specs=block,
-        out_shape=jax.ShapeDtypeStruct(base.shape, jnp.float32),
-        input_output_aliases={3: 0},
+        in_specs=[pl.BlockSpec(memory_space=pltpu.SMEM), part, part, whole, whole]
+        + [column_block, window_block],
+        out_specs=[column_block, window_block],
+        out_shape=[
+            jax.ShapeDtypeStruct(columns.shape, jnp.float32),
+            jax.ShapeDtypeStruct(base.shape, jnp.float32),
+        ],
+        input_output_aliases={5: 0, 6: 1},
         scratch_shapes=[pltpu.VMEM((width, width), jnp.float32)],
         compiler_params=pltpu.CompilerParams(vmem_limit_bytes=vmem_bytes),
         cost_estimate=little,
-    )(index, mine, other, base)
+    )(index, mine, other, image, add, columns, base)
 
 
 def window_kernel(width, steps, tops, core_ref, *refs):
@@ -486,57 +506,59 @@
     hold = lax.optimization_barrier
     ring_a = ring(turned[: len(plan[0])])
     pieces_b = turned[len(plan[0]) :]
-    ups, _ = next(ring_a)
-    a = [ups]
-    ups, downs = next(ring_a)
-    for s in range(2, half_way):
-        a += [ups, downs]
-        ups, downs = ring_a.send((ups, downs))
-    near = product(0, a)
-    (ups, downs), near = hold(((ups, downs), near))
-    pieces_b, downs = hold((pieces_b, downs))
-    far = ring_a.send((ups, downs))
+    a = [next(ring_a)[0]]
+    ups_a, downs_a = next(ring_a)
+    a += [ups_a, downs_a]
+    ups_a, downs_a = ring_a.send((ups_a, downs_a))
+    a += [ups_a, downs_a]
+    ups_a, downs_a = ring_a.send((ups_a, downs_a))
+    near = product(0, a[:4])
+    (ups_a, downs_a), near = hold(((ups_a, downs_a), near))
+    pieces_b, downs_a = hold((pieces_b, downs_a))
+    far = ring_a.send((ups_a, downs_a))
+    a += [ups_a, downs_a, far]
     ring_b = ring(pieces_b)
     b = [next(ring_b)[0]]
     ups_b, downs_b = next(ring_b)
-    mid = product(5, [ups, downs], near)
-    mine_a, theirs_a, local = product(7, [far], mid, strips(plan[0]))
+    mid = product(4, a[4:6], near)
+    mine_a, theirs_a, local = product(6, a[6:], mid, strips(plan[0]))
     (ups_b, downs_b), local = hold(((ups_b, downs_b), local))
     sum_a = sum_large(local)
     got = next(sum_a)
+    got = sum_a.send(got)
     b += [ups_b, downs_b]
     ups_b, downs_b = ring_b.send((ups_b, downs_b))
-    (ups_b, downs_b), got = hold(((ups_b, downs_b), got))
-    got = sum_a.send(got)
     adds_a = send(theirs_a, flip(1))
     b += [ups_b, downs_b]
-    near = product(0, b)
-    ups_b, downs_b = ring_b.send((ups_b, downs_b))
+    near = product(0, b[:4])
     (ups_b, downs_b), got, near = hold(((ups_b, downs_b), got, near))
     got = sum_a.send(got)
-    far = ring_b.send((ups_b, downs_b))
-    mid = product(5, [ups_b, downs_b], near)
+    ups_b, downs_b = ring_b.send((ups_b, downs_b))
+    b += [ups_b, downs_b]
+    mid = product(4, b[4:6], near)
+    columns = solve_columns(width, steps_total, mine_a, adds_a, win_factor)
+    got, mid, columns = hold((got, mid, columns))
     got = sum_a.send(got)
-    mine_b, theirs_b, local = product(7, [far], mid, strips(plan[1]))
+    b += [ring_b.send((ups_b, downs_b))]
+    mine_b, theirs_b, local = product(6, b[6:], mid, strips(plan[1]))
+    adds_b = send(theirs_b, flip(1))
     sum_b = sum_small(local)
     got_b = next(sum_b)
+    got = sum_a.send(got)
     got_b, got = hold((got_b, got))
+    got_b = sum_b.send(got_b)
     got = sum_a.send(got)
-    got_b = sum_b.send(got_b)
-    adds_b = send(theirs_b, flip(1))
     got_b, got = hold((got_b, got))
-    got = sum_a.send(got)
-    got_b = sum_b.send(got_b)
-    tops = [plan[0][0][0], plan[1][0][0]]
-    images, adds = [mine_a, mine_b], [adds_a, adds_b]
-    anc_columns = solve_columns(width, steps_total, tops, images, adds, win_factor)
-    got_b, got, anc_columns = hold((got_b, got, anc_columns))
     got_b = sum_b.send(got_b)
     mine, other = sum_a.send(got)
     base = window_blocks_of(
-        width, steps_total, tops[:1], at, [mine], [other], win_factor, pivot_inverse
-    )
-    win_inverse = add_last(at, *sum_b.send(got_b), base, width)
+        width, steps_total, (width,), at, [mine], [other], win_factor, pivot_inverse
+    )
+    got_b, base = hold((got_b, base))
+    got_b = sum_b.send(got_b)
+    anc_columns, win_inverse = add_last(
+        at, *sum_b.send(got_b), mine_b, adds_b, columns, base
+    )
     return (anc_columns, win_inverse)
 
 

time: 176 us -> 166 us (0.943)
  Pallas kernels: 58.7 us -> 54 us
  waiting for transfers between devices: 67.4 us -> 62.8 us
  starting transfers between devices: 42.8 us -> 40.7 us
    pallas_call x6, Pallas kernels: 43.7 us -> 38.8 us  [multiply(): pl.pallas_call(functools.partial(multiply_kernel, tuple(layout), start is...]
    ppermute x42, waiting for transfers between devices: 67.4 us -> 62.8 us  [send(): return lax.ppermute(value, 'pcol', pairs)]
    ppermute x42, starting transfers between devices: 42.8 us -> 40.7 us  [send(): return lax.ppermute(value, 'pcol', pairs)]
    unnamed x52 -> x54, local copies, waits for them, and re-layouts: 2.91 us -> 3.94 us
  transfers between devices with their start and end apart: 42 -> 42, of which waited for: 15 -> 18; matrix products, arithmetic and copies ran while one was open for 1% -> 1% of each run, Pallas kernels for 32% -> 31%
where the time goes in v2:
time: 166 us
  waiting for transfers between devices  62.8 us (38%)
  Pallas kernels  54 us (33%)
  starting transfers between devices  40.7 us (25%)
  local copies, waits for them, and re-layouts  7.05 us (4%)
    ppermute x42, waiting for transfers between devices, send(): return lax.ppermute(value, 'pcol', pairs)  62.8 us
    ppermute x42, starting transfers between devices, send(): return lax.ppermute(value, 'pcol', pairs)  40.7 us
    pallas_call x6, Pallas kernels, multiply(): pl.pallas_call(functools.partial(multiply_kernel, tuple(layout), start is...  38.8 us
    pallas_call x1, Pallas kernels, window_blocks_of(): pl.pallas_call(functools.partial(window_kernel, width, steps, tops), in_s...  5.67 us
    pallas_call x1, Pallas kernels, solve_columns(): pl.pallas_call(functools.partial(columns_kernel, width, steps), out_shape...  4.29 us
    unnamed x54, local copies, waits for them, and re-layouts  3.94 us
  transfers between devices with their start and end apart: 42, of which 18 were waited for; matrix products, arithmetic and copies ran while one was open for 1% of the time, Pallas kernels for 31%

profile of v2, /device:TPU:0, one launch (start us, length us, event | category | flops | bytes accessed | tf_op | source)
XLA Modules:
  0.0 165.8 jit_solution(12036016196953310155)
XLA Ops:
  1.1 2.9 %shard_map.68 = (f32[384,768]{1,0:T(8,128)}, f32[256,384]{1,0:T(8,128)}, f32[256,384]{1,0:T(8,128)}, f32[256,384]{1,0:T(8,128)}) custom-call(s32[1]{0:T(128)} %bitcast.index_ref.core_ref, s32[3,24]{1,0:T(4,128)} %structure_ref.1, f32[384,768]{1,0:T(8,128)} %factor_ref.2), custom_call_target="tpu_custom_call" | custom-call | flops 1 | bytes 1 | tf_op jit(solution)/shard_map/pallas_call | solution.py:170
  4.0 2.6 %collective-permute-start.1 = (f32[256,384]{1,0:T(8,128)}, f32[256,384]{1,0:T(8,128)S(1)}, u32[]{:S(2)}, u32[]{:S(2)}) collective-permute-start(f32[256,384]{1,0:T(8,128)} %get-tuple-element.52.refs_4_), channel_id=1, source_target_pairs={{0,4},{1,5},{4,8},{5,9},{8,12},{9,13},{12,14},{13,15},{14,10},{15,... | collective-permute-start | bytes 1179656 | tf_op jit(solution)/shard_map/ppermute | solution.py:422
  6.6 2.0 %collective-permute-start.4 = (f32[256,384]{1,0:T(8,128)}, f32[256,384]{1,0:T(8,128)S(1)}, u32[]{:S(2)}, u32[]{:S(2)}) collective-permute-start(f32[256,384]{1,0:T(8,128)} %get-tuple-element.53.refs_5_), channel_id=1, source_target_pairs={{0,4},{1,5},{4,8},{5,9},{8,12},{9,13},{12,14},{13,15},{14,10},{15,... | collective-permute-start | bytes 1179656 | tf_op jit(solution)/shard_map/ppermute | solution.py:422
  8.6 8.1 %collective-permute-done.1.refs_6_ = f32[256,384]{1,0:T(8,128)S(1)} collective-permute-done((f32[256,384]{1,0:T(8,128)}, f32[256,384]{1,0:T(8,128)S(1)}, u32[]{:S(2)}, u32[]{:S(2)}) %collective-permute-start.1) | collective-permute-done | bytes 393248 | tf_op jit(solution)/shard_map/ppermute | solution.py:422
  16.7 2.0 %collective-permute-start.2 = (f32[256,384]{1,0:T(8,128)S(1)}, f32[256,384]{1,0:T(8,128)}, u32[]{:S(2)}, u32[]{:S(2)}) collective-permute-start(f32[256,384]{1,0:T(8,128)S(1)} %collective-permute-done.1.refs_6_), channel_id=1, source_target_pairs={{0,4},{1,5},{4,8},{5,9},{8,12},{9,13},{12,14},{13,15},{14,10},{15,... | collective-permute-start | bytes 1179656 | tf_op jit(solution)/shard_map/ppermute | solution.py:422
  18.8 6.3 %collective-permute-done.4.refs_7_ = f32[256,384]{1,0:T(8,128)S(1)} collective-permute-done((f32[256,384]{1,0:T(8,128)}, f32[256,384]{1,0:T(8,128)S(1)}, u32[]{:S(2)}, u32[]{:S(2)}) %collective-permute-start.4) | collective-permute-done | bytes 393248 | tf_op jit(solution)/shard_map/ppermute | solution.py:422
  25.1 2.0 %collective-permute-start.5 = (f32[256,384]{1,0:T(8,128)S(1)}, f32[256,384]{1,0:T(8,128)}, u32[]{:S(2)}, u32[]{:S(2)}) collective-permute-start(f32[256,384]{1,0:T(8,128)S(1)} %collective-permute-done.4.refs_7_), channel_id=1, source_target_pairs={{0,4},{1,5},{4,8},{5,9},{8,12},{9,13},{12,14},{13,15},{14,10},{15,... | collective-permute-start | bytes 1179656 | tf_op jit(solution)/shard_map/ppermute | solution.py:422
  27.2 6.5 %collective-permute-done.2.refs_10_ = f32[256,384]{1,0:T(8,128)} collective-permute-done((f32[256,384]{1,0:T(8,128)S(1)}, f32[256,384]{1,0:T(8,128)}, u32[]{:S(2)}, u32[]{:S(2)}) %collective-permute-start.2) | collective-permute-done | bytes 393248 | tf_op jit(solution)/shard_map/ppermute | solution.py:422
  33.7 2.0 %collective-permute-done.11.refs_5_ = f32[256,384]{1,0:T(8,128)S(1)} collective-permute-done((f32[256,384]{1,0:T(8,128)S(1)}, f32[256,384]{1,0:T(8,128)S(1)}, u32[]{:S(2)}, u32[]{:S(2)}) %collective-permute-start.11) | collective-permute-done | bytes 393248 | tf_op jit(solution)/shard_map/ppermute | solution.py:422
  35.7 6.2 %collective-permute-done.5.refs_11_ = f32[256,384]{1,0:T(8,128)} collective-permute-done((f32[256,384]{1,0:T(8,128)S(1)}, f32[256,384]{1,0:T(8,128)}, u32[]{:S(2)}, u32[]{:S(2)}) %collective-permute-start.5) | collective-permute-done | bytes 393248 | tf_op jit(solution)/shard_map/ppermute | solution.py:422
  41.9 1.8 %collective-permute-start.3 = (f32[256,384]{1,0:T(8,128)}, f32[256,384]{1,0:T(8,128)S(1)}, u32[]{:S(2)}, u32[]{:S(2)}) collective-permute-start(f32[256,384]{1,0:T(8,128)} %collective-permute-done.2.refs_10_), channel_id=1, source_target_pairs={{0,4},{1,5},{4,8},{5,9},{8,12},{9,13},{12,14},{13,15},{14,10},{15,... | collective-permute-start | bytes 1179656 | tf_op jit(solution)/shard_map/ppermute | solution.py:422
  46.1 8.4 %shard_map.69 = (f32[512,384]{1,0:T(8,128)}, f32[512,384]{1,0:T(8,128)}) custom-call(s32[1]{0:T(128)} %bitcast.index_ref.core_ref, f32[6144,384]{1,0:T(8,128)} %refs_2_.12, f32[6144,384]{1,0:T(8,128)} %collective-permute-done.refs_1_.refs_3_, f32[6144,384]{1,0:T(8,128)} %refs_2_.12, f32[6144,384]{1,0:T(8,128)} %collective-permute-done.refs_1_.refs_3_, ...), custom_call_target="tpu_custom_call" | custom-call | flops 1 | bytes 1 | tf_op jit(solution)/shard_map/pallas_call | solution.py:265
  54.6 6.9 %collective-permute-done.6.refs_7_ = f32[256,384]{1,0:T(8,128)S(1)} collective-permute-done((f32[256,384]{1,0:T(8,128)}, f32[256,384]{1,0:T(8,128)S(1)}, u32[]{:S(2)}, u32[]{:S(2)}) %collective-permute-start.6) | collective-permute-done | bytes 393248 | tf_op jit(solution)/shard_map/ppermute | solution.py:422
  63.5 1.6 collective-permute-start.13
  65.6 5.8 %shard_map.70 = (f32[512,384]{1,0:T(8,128)}, f32[512,384]{1,0:T(8,128)}) custom-call(s32[1]{0:T(128)} %bitcast.index_ref.core_ref, f32[6144,384]{1,0:T(8,128)} %refs_2_.12, f32[6144,384]{1,0:T(8,128)} %collective-permute-done.refs_1_.refs_3_, f32[6144,384]{1,0:T(8,128)} %refs_2_.12, f32[6144,384]{1,0:T(8,128)} %collective-permute-done.refs_1_.refs_3_, ...), custom_call_target="tpu_custom_call" | custom-call | flops 1 | bytes 1 | tf_op jit(solution)/shard_map/pallas_call | solution.py:265
  71.3 2.2 %collective-permute-done.16.refs_7_ = f32[256,384]{1,0:T(8,128)S(1)} collective-permute-done((f32[256,384]{1,0:T(8,128)S(1)}, f32[256,384]{1,0:T(8,128)S(1)}, u32[]{:S(2)}, u32[]{:S(2)}) %collective-permute-start.16) | collective-permute-done | bytes 393248 | tf_op jit(solution)/shard_map/ppermute | solution.py:422
  75.9 9.4 %shard_map.71 = (f32[512,384]{1,0:T(8,128)}, f32[512,384]{1,0:T(8,128)}, f32[2304,128]{1,0:T(8,128)}) custom-call(s32[1]{0:T(128)} %bitcast.index_ref.core_ref, f32[6144,384]{1,0:T(8,128)} %refs_2_.12, f32[6144,384]{1,0:T(8,128)} %collective-permute-done.refs_1_.refs_3_, f32[6144,384]{1,0:T(8,128)} %refs_2_.12, ...), custom_call_target="tpu_custom_call" | custom-call | flops 1 | bytes 1 | tf_op jit(solution)/shard_map/pallas_call | solution.py:265
  89.2 1.6 collective-permute-start.21
  90.8 8.5 %collective-permute-done.18.refs_7_ = f32[256,384]{1,0:T(8,128)} collective-permute-done((f32[256,384]{1,0:T(8,128)}, f32[256,384]{1,0:T(8,128)}, u32[]{:S(2)}, u32[]{:S(2)}) %collective-permute-start.18) | collective-permute-done | bytes 393248 | tf_op jit(solution)/shard_map/ppermute | solution.py:422
  99.3 5.6 %shard_map.72 = (f32[256,384]{1,0:T(8,128)}, f32[256,384]{1,0:T(8,128)}) custom-call(s32[1]{0:T(128)} %bitcast.index_ref.core_ref, f32[6144,384]{1,0:T(8,128)} %refs_2_.12, f32[6144,384]{1,0:T(8,128)} %collective-permute-done.refs_1_.refs_3_, f32[6144,384]{1,0:T(8,128)} %refs_2_.12, f32[6144,384]{1,0:T(8,128)} %collective-permute-done.refs_1_.refs_3_, ...), custom_call_target="tpu_custom_call" | custom-call | flops 1 | bytes 1 | tf_op jit(solution)/shard_map/pallas_call | solution.py:265
  105.6 2.0 %collective-permute-start.22 = (f32[256,384]{1,0:T(8,128)}, f32[256,384]{1,0:T(8,128)S(1)}, u32[]{:S(2)}, u32[]{:S(2)}) collective-permute-start(f32[256,384]{1,0:T(8,128)} %copy-done.21), channel_id=1, source_target_pairs={{4,0},{5,1},{8,4},{9,5},{12,8},{13,9},{14,12},{15,13},{10,14},{11,... | collective-permute-start | bytes 1179656 | tf_op jit(solution)/shard_map/ppermute | solution.py:422
  107.8 3.5 %collective-permute-start.27 = (f32[144,128]{1,0:T(8,128)S(1)}, f32[144,128]{1,0:T(8,128)S(1)}, u32[]{:S(2)}, u32[]{:S(2)}) collective-permute-start(f32[144,128]{1,0:T(8,128)S(1)} %get-tuple-element.105), channel_id=1, source_target_pairs={{0,8},{1,9},{2,10},{3,11},{4,12},{5,13},{6,14},{7,15},{8,0},{9,1},... | collective-permute-start | bytes 221192 | tf_op jit(solution)/shard_map/ppermute | solution.py:422
  112.2 4.3 %shard_map.74.columns_ref = f32[384,768]{1,0:T(8,128)} custom-call(f32[512,384]{1,0:T(8,128)} %get-tuple-element.81.image_ref, f32[512,384]{1,0:T(8,128)} %copy-done.5, f32[768,768]{1,0:T(8,128)} %refs_2_.13), custom_call_target="tpu_custom_call" | custom-call | flops 1 | bytes 1 | tf_op jit(solution)/shard_map/pallas_call | solution.py:298
  117.3 4.1 %shard_map.73 = (f32[256,384]{1,0:T(8,128)}, f32[256,384]{1,0:T(8,128)}) custom-call(s32[1]{0:T(128)} %bitcast.index_ref.core_ref, f32[6144,384]{1,0:T(8,128)} %refs_2_.12, f32[6144,384]{1,0:T(8,128)} %collective-permute-done.refs_1_.refs_3_, f32[6144,384]{1,0:T(8,128)} %refs_2_.12, f32[6144,384]{1,0:T(8,128)} %collective-permute-done.refs_1_.refs_3_, ...), custom_call_target="tpu_custom_call" | custom-call | flops 1 | bytes 1 | tf_op jit(solution)/shard_map/pallas_call | solution.py:265
  121.4 1.9 %collective-permute-done.28 = f32[144,128]{1,0:T(8,128)S(1)} collective-permute-done((f32[144,128]{1,0:T(8,128)S(1)}, f32[144,128]{1,0:T(8,128)S(1)}, u32[]{:S(2)}, u32[]{:S(2)}) %collective-permute-start.28) | collective-permute-done | bytes 73760 | tf_op jit(solution)/shard_map/ppermute | solution.py:422
  124.3 2.5 %collective-permute-start.32 = (f32[144,128]{1,0:T(8,128)S(1)}, f32[144,128]{1,0:T(8,128)S(1)}, u32[]{:S(2)}, u32[]{:S(2)}) collective-permute-start(f32[144,128]{1,0:T(8,128)S(1)} %fusion.3), channel_id=1, source_target_pairs={{0,8},{1,9},{2,10},{3,11},{4,12},{5,13},{6,14},{7,15},{8,0},{9,1},... | collective-permute-start | bytes 221192 | tf_op jit(solution)/shard_map/ppermute | solution.py:422
  131.2 2.6 %collective-permute-done.33 = f32[144,128]{1,0:T(8,128)S(1)} collective-permute-done((f32[144,128]{1,0:T(8,128)S(1)}, f32[144,128]{1,0:T(8,128)S(1)}, u32[]{:S(2)}, u32[]{:S(2)}) %collective-permute-start.33) | collective-permute-done | bytes 73760 | tf_op jit(solution)/shard_map/ppermute | solution.py:422
  136.8 5.6 %shard_map.75 = (f32[256,384]{1,0:T(8,128)}, f32[256,384]{1,0:T(8,128)}, f32[384,128]{1,0:T(8,128)}) custom-call(s32[1]{0:T(128)} %bitcast.index_ref.core_ref, f32[6144,384]{1,0:T(8,128)} %refs_2_.12, f32[6144,384]{1,0:T(8,128)} %collective-permute-done.refs_1_.refs_3_, f32[6144,384]{1,0:T(8,128)} %refs_2_.12, ...), custom_call_target="tpu_custom_call" | custom-call | flops 1 | bytes 1 | tf_op jit(solution)/shard_map/pallas_call | solution.py:265
  146.0 4.1 %collective-permute-done.35 = f32[192,128]{1,0:T(8,128)S(1)} collective-permute-done((f32[192,128]{1,0:T(8,128)S(1)}, f32[192,128]{1,0:T(8,128)S(1)}, u32[]{:S(2)}, u32[]{:S(2)}) %collective-permute-start.35) | collective-permute-done | bytes 98336 | tf_op jit(solution)/shard_map/ppermute | solution.py:422
  152.5 2.1 %collective-permute-start.39 = (f32[192,128]{1,0:T(8,128)S(1)}, f32[192,128]{1,0:T(8,128)S(1)}, u32[]{:S(2)}, u32[]{:S(2)}) collective-permute-start(f32[192,128]{1,0:T(8,128)S(1)} %add.98), channel_id=1, source_target_pairs={{0,12},{1,13},{2,14},{3,15},{4,8},{5,9},{6,10},{7,11},{8,4},{9,5},... | collective-permute-start | bytes 294920 | tf_op jit(solution)/shard_map/ppermute | solution.py:422
  154.6 5.7 %shard_map.76.base_ref = f32[768,768]{1,0:T(8,128)} custom-call(s32[1]{0:T(128)} %bitcast.index_ref.core_ref, f32[1152,128]{1,0:T(8,128)} %copy-done.1, f32[1152,128]{1,0:T(8,128)} %copy-done.6, f32[768,768]{1,0:T(8,128)} %refs_2_.13, f32[3,256,256]{2,1,0:T(8,128)} %refs_3_.1), custom_call_target="tpu_custom_call" | custom-call | flops 1 | bytes 1 | tf_op jit(solution)/shard_map/pallas_call | solution.py:389
  163.4 2.4 %shard_map.77 = (f32[384,768]{1,0:T(8,128)}, f32[768,768]{1,0:T(8,128)}) custom-call(s32[1]{0:T(128)} %bitcast.index_ref.core_ref, f32[192,128]{1,0:T(8,128)} %copy-done.20, f32[192,128]{1,0:T(8,128)} %copy-done.25, f32[256,384]{1,0:T(8,128)} %get-tuple-element.96.image_ref, f32[256,384]{1,0:T(8,128)} %copy-done.19, ...), custom_call_target="tpu_custom_call", output_to_operand_aliasing={{0}: (5, {}), {1}: (6, {})} | custom-call | flops 1 | bytes 1 | tf_op jit(solution)/shard_map/pallas_call | solution.py:336
  (134 shorter events, 31.8 us)
Async XLA Ops:
  0.6 45.0 %collective-permute-start = (f32[6144,384]{1,0:T(8,128)}, f32[6144,384]{1,0:T(8,128)}, u32[]{:S(2)}, u32[]{:S(2)}) collective-permute-start(f32[6144,384]{1,0:T(8,128)} %refs_2_.12), channel_id=1, source_target_pairs={{0,1},{1,0},{2,3},{3,2},{4,5},{5,4},{6,7},{7,6},{8,9},{9,8},{10,11... | collective-permute-start | bytes 28311560 | tf_op jit(solution)/shard_map/ppermute | solution.py:422
  4.0 12.7 %collective-permute-start.1 = (f32[256,384]{1,0:T(8,128)}, f32[256,384]{1,0:T(8,128)S(1)}, u32[]{:S(2)}, u32[]{:S(2)}) collective-permute-start(f32[256,384]{1,0:T(8,128)} %get-tuple-element.52.refs_4_), channel_id=1, source_target_pairs={{0,4},{1,5},{4,8},{5,9},{8,12},{9,13},{12,14},{13,15},{14,10},{15,... | collective-permute-start | bytes 1179656 | tf_op jit(solution)/shard_map/ppermute | solution.py:422
  6.6 12.2 %collective-permute-start.10 = (f32[256,384]{1,0:T(8,128)}, f32[256,384]{1,0:T(8,128)S(1)}, u32[]{:S(2)}, u32[]{:S(2)}) collective-permute-start(f32[256,384]{1,0:T(8,128)} %get-tuple-element.53.refs_5_), channel_id=1, source_target_pairs={{4,0},{5,1},{8,4},{9,5},{12,8},{13,9},{14,12},{15,13},{10,14},{11,... | collective-permute-start | bytes 1179656 | tf_op jit(solution)/shard_map/ppermute | solution.py:422
  6.6 18.5 %collective-permute-start.4 = (f32[256,384]{1,0:T(8,128)}, f32[256,384]{1,0:T(8,128)S(1)}, u32[]{:S(2)}, u32[]{:S(2)}) collective-permute-start(f32[256,384]{1,0:T(8,128)} %get-tuple-element.53.refs_5_), channel_id=1, source_target_pairs={{0,4},{1,5},{4,8},{5,9},{8,12},{9,13},{12,14},{13,15},{14,10},{15,... | collective-permute-start | bytes 1179656 | tf_op jit(solution)/shard_map/ppermute | solution.py:422
  8.6 18.6 %collective-permute-start.7 = (f32[256,384]{1,0:T(8,128)}, f32[256,384]{1,0:T(8,128)S(1)}, u32[]{:S(2)}, u32[]{:S(2)}) collective-permute-start(f32[256,384]{1,0:T(8,128)} %get-tuple-element.52.refs_4_), channel_id=1, source_target_pairs={{4,0},{5,1},{8,4},{9,5},{12,8},{13,9},{14,12},{15,13},{10,14},{11,... | collective-permute-start | bytes 1179656 | tf_op jit(solution)/shard_map/ppermute | solution.py:422
  16.7 17.0 %collective-permute-start.2 = (f32[256,384]{1,0:T(8,128)S(1)}, f32[256,384]{1,0:T(8,128)}, u32[]{:S(2)}, u32[]{:S(2)}) collective-permute-start(f32[256,384]{1,0:T(8,128)S(1)} %collective-permute-done.1.refs_6_), channel_id=1, source_target_pairs={{0,4},{1,5},{4,8},{5,9},{8,12},{9,13},{12,14},{13,15},{14,10},{15,... | collective-permute-start | bytes 1179656 | tf_op jit(solution)/shard_map/ppermute | solution.py:422
  18.8 16.9 %collective-permute-start.11 = (f32[256,384]{1,0:T(8,128)S(1)}, f32[256,384]{1,0:T(8,128)S(1)}, u32[]{:S(2)}, u32[]{:S(2)}) collective-permute-start(f32[256,384]{1,0:T(8,128)S(1)} %collective-permute-done.10.refs_9_), channel_id=1, source_target_pairs={{4,0},{5,1},{8,4},{9,5},{12,8},{13,9},{14,12},{15,13},{10,14},{11,... | collective-permute-start | bytes 1179656 | tf_op jit(solution)/shard_map/ppermute | solution.py:422
  25.1 16.8 %collective-permute-start.5 = (f32[256,384]{1,0:T(8,128)S(1)}, f32[256,384]{1,0:T(8,128)}, u32[]{:S(2)}, u32[]{:S(2)}) collective-permute-start(f32[256,384]{1,0:T(8,128)S(1)} %collective-permute-done.4.refs_7_), channel_id=1, source_target_pairs={{0,4},{1,5},{4,8},{5,9},{8,12},{9,13},{12,14},{13,15},{14,10},{15,... | collective-permute-start | bytes 1179656 | tf_op jit(solution)/shard_map/ppermute | solution.py:422
  27.2 16.9 %collective-permute-start.8 = (f32[256,384]{1,0:T(8,128)S(1)}, f32[256,384]{1,0:T(8,128)S(1)}, u32[]{:S(2)}, u32[]{:S(2)}) collective-permute-start(f32[256,384]{1,0:T(8,128)S(1)} %collective-permute-done.7.refs_8_), channel_id=1, source_target_pairs={{4,0},{5,1},{8,4},{9,5},{12,8},{13,9},{14,12},{15,13},{10,14},{11,... | collective-permute-start | bytes 1179656 | tf_op jit(solution)/shard_map/ppermute | solution.py:422
  33.7 37.7 %collective-permute-start.17 = (f32[384,768]{1,0:T(8,128)}, f32[384,768]{1,0:T(8,128)S(1)}, u32[]{:S(2)}, u32[]{:S(2)}) collective-permute-start(f32[384,768]{1,0:T(8,128)} %get-tuple-element.67.refs_10_.refs_9_), channel_id=1, source_target_pairs={{0,1},{1,0},{2,3},{3,2},{4,5},{5,4},{6,7},{7,6},{8,9},{9,8},{10,11... | collective-permute-start | bytes 3538952 | tf_op jit(solution)/shard_map/ppermute | solution.py:422
  35.6 18.9 %collective-permute-start.12 = (f32[256,384]{1,0:T(8,128)S(1)}, f32[256,384]{1,0:T(8,128)S(1)}, u32[]{:S(2)}, u32[]{:S(2)}) collective-permute-start(f32[256,384]{1,0:T(8,128)S(1)} %collective-permute-done.11.refs_5_), channel_id=1, source_target_pairs={{4,0},{5,1},{8,4},{9,5},{12,8},{13,9},{14,12},{15,13},{10,14},{11,... | collective-permute-start | bytes 1179656 | tf_op jit(solution)/shard_map/ppermute | solution.py:422
  41.9 12.7 %collective-permute-start.3 = (f32[256,384]{1,0:T(8,128)}, f32[256,384]{1,0:T(8,128)S(1)}, u32[]{:S(2)}, u32[]{:S(2)}) collective-permute-start(f32[256,384]{1,0:T(8,128)} %collective-permute-done.2.refs_10_), channel_id=1, source_target_pairs={{0,4},{1,5},{4,8},{5,9},{8,12},{9,13},{12,14},{13,15},{14,10},{15,... | collective-permute-start | bytes 1179656 | tf_op jit(solution)/shard_map/ppermute | solution.py:422
  44.1 17.4 %collective-permute-start.6 = (f32[256,384]{1,0:T(8,128)}, f32[256,384]{1,0:T(8,128)S(1)}, u32[]{:S(2)}, u32[]{:S(2)}) collective-permute-start(f32[256,384]{1,0:T(8,128)} %collective-permute-done.5.refs_11_), channel_id=1, source_target_pairs={{0,4},{1,5},{4,8},{5,9},{8,12},{9,13},{12,14},{13,15},{14,10},{15,... | collective-permute-start | bytes 1179656 | tf_op jit(solution)/shard_map/ppermute | solution.py:422
  45.6 15.8 %collective-permute-start.9 = (f32[256,384]{1,0:T(8,128)S(1)}, f32[256,384]{1,0:T(8,128)S(1)}, u32[]{:S(2)}, u32[]{:S(2)}) collective-permute-start(f32[256,384]{1,0:T(8,128)S(1)} %collective-permute-done.8.refs_4_), channel_id=1, source_target_pairs={{4,0},{5,1},{8,4},{9,5},{12,8},{13,9},{14,12},{15,13},{10,14},{11,... | collective-permute-start | bytes 1179656 | tf_op jit(solution)/shard_map/ppermute | solution.py:422
  61.5 12.1 %collective-permute-start.16 = (f32[256,384]{1,0:T(8,128)S(1)}, f32[256,384]{1,0:T(8,128)S(1)}, u32[]{:S(2)}, u32[]{:S(2)}) collective-permute-start(f32[256,384]{1,0:T(8,128)S(1)} %collective-permute-done.12.refs_5_), channel_id=1, source_target_pairs={{4,0},{5,1},{8,4},{9,5},{12,8},{13,9},{14,12},{15,13},{10,14},{11,... | collective-permute-start | bytes 1179656 | tf_op jit(solution)/shard_map/ppermute | solution.py:422
  63.0 12.1 %collective-permute-start.15 = (f32[256,384]{1,0:T(8,128)S(1)}, f32[256,384]{1,0:T(8,128)S(1)}, u32[]{:S(2)}, u32[]{:S(2)}) collective-permute-start(f32[256,384]{1,0:T(8,128)S(1)} %collective-permute-done.3.refs_6_), channel_id=1, source_target_pairs={{0,4},{1,5},{4,8},{5,9},{8,12},{9,13},{12,14},{13,15},{14,10},{15,... | collective-permute-start | bytes 1179656 | tf_op jit(solution)/shard_map/ppermute | solution.py:422
  63.5 21.7 %collective-permute-start.13 = (f32[256,384]{1,0:T(8,128)}, f32[256,384]{1,0:T(8,128)}, u32[]{:S(2)}, u32[]{:S(2)}) collective-permute-start(f32[256,384]{1,0:T(8,128)} %get-tuple-element.58.refs_4_), channel_id=1, source_target_pairs={{0,4},{1,5},{4,8},{5,9},{8,12},{9,13},{12,14},{13,15},{14,10},{15,... | collective-permute-start | bytes 1179656 | tf_op jit(solution)/shard_map/ppermute | solution.py:422
  65.2 20.1 %collective-permute-start.14 = (f32[256,384]{1,0:T(8,128)}, f32[256,384]{1,0:T(8,128)}, u32[]{:S(2)}, u32[]{:S(2)}) collective-permute-start(f32[256,384]{1,0:T(8,128)} %get-tuple-element.58.refs_4_), channel_id=1, source_target_pairs={{4,0},{5,1},{8,4},{9,5},{12,8},{13,9},{14,12},{15,13},{10,14},{11,... | collective-permute-start | bytes 1179656 | tf_op jit(solution)/shard_map/ppermute | solution.py:422
  86.6 24.7 %collective-permute-start.29 = (f32[512,384]{1,0:T(8,128)}, f32[512,384]{1,0:T(8,128)S(1)}, u32[]{:S(2)}, u32[]{:S(2)}) collective-permute-start(f32[512,384]{1,0:T(8,128)} %get-tuple-element.82), channel_id=1, source_target_pairs={{0,1},{1,0},{2,3},{3,2},{4,5},{5,4},{6,7},{7,6},{8,9},{9,8},{10,11... | collective-permute-start | bytes 2359304 | tf_op jit(solution)/shard_map/ppermute | solution.py:422
  87.0 12.3 %collective-permute-start.18 = (f32[256,384]{1,0:T(8,128)}, f32[256,384]{1,0:T(8,128)}, u32[]{:S(2)}, u32[]{:S(2)}) collective-permute-start(f32[256,384]{1,0:T(8,128)} %collective-permute-done.13.refs_5_), channel_id=1, source_target_pairs={{0,4},{1,5},{4,8},{5,9},{8,12},{9,13},{12,14},{13,15},{14,10},{15,... | collective-permute-start | bytes 1179656 | tf_op jit(solution)/shard_map/ppermute | solution.py:422
  87.5 17.4 %collective-permute-start.19 = (f32[256,384]{1,0:T(8,128)}, f32[256,384]{1,0:T(8,128)S(1)}, u32[]{:S(2)}, u32[]{:S(2)}) collective-permute-start(f32[256,384]{1,0:T(8,128)} %collective-permute-done.14.refs_6_), channel_id=1, source_target_pairs={{4,0},{5,1},{8,4},{9,5},{12,8},{13,9},{14,12},{15,13},{10,14},{11,... | collective-permute-start | bytes 1179656 | tf_op jit(solution)/shard_map/ppermute | solution.py:422
  89.2 15.7 %collective-permute-start.21 = (f32[576,128]{1,0:T(8,128)S(1)}, f32[576,128]{1,0:T(8,128)S(1)}, u32[]{:S(2)}, u32[]{:S(2)}) collective-permute-start(f32[576,128]{1,0:T(8,128)S(1)} %dynamic-slice_bitcast_fusion.1), channel_id=1, source_target_pairs={{0,2},{1,3},{2,0},{3,1},{4,6},{5,7},{6,4},{7,5},{8,10},{9,11},{10,... | collective-permute-start | bytes 884744 | tf_op jit(solution)/shard_map/ppermute | solution.py:422
  105.6 10.9 %collective-permute-start.23 = (f32[256,384]{1,0:T(8,128)}, f32[256,384]{1,0:T(8,128)S(1)}, u32[]{:S(2)}, u32[]{:S(2)}) collective-permute-start(f32[256,384]{1,0:T(8,128)} %collective-permute-done.18.refs_7_), channel_id=1, source_target_pairs={{0,4},{1,5},{4,8},{5,9},{8,12},{9,13},{12,14},{13,15},{14,10},{15,... | collective-permute-start | bytes 1179656 | tf_op jit(solution)/shard_map/ppermute | solution.py:422
  105.6 24.0 %collective-permute-start.22 = (f32[256,384]{1,0:T(8,128)}, f32[256,384]{1,0:T(8,128)S(1)}, u32[]{:S(2)}, u32[]{:S(2)}) collective-permute-start(f32[256,384]{1,0:T(8,128)} %copy-done.21), channel_id=1, source_target_pairs={{4,0},{5,1},{8,4},{9,5},{12,8},{13,9},{14,12},{15,13},{10,14},{11,... | collective-permute-start | bytes 1179656 | tf_op jit(solution)/shard_map/ppermute | solution.py:422
  107.7 13.7 %collective-permute-start.26 = (f32[144,128]{1,0:T(8,128)S(1)}, f32[144,128]{1,0:T(8,128)S(1)}, u32[]{:S(2)}, u32[]{:S(2)}) collective-permute-start(f32[144,128]{1,0:T(8,128)S(1)} %get-tuple-element.106), channel_id=1, source_target_pairs={{0,4},{1,5},{2,6},{3,7},{4,0},{5,1},{6,2},{7,3},{8,12},{9,13},{10,... | collective-permute-start | bytes 221192 | tf_op jit(solution)/shard_map/ppermute | solution.py:422
  107.8 13.6 %collective-permute-start.27 = (f32[144,128]{1,0:T(8,128)S(1)}, f32[144,128]{1,0:T(8,128)S(1)}, u32[]{:S(2)}, u32[]{:S(2)}) collective-permute-start(f32[144,128]{1,0:T(8,128)S(1)} %get-tuple-element.105), channel_id=1, source_target_pairs={{0,8},{1,9},{2,10},{3,11},{4,12},{5,13},{6,14},{7,15},{8,0},{9,1},... | collective-permute-start | bytes 221192 | tf_op jit(solution)/shard_map/ppermute | solution.py:422
  111.3 12.0 %collective-permute-start.28 = (f32[144,128]{1,0:T(8,128)S(1)}, f32[144,128]{1,0:T(8,128)S(1)}, u32[]{:S(2)}, u32[]{:S(2)}) collective-permute-start(f32[144,128]{1,0:T(8,128)S(1)} %get-tuple-element.104), channel_id=1, source_target_pairs={{0,12},{1,13},{2,14},{3,15},{4,8},{5,9},{6,10},{7,11},{8,4},{9,5},... | collective-permute-start | bytes 221192 | tf_op jit(solution)/shard_map/ppermute | solution.py:422
  123.4 7.8 %collective-permute-start.31 = (f32[144,128]{1,0:T(8,128)S(1)}, f32[144,128]{1,0:T(8,128)S(1)}, u32[]{:S(2)}, u32[]{:S(2)}) collective-permute-start(f32[144,128]{1,0:T(8,128)S(1)} %fusion.3), channel_id=1, source_target_pairs={{0,4},{1,5},{2,6},{3,7},{4,0},{5,1},{6,2},{7,3},{8,12},{9,13},{10,... | collective-permute-start | bytes 221192 | tf_op jit(solution)/shard_map/ppermute | solution.py:422
  133.9 10.7 %collective-permute-start.34 = (f32[576,128]{1,0:T(8,128)S(1)}, f32[576,128]{1,0:T(8,128)S(1)}, u32[]{:S(2)}, u32[]{:S(2)}) collective-permute-start(f32[576,128]{1,0:T(8,128)S(1)} %pad_maximum_fusion.1), channel_id=1, source_target_pairs={{0,2},{1,3},{2,0},{3,1},{4,6},{5,7},{6,4},{7,5},{8,10},{9,11},{10,... | collective-permute-start | bytes 884744 | tf_op jit(solution)/shard_map/ppermute | solution.py:422
  150.1 10.2 %collective-permute-start.37 = (f32[192,128]{1,0:T(8,128)S(1)}, f32[192,128]{1,0:T(8,128)S(1)}, u32[]{:S(2)}, u32[]{:S(2)}) collective-permute-start(f32[192,128]{1,0:T(8,128)S(1)} %add.98), channel_id=1, source_target_pairs={{0,4},{1,5},{2,6},{3,7},{4,0},{5,1},{6,2},{7,3},{8,12},{9,13},{10,... | collective-permute-start | bytes 294920 | tf_op jit(solution)/shard_map/ppermute | solution.py:422
  151.4 9.9 %collective-permute-start.38 = (f32[192,128]{1,0:T(8,128)S(1)}, f32[192,128]{1,0:T(8,128)S(1)}, u32[]{:S(2)}, u32[]{:S(2)}) collective-permute-start(f32[192,128]{1,0:T(8,128)S(1)} %add.98), channel_id=1, source_target_pairs={{0,8},{1,9},{2,10},{3,11},{4,12},{5,13},{6,14},{7,15},{8,0},{9,1},... | collective-permute-start | bytes 294920 | tf_op jit(solution)/shard_map/ppermute | solution.py:422
  152.5 8.9 %collective-permute-start.39 = (f32[192,128]{1,0:T(8,128)S(1)}, f32[192,128]{1,0:T(8,128)S(1)}, u32[]{:S(2)}, u32[]{:S(2)}) collective-permute-start(f32[192,128]{1,0:T(8,128)S(1)} %add.98), channel_id=1, source_target_pairs={{0,12},{1,13},{2,14},{3,15},{4,8},{5,9},{6,10},{7,11},{8,4},{9,5},... | collective-permute-start | bytes 294920 | tf_op jit(solution)/shard_map/ppermute | solution.py:422
  (37 other events, 252.9 us)

commit v3 on v2

--- a/solution.py
+++ b/solution.py
@@ -223,16 +223,19 @@
             image = halves_of(jnp.concatenate([out[...] for out in outs], axis=1))
             side = halves_of(jnp.concatenate([ref[...] for ref in factors], axis=0))
             spot = 0
-            for top, first in rows_at:
+            for start in range(0, len(rows_at), 2):
+                group = rows_at[start : start + 2]
+                top, last = group[0][0], group[-1][1] + tile
                 value = product_of(
-                    tuple(half[top : top + tile] for half in image),
-                    tuple(half[:, : first + tile] for half in side),
+                    tuple(half[top : top + len(group) * tile] for half in image),
+                    tuple(half[:, :last] for half in side),
                 )
-                for i in range(first // tile + 1):
-                    inner_ref[spot * tile : (spot + 1) * tile, :] = value[
-                        :, i * tile : (i + 1) * tile
-                    ]
-                    spot += 1
+                for place, (_, first) in enumerate(group):
+                    for i in range(first // tile + 1):
+                        inner_ref[spot * tile : (spot + 1) * tile, :] = value[
+                            place * tile : (place + 1) * tile, i * tile : (i + 1) * tile
+                        ]
+                        spot += 1
 
 
 def multiply(index, inverse, twin, first, blocks, start=None, rows_at=(), factors=()):
@@ -268,7 +271,8 @@
             num_scalar_prefetch=1,
             grid=(len(blocks) // 2,),
             in_specs=[source(0), source(0), source(1), source(1)]
-            + [whole(v.shape) for v in operands],
+            + [whole(v.shape) for v in flat + list(start or ())]
+            + [whole((rows, rows_at[-1][1] + tile)) for _ in factors],
             out_specs=[whole(v.shape) for v in out_shape],
             scratch_shapes=[pltpu.VMEM((height, 2 * rows), jnp.float32)],
         ),

time: 166 us -> 165 us (level)
  transfers between devices with their start and end apart: 42 -> 42, of which waited for: 18 -> 18; matrix products, arithmetic and copies ran while one was open for 1% -> 1% of each run, Pallas kernels for 31% -> 30%
where the time goes in v3:
time: 165 us; the launch traced here: 164 us
  waiting for transfers between devices  62.8 us (38%)
  Pallas kernels  52.5 us (32%)
  starting transfers between devices  40.7 us (25%)
  local copies, waits for them, and re-layouts  7.05 us (4%)
    ppermute x42, waiting for transfers between devices, send(): return lax.ppermute(value, 'pcol', pairs)  62.8 us
    ppermute x42, starting transfers between devices, send(): return lax.ppermute(value, 'pcol', pairs)  40.7 us
    pallas_call x6, Pallas kernels, multiply(): pl.pallas_call(functools.partial(multiply_kernel, tuple(layout), start is...  37.2 us
    pallas_call x1, Pallas kernels, window_blocks_of(): pl.pallas_call(functools.partial(window_kernel, width, steps, tops), in_s...  5.67 us
    pallas_call x1, Pallas kernels, solve_columns(): pl.pallas_call(functools.partial(columns_kernel, width, steps), out_shape...  4.3 us
    unnamed x54, local copies, waits for them, and re-layouts  3.94 us
  transfers between devices with their start and end apart: 42, of which 18 were waited for; matrix products, arithmetic and copies ran while one was open for 1% of the time, Pallas kernels for 30%

profile of v3, /device:TPU:0, one launch (start us, length us, event | category | flops | bytes accessed | tf_op | source)
XLA Modules:
  0.0 164.3 jit_solution(1484509069483925874)
XLA Ops:
  1.1 2.9 %shard_map.68 = (f32[384,768]{1,0:T(8,128)}, f32[256,384]{1,0:T(8,128)}, f32[256,384]{1,0:T(8,128)}, f32[256,384]{1,0:T(8,128)}) custom-call(s32[1]{0:T(128)} %bitcast.index_ref.core_ref, s32[3,24]{1,0:T(4,128)} %structure_ref.1, f32[384,768]{1,0:T(8,128)} %factor_ref.2), custom_call_target="tpu_custom_call" | custom-call | flops 1 | bytes 1 | tf_op jit(solution)/shard_map/pallas_call | solution.py:170
  4.0 2.6 %collective-permute-start.1 = (f32[256,384]{1,0:T(8,128)}, f32[256,384]{1,0:T(8,128)S(1)}, u32[]{:S(2)}, u32[]{:S(2)}) collective-permute-start(f32[256,384]{1,0:T(8,128)} %get-tuple-element.52.refs_4_), channel_id=1, source_target_pairs={{0,4},{1,5},{4,8},{5,9},{8,12},{9,13},{12,14},{13,15},{14,10},{15,... | collective-permute-start | bytes 1179656 | tf_op jit(solution)/shard_map/ppermute | solution.py:426
  6.6 2.0 %collective-permute-start.4 = (f32[256,384]{1,0:T(8,128)}, f32[256,384]{1,0:T(8,128)S(1)}, u32[]{:S(2)}, u32[]{:S(2)}) collective-permute-start(f32[256,384]{1,0:T(8,128)} %get-tuple-element.53.refs_5_), channel_id=1, source_target_pairs={{0,4},{1,5},{4,8},{5,9},{8,12},{9,13},{12,14},{13,15},{14,10},{15,... | collective-permute-start | bytes 1179656 | tf_op jit(solution)/shard_map/ppermute | solution.py:426
  8.6 8.1 %collective-permute-done.1.refs_6_ = f32[256,384]{1,0:T(8,128)S(1)} collective-permute-done((f32[256,384]{1,0:T(8,128)}, f32[256,384]{1,0:T(8,128)S(1)}, u32[]{:S(2)}, u32[]{:S(2)}) %collective-permute-start.1) | collective-permute-done | bytes 393248 | tf_op jit(solution)/shard_map/ppermute | solution.py:426
  16.7 2.0 %collective-permute-start.2 = (f32[256,384]{1,0:T(8,128)S(1)}, f32[256,384]{1,0:T(8,128)}, u32[]{:S(2)}, u32[]{:S(2)}) collective-permute-start(f32[256,384]{1,0:T(8,128)S(1)} %collective-permute-done.1.refs_6_), channel_id=1, source_target_pairs={{0,4},{1,5},{4,8},{5,9},{8,12},{9,13},{12,14},{13,15},{14,10},{15,... | collective-permute-start | bytes 1179656 | tf_op jit(solution)/shard_map/ppermute | solution.py:426
  18.8 6.3 %collective-permute-done.4.refs_7_ = f32[256,384]{1,0:T(8,128)S(1)} collective-permute-done((f32[256,384]{1,0:T(8,128)}, f32[256,384]{1,0:T(8,128)S(1)}, u32[]{:S(2)}, u32[]{:S(2)}) %collective-permute-start.4) | collective-permute-done | bytes 393248 | tf_op jit(solution)/shard_map/ppermute | solution.py:426
  25.1 2.0 %collective-permute-start.5 = (f32[256,384]{1,0:T(8,128)S(1)}, f32[256,384]{1,0:T(8,128)}, u32[]{:S(2)}, u32[]{:S(2)}) collective-permute-start(f32[256,384]{1,0:T(8,128)S(1)} %collective-permute-done.4.refs_7_), channel_id=1, source_target_pairs={{0,4},{1,5},{4,8},{5,9},{8,12},{9,13},{12,14},{13,15},{14,10},{15,... | collective-permute-start | bytes 1179656 | tf_op jit(solution)/shard_map/ppermute | solution.py:426
  27.2 6.5 %collective-permute-done.2.refs_10_ = f32[256,384]{1,0:T(8,128)} collective-permute-done((f32[256,384]{1,0:T(8,128)S(1)}, f32[256,384]{1,0:T(8,128)}, u32[]{:S(2)}, u32[]{:S(2)}) %collective-permute-start.2) | collective-permute-done | bytes 393248 | tf_op jit(solution)/shard_map/ppermute | solution.py:426
  33.7 2.0 %collective-permute-done.11.refs_5_ = f32[256,384]{1,0:T(8,128)S(1)} collective-permute-done((f32[256,384]{1,0:T(8,128)S(1)}, f32[256,384]{1,0:T(8,128)S(1)}, u32[]{:S(2)}, u32[]{:S(2)}) %collective-permute-start.11) | collective-permute-done | bytes 393248 | tf_op jit(solution)/shard_map/ppermute | solution.py:426
  35.7 6.2 %collective-permute-done.5.refs_11_ = f32[256,384]{1,0:T(8,128)} collective-permute-done((f32[256,384]{1,0:T(8,128)S(1)}, f32[256,384]{1,0:T(8,128)}, u32[]{:S(2)}, u32[]{:S(2)}) %collective-permute-start.5) | collective-permute-done | bytes 393248 | tf_op jit(solution)/shard_map/ppermute | solution.py:426
  41.9 1.8 %collective-permute-start.3 = (f32[256,384]{1,0:T(8,128)}, f32[256,384]{1,0:T(8,128)S(1)}, u32[]{:S(2)}, u32[]{:S(2)}) collective-permute-start(f32[256,384]{1,0:T(8,128)} %collective-permute-done.2.refs_10_), channel_id=1, source_target_pairs={{0,4},{1,5},{4,8},{5,9},{8,12},{9,13},{12,14},{13,15},{14,10},{15,... | collective-permute-start | bytes 1179656 | tf_op jit(solution)/shard_map/ppermute | solution.py:426
  46.1 8.4 %shard_map.69 = (f32[512,384]{1,0:T(8,128)}, f32[512,384]{1,0:T(8,128)}) custom-call(s32[1]{0:T(128)} %bitcast.index_ref.core_ref, f32[6144,384]{1,0:T(8,128)} %refs_2_.12, f32[6144,384]{1,0:T(8,128)} %collective-permute-done.refs_1_.refs_3_, f32[6144,384]{1,0:T(8,128)} %refs_2_.12, f32[6144,384]{1,0:T(8,128)} %collective-permute-done.refs_1_.refs_3_, ...), custom_call_target="tpu_custom_call" | custom-call | flops 1 | bytes 1 | tf_op jit(solution)/shard_map/pallas_call | solution.py:268
  54.6 6.9 %collective-permute-done.6.refs_7_ = f32[256,384]{1,0:T(8,128)S(1)} collective-permute-done((f32[256,384]{1,0:T(8,128)}, f32[256,384]{1,0:T(8,128)S(1)}, u32[]{:S(2)}, u32[]{:S(2)}) %collective-permute-start.6) | collective-permute-done | bytes 393248 | tf_op jit(solution)/shard_map/ppermute | solution.py:426
  63.5 1.6 collective-permute-start.13
  65.6 5.8 %shard_map.70 = (f32[512,384]{1,0:T(8,128)}, f32[512,384]{1,0:T(8,128)}) custom-call(s32[1]{0:T(128)} %bitcast.index_ref.core_ref, f32[6144,384]{1,0:T(8,128)} %refs_2_.12, f32[6144,384]{1,0:T(8,128)} %collective-permute-done.refs_1_.refs_3_, f32[6144,384]{1,0:T(8,128)} %refs_2_.12, f32[6144,384]{1,0:T(8,128)} %collective-permute-done.refs_1_.refs_3_, ...), custom_call_target="tpu_custom_call" | custom-call | flops 1 | bytes 1 | tf_op jit(solution)/shard_map/pallas_call | solution.py:268
  71.3 2.2 %collective-permute-done.16.refs_7_ = f32[256,384]{1,0:T(8,128)S(1)} collective-permute-done((f32[256,384]{1,0:T(8,128)S(1)}, f32[256,384]{1,0:T(8,128)S(1)}, u32[]{:S(2)}, u32[]{:S(2)}) %collective-permute-start.16) | collective-permute-done | bytes 393248 | tf_op jit(solution)/shard_map/ppermute | solution.py:426
  75.9 8.4 %shard_map.71 = (f32[512,384]{1,0:T(8,128)}, f32[512,384]{1,0:T(8,128)}, f32[2304,128]{1,0:T(8,128)}) custom-call(s32[1]{0:T(128)} %bitcast.index_ref.core_ref, f32[6144,384]{1,0:T(8,128)} %refs_2_.12, f32[6144,384]{1,0:T(8,128)} %collective-permute-done.refs_1_.refs_3_, f32[6144,384]{1,0:T(8,128)} %refs_2_.12, ...), custom_call_target="tpu_custom_call" | custom-call | flops 1 | bytes 1 | tf_op jit(solution)/shard_map/pallas_call | solution.py:268
  88.2 1.6 collective-permute-start.21
  89.8 8.5 %collective-permute-done.18.refs_7_ = f32[256,384]{1,0:T(8,128)} collective-permute-done((f32[256,384]{1,0:T(8,128)}, f32[256,384]{1,0:T(8,128)}, u32[]{:S(2)}, u32[]{:S(2)}) %collective-permute-start.18) | collective-permute-done | bytes 393248 | tf_op jit(solution)/shard_map/ppermute | solution.py:426
  98.3 5.6 %shard_map.72 = (f32[256,384]{1,0:T(8,128)}, f32[256,384]{1,0:T(8,128)}) custom-call(s32[1]{0:T(128)} %bitcast.index_ref.core_ref, f32[6144,384]{1,0:T(8,128)} %refs_2_.12, f32[6144,384]{1,0:T(8,128)} %collective-permute-done.refs_1_.refs_3_, f32[6144,384]{1,0:T(8,128)} %refs_2_.12, f32[6144,384]{1,0:T(8,128)} %collective-permute-done.refs_1_.refs_3_, ...), custom_call_target="tpu_custom_call" | custom-call | flops 1 | bytes 1 | tf_op jit(solution)/shard_map/pallas_call | solution.py:268
  104.7 2.0 %collective-permute-start.22 = (f32[256,384]{1,0:T(8,128)}, f32[256,384]{1,0:T(8,128)S(1)}, u32[]{:S(2)}, u32[]{:S(2)}) collective-permute-start(f32[256,384]{1,0:T(8,128)} %copy-done.21), channel_id=1, source_target_pairs={{4,0},{5,1},{8,4},{9,5},{12,8},{13,9},{14,12},{15,13},{10,14},{11,... | collective-permute-start | bytes 1179656 | tf_op jit(solution)/shard_map/ppermute | solution.py:426
  106.8 3.5 %collective-permute-start.27 = (f32[144,128]{1,0:T(8,128)S(1)}, f32[144,128]{1,0:T(8,128)S(1)}, u32[]{:S(2)}, u32[]{:S(2)}) collective-permute-start(f32[144,128]{1,0:T(8,128)S(1)} %get-tuple-element.105), channel_id=1, source_target_pairs={{0,8},{1,9},{2,10},{3,11},{4,12},{5,13},{6,14},{7,15},{8,0},{9,1},... | collective-permute-start | bytes 221192 | tf_op jit(solution)/shard_map/ppermute | solution.py:426
  111.3 4.3 %shard_map.74.columns_ref = f32[384,768]{1,0:T(8,128)} custom-call(f32[512,384]{1,0:T(8,128)} %get-tuple-element.81.image_ref, f32[512,384]{1,0:T(8,128)} %copy-done.5, f32[768,768]{1,0:T(8,128)} %refs_2_.13), custom_call_target="tpu_custom_call" | custom-call | flops 1 | bytes 1 | tf_op jit(solution)/shard_map/pallas_call | solution.py:302
  116.3 4.1 %shard_map.73 = (f32[256,384]{1,0:T(8,128)}, f32[256,384]{1,0:T(8,128)}) custom-call(s32[1]{0:T(128)} %bitcast.index_ref.core_ref, f32[6144,384]{1,0:T(8,128)} %refs_2_.12, f32[6144,384]{1,0:T(8,128)} %collective-permute-done.refs_1_.refs_3_, f32[6144,384]{1,0:T(8,128)} %refs_2_.12, f32[6144,384]{1,0:T(8,128)} %collective-permute-done.refs_1_.refs_3_, ...), custom_call_target="tpu_custom_call" | custom-call | flops 1 | bytes 1 | tf_op jit(solution)/shard_map/pallas_call | solution.py:268
  120.5 1.9 %collective-permute-done.28 = f32[144,128]{1,0:T(8,128)S(1)} collective-permute-done((f32[144,128]{1,0:T(8,128)S(1)}, f32[144,128]{1,0:T(8,128)S(1)}, u32[]{:S(2)}, u32[]{:S(2)}) %collective-permute-start.28) | collective-permute-done | bytes 73760 | tf_op jit(solution)/shard_map/ppermute | solution.py:426
  123.3 2.5 %collective-permute-start.32 = (f32[144,128]{1,0:T(8,128)S(1)}, f32[144,128]{1,0:T(8,128)S(1)}, u32[]{:S(2)}, u32[]{:S(2)}) collective-permute-start(f32[144,128]{1,0:T(8,128)S(1)} %fusion.3), channel_id=1, source_target_pairs={{0,8},{1,9},{2,10},{3,11},{4,12},{5,13},{6,14},{7,15},{8,0},{9,1},... | collective-permute-start | bytes 221192 | tf_op jit(solution)/shard_map/ppermute | solution.py:426
  130.2 2.6 %collective-permute-done.33 = f32[144,128]{1,0:T(8,128)S(1)} collective-permute-done((f32[144,128]{1,0:T(8,128)S(1)}, f32[144,128]{1,0:T(8,128)S(1)}, u32[]{:S(2)}, u32[]{:S(2)}) %collective-permute-start.33) | collective-permute-done | bytes 73760 | tf_op jit(solution)/shard_map/ppermute | solution.py:426
  135.9 5.0 %shard_map.75 = (f32[256,384]{1,0:T(8,128)}, f32[256,384]{1,0:T(8,128)}, f32[384,128]{1,0:T(8,128)}) custom-call(s32[1]{0:T(128)} %bitcast.index_ref.core_ref, f32[6144,384]{1,0:T(8,128)} %refs_2_.12, f32[6144,384]{1,0:T(8,128)} %collective-permute-done.refs_1_.refs_3_, f32[6144,384]{1,0:T(8,128)} %refs_2_.12, ...), custom_call_target="tpu_custom_call" | custom-call | flops 1 | bytes 1 | tf_op jit(solution)/shard_map/pallas_call | solution.py:268
  144.5 4.1 %collective-permute-done.35 = f32[192,128]{1,0:T(8,128)S(1)} collective-permute-done((f32[192,128]{1,0:T(8,128)S(1)}, f32[192,128]{1,0:T(8,128)S(1)}, u32[]{:S(2)}, u32[]{:S(2)}) %collective-permute-start.35) | collective-permute-done | bytes 98336 | tf_op jit(solution)/shard_map/ppermute | solution.py:426
  150.9 2.1 %collective-permute-start.39 = (f32[192,128]{1,0:T(8,128)S(1)}, f32[192,128]{1,0:T(8,128)S(1)}, u32[]{:S(2)}, u32[]{:S(2)}) collective-permute-start(f32[192,128]{1,0:T(8,128)S(1)} %add.98), channel_id=1, source_target_pairs={{0,12},{1,13},{2,14},{3,15},{4,8},{5,9},{6,10},{7,11},{8,4},{9,5},... | collective-permute-start | bytes 294920 | tf_op jit(solution)/shard_map/ppermute | solution.py:426
  153.0 5.7 %shard_map.76.base_ref = f32[768,768]{1,0:T(8,128)} custom-call(s32[1]{0:T(128)} %bitcast.index_ref.core_ref, f32[1152,128]{1,0:T(8,128)} %copy-done.1, f32[1152,128]{1,0:T(8,128)} %copy-done.6, f32[768,768]{1,0:T(8,128)} %refs_2_.13, f32[3,256,256]{2,1,0:T(8,128)} %refs_3_.1), custom_call_target="tpu_custom_call" | custom-call | flops 1 | bytes 1 | tf_op jit(solution)/shard_map/pallas_call | solution.py:393
  161.9 2.4 %shard_map.77 = (f32[384,768]{1,0:T(8,128)}, f32[768,768]{1,0:T(8,128)}) custom-call(s32[1]{0:T(128)} %bitcast.index_ref.core_ref, f32[192,128]{1,0:T(8,128)} %copy-done.20, f32[192,128]{1,0:T(8,128)} %copy-done.25, f32[256,384]{1,0:T(8,128)} %get-tuple-element.96.image_ref, f32[256,384]{1,0:T(8,128)} %copy-done.19, ...), custom_call_target="tpu_custom_call", output_to_operand_aliasing={{0}: (5, {}), {1}: (6, {})} | custom-call | flops 1 | bytes 1 | tf_op jit(solution)/shard_map/pallas_call | solution.py:340
  (134 shorter events, 31.8 us)
Async XLA Ops:
  0.6 45.0 %collective-permute-start = (f32[6144,384]{1,0:T(8,128)}, f32[6144,384]{1,0:T(8,128)}, u32[]{:S(2)}, u32[]{:S(2)}) collective-permute-start(f32[6144,384]{1,0:T(8,128)} %refs_2_.12), channel_id=1, source_target_pairs={{0,1},{1,0},{2,3},{3,2},{4,5},{5,4},{6,7},{7,6},{8,9},{9,8},{10,11... | collective-permute-start | bytes 28311560 | tf_op jit(solution)/shard_map/ppermute | solution.py:426
  4.0 12.7 %collective-permute-start.1 = (f32[256,384]{1,0:T(8,128)}, f32[256,384]{1,0:T(8,128)S(1)}, u32[]{:S(2)}, u32[]{:S(2)}) collective-permute-start(f32[256,384]{1,0:T(8,128)} %get-tuple-element.52.refs_4_), channel_id=1, source_target_pairs={{0,4},{1,5},{4,8},{5,9},{8,12},{9,13},{12,14},{13,15},{14,10},{15,... | collective-permute-start | bytes 1179656 | tf_op jit(solution)/shard_map/ppermute | solution.py:426
  6.6 12.2 %collective-permute-start.10 = (f32[256,384]{1,0:T(8,128)}, f32[256,384]{1,0:T(8,128)S(1)}, u32[]{:S(2)}, u32[]{:S(2)}) collective-permute-start(f32[256,384]{1,0:T(8,128)} %get-tuple-element.53.refs_5_), channel_id=1, source_target_pairs={{4,0},{5,1},{8,4},{9,5},{12,8},{13,9},{14,12},{15,13},{10,14},{11,... | collective-permute-start | bytes 1179656 | tf_op jit(solution)/shard_map/ppermute | solution.py:426
  6.6 18.5 %collective-permute-start.4 = (f32[256,384]{1,0:T(8,128)}, f32[256,384]{1,0:T(8,128)S(1)}, u32[]{:S(2)}, u32[]{:S(2)}) collective-permute-start(f32[256,384]{1,0:T(8,128)} %get-tuple-element.53.refs_5_), channel_id=1, source_target_pairs={{0,4},{1,5},{4,8},{5,9},{8,12},{9,13},{12,14},{13,15},{14,10},{15,... | collective-permute-start | bytes 1179656 | tf_op jit(solution)/shard_map/ppermute | solution.py:426
  8.6 18.6 %collective-permute-start.7 = (f32[256,384]{1,0:T(8,128)}, f32[256,384]{1,0:T(8,128)S(1)}, u32[]{:S(2)}, u32[]{:S(2)}) collective-permute-start(f32[256,384]{1,0:T(8,128)} %get-tuple-element.52.refs_4_), channel_id=1, source_target_pairs={{4,0},{5,1},{8,4},{9,5},{12,8},{13,9},{14,12},{15,13},{10,14},{11,... | collective-permute-start | bytes 1179656 | tf_op jit(solution)/shard_map/ppermute | solution.py:426
  16.7 17.0 %collective-permute-start.2 = (f32[256,384]{1,0:T(8,128)S(1)}, f32[256,384]{1,0:T(8,128)}, u32[]{:S(2)}, u32[]{:S(2)}) collective-permute-start(f32[256,384]{1,0:T(8,128)S(1)} %collective-permute-done.1.refs_6_), channel_id=1, source_target_pairs={{0,4},{1,5},{4,8},{5,9},{8,12},{9,13},{12,14},{13,15},{14,10},{15,... | collective-permute-start | bytes 1179656 | tf_op jit(solution)/shard_map/ppermute | solution.py:426
  18.8 16.9 %collective-permute-start.11 = (f32[256,384]{1,0:T(8,128)S(1)}, f32[256,384]{1,0:T(8,128)S(1)}, u32[]{:S(2)}, u32[]{:S(2)}) collective-permute-start(f32[256,384]{1,0:T(8,128)S(1)} %collective-permute-done.10.refs_9_), channel_id=1, source_target_pairs={{4,0},{5,1},{8,4},{9,5},{12,8},{13,9},{14,12},{15,13},{10,14},{11,... | collective-permute-start | bytes 1179656 | tf_op jit(solution)/shard_map/ppermute | solution.py:426
  25.1 16.8 %collective-permute-start.5 = (f32[256,384]{1,0:T(8,128)S(1)}, f32[256,384]{1,0:T(8,128)}, u32[]{:S(2)}, u32[]{:S(2)}) collective-permute-start(f32[256,384]{1,0:T(8,128)S(1)} %collective-permute-done.4.refs_7_), channel_id=1, source_target_pairs={{0,4},{1,5},{4,8},{5,9},{8,12},{9,13},{12,14},{13,15},{14,10},{15,... | collective-permute-start | bytes 1179656 | tf_op jit(solution)/shard_map/ppermute | solution.py:426
  27.2 16.9 %collective-permute-start.8 = (f32[256,384]{1,0:T(8,128)S(1)}, f32[256,384]{1,0:T(8,128)S(1)}, u32[]{:S(2)}, u32[]{:S(2)}) collective-permute-start(f32[256,384]{1,0:T(8,128)S(1)} %collective-permute-done.7.refs_8_), channel_id=1, source_target_pairs={{4,0},{5,1},{8,4},{9,5},{12,8},{13,9},{14,12},{15,13},{10,14},{11,... | collective-permute-start | bytes 1179656 | tf_op jit(solution)/shard_map/ppermute | solution.py:426
  33.7 37.7 %collective-permute-start.17 = (f32[384,768]{1,0:T(8,128)}, f32[384,768]{1,0:T(8,128)S(1)}, u32[]{:S(2)}, u32[]{:S(2)}) collective-permute-start(f32[384,768]{1,0:T(8,128)} %get-tuple-element.67.refs_10_.refs_9_), channel_id=1, source_target_pairs={{0,1},{1,0},{2,3},{3,2},{4,5},{5,4},{6,7},{7,6},{8,9},{9,8},{10,11... | collective-permute-start | bytes 3538952 | tf_op jit(solution)/shard_map/ppermute | solution.py:426
  35.6 18.9 %collective-permute-start.12 = (f32[256,384]{1,0:T(8,128)S(1)}, f32[256,384]{1,0:T(8,128)S(1)}, u32[]{:S(2)}, u32[]{:S(2)}) collective-permute-start(f32[256,384]{1,0:T(8,128)S(1)} %collective-permute-done.11.refs_5_), channel_id=1, source_target_pairs={{4,0},{5,1},{8,4},{9,5},{12,8},{13,9},{14,12},{15,13},{10,14},{11,... | collective-permute-start | bytes 1179656 | tf_op jit(solution)/shard_map/ppermute | solution.py:426
  41.9 12.7 %collective-permute-start.3 = (f32[256,384]{1,0:T(8,128)}, f32[256,384]{1,0:T(8,128)S(1)}, u32[]{:S(2)}, u32[]{:S(2)}) collective-permute-start(f32[256,384]{1,0:T(8,128)} %collective-permute-done.2.refs_10_), channel_id=1, source_target_pairs={{0,4},{1,5},{4,8},{5,9},{8,12},{9,13},{12,14},{13,15},{14,10},{15,... | collective-permute-start | bytes 1179656 | tf_op jit(solution)/shard_map/ppermute | solution.py:426
  44.1 17.4 %collective-permute-start.6 = (f32[256,384]{1,0:T(8,128)}, f32[256,384]{1,0:T(8,128)S(1)}, u32[]{:S(2)}, u32[]{:S(2)}) collective-permute-start(f32[256,384]{1,0:T(8,128)} %collective-permute-done.5.refs_11_), channel_id=1, source_target_pairs={{0,4},{1,5},{4,8},{5,9},{8,12},{9,13},{12,14},{13,15},{14,10},{15,... | collective-permute-start | bytes 1179656 | tf_op jit(solution)/shard_map/ppermute | solution.py:426
  45.6 15.8 %collective-permute-start.9 = (f32[256,384]{1,0:T(8,128)S(1)}, f32[256,384]{1,0:T(8,128)S(1)}, u32[]{:S(2)}, u32[]{:S(2)}) collective-permute-start(f32[256,384]{1,0:T(8,128)S(1)} %collective-permute-done.8.refs_4_), channel_id=1, source_target_pairs={{4,0},{5,1},{8,4},{9,5},{12,8},{13,9},{14,12},{15,13},{10,14},{11,... | collective-permute-start | bytes 1179656 | tf_op jit(solution)/shard_map/ppermute | solution.py:426
  61.5 12.1 %collective-permute-start.16 = (f32[256,384]{1,0:T(8,128)S(1)}, f32[256,384]{1,0:T(8,128)S(1)}, u32[]{:S(2)}, u32[]{:S(2)}) collective-permute-start(f32[256,384]{1,0:T(8,128)S(1)} %collective-permute-done.12.refs_5_), channel_id=1, source_target_pairs={{4,0},{5,1},{8,4},{9,5},{12,8},{13,9},{14,12},{15,13},{10,14},{11,... | collective-permute-start | bytes 1179656 | tf_op jit(solution)/shard_map/ppermute | solution.py:426
  63.0 12.1 %collective-permute-start.15 = (f32[256,384]{1,0:T(8,128)S(1)}, f32[256,384]{1,0:T(8,128)S(1)}, u32[]{:S(2)}, u32[]{:S(2)}) collective-permute-start(f32[256,384]{1,0:T(8,128)S(1)} %collective-permute-done.3.refs_6_), channel_id=1, source_target_pairs={{0,4},{1,5},{4,8},{5,9},{8,12},{9,13},{12,14},{13,15},{14,10},{15,... | collective-permute-start | bytes 1179656 | tf_op jit(solution)/shard_map/ppermute | solution.py:426
  63.5 20.7 %collective-permute-start.13 = (f32[256,384]{1,0:T(8,128)}, f32[256,384]{1,0:T(8,128)}, u32[]{:S(2)}, u32[]{:S(2)}) collective-permute-start(f32[256,384]{1,0:T(8,128)} %get-tuple-element.58.refs_4_), channel_id=1, source_target_pairs={{0,4},{1,5},{4,8},{5,9},{8,12},{9,13},{12,14},{13,15},{14,10},{15,... | collective-permute-start | bytes 1179656 | tf_op jit(solution)/shard_map/ppermute | solution.py:426
  65.2 19.1 %collective-permute-start.14 = (f32[256,384]{1,0:T(8,128)}, f32[256,384]{1,0:T(8,128)}, u32[]{:S(2)}, u32[]{:S(2)}) collective-permute-start(f32[256,384]{1,0:T(8,128)} %get-tuple-element.58.refs_4_), channel_id=1, source_target_pairs={{4,0},{5,1},{8,4},{9,5},{12,8},{13,9},{14,12},{15,13},{10,14},{11,... | collective-permute-start | bytes 1179656 | tf_op jit(solution)/shard_map/ppermute | solution.py:426
  85.6 24.7 %collective-permute-start.29 = (f32[512,384]{1,0:T(8,128)}, f32[512,384]{1,0:T(8,128)S(1)}, u32[]{:S(2)}, u32[]{:S(2)}) collective-permute-start(f32[512,384]{1,0:T(8,128)} %get-tuple-element.82), channel_id=1, source_target_pairs={{0,1},{1,0},{2,3},{3,2},{4,5},{5,4},{6,7},{7,6},{8,9},{9,8},{10,11... | collective-permute-start | bytes 2359304 | tf_op jit(solution)/shard_map/ppermute | solution.py:426
  86.1 12.3 %collective-permute-start.18 = (f32[256,384]{1,0:T(8,128)}, f32[256,384]{1,0:T(8,128)}, u32[]{:S(2)}, u32[]{:S(2)}) collective-permute-start(f32[256,384]{1,0:T(8,128)} %collective-permute-done.13.refs_5_), channel_id=1, source_target_pairs={{0,4},{1,5},{4,8},{5,9},{8,12},{9,13},{12,14},{13,15},{14,10},{15,... | collective-permute-start | bytes 1179656 | tf_op jit(solution)/shard_map/ppermute | solution.py:426
  86.6 17.4 %collective-permute-start.19 = (f32[256,384]{1,0:T(8,128)}, f32[256,384]{1,0:T(8,128)S(1)}, u32[]{:S(2)}, u32[]{:S(2)}) collective-permute-start(f32[256,384]{1,0:T(8,128)} %collective-permute-done.14.refs_6_), channel_id=1, source_target_pairs={{4,0},{5,1},{8,4},{9,5},{12,8},{13,9},{14,12},{15,13},{10,14},{11,... | collective-permute-start | bytes 1179656 | tf_op jit(solution)/shard_map/ppermute | solution.py:426
  88.2 15.7 %collective-permute-start.21 = (f32[576,128]{1,0:T(8,128)S(1)}, f32[576,128]{1,0:T(8,128)S(1)}, u32[]{:S(2)}, u32[]{:S(2)}) collective-permute-start(f32[576,128]{1,0:T(8,128)S(1)} %dynamic-slice_bitcast_fusion.1), channel_id=1, source_target_pairs={{0,2},{1,3},{2,0},{3,1},{4,6},{5,7},{6,4},{7,5},{8,10},{9,11},{10,... | collective-permute-start | bytes 884744 | tf_op jit(solution)/shard_map/ppermute | solution.py:426
  104.7 10.9 %collective-permute-start.23 = (f32[256,384]{1,0:T(8,128)}, f32[256,384]{1,0:T(8,128)S(1)}, u32[]{:S(2)}, u32[]{:S(2)}) collective-permute-start(f32[256,384]{1,0:T(8,128)} %collective-permute-done.18.refs_7_), channel_id=1, source_target_pairs={{0,4},{1,5},{4,8},{5,9},{8,12},{9,13},{12,14},{13,15},{14,10},{15,... | collective-permute-start | bytes 1179656 | tf_op jit(solution)/shard_map/ppermute | solution.py:426
  104.7 24.0 %collective-permute-start.22 = (f32[256,384]{1,0:T(8,128)}, f32[256,384]{1,0:T(8,128)S(1)}, u32[]{:S(2)}, u32[]{:S(2)}) collective-permute-start(f32[256,384]{1,0:T(8,128)} %copy-done.21), channel_id=1, source_target_pairs={{4,0},{5,1},{8,4},{9,5},{12,8},{13,9},{14,12},{15,13},{10,14},{11,... | collective-permute-start | bytes 1179656 | tf_op jit(solution)/shard_map/ppermute | solution.py:426
  106.8 13.7 %collective-permute-start.26 = (f32[144,128]{1,0:T(8,128)S(1)}, f32[144,128]{1,0:T(8,128)S(1)}, u32[]{:S(2)}, u32[]{:S(2)}) collective-permute-start(f32[144,128]{1,0:T(8,128)S(1)} %get-tuple-element.106), channel_id=1, source_target_pairs={{0,4},{1,5},{2,6},{3,7},{4,0},{5,1},{6,2},{7,3},{8,12},{9,13},{10,... | collective-permute-start | bytes 221192 | tf_op jit(solution)/shard_map/ppermute | solution.py:426
  106.8 13.6 %collective-permute-start.27 = (f32[144,128]{1,0:T(8,128)S(1)}, f32[144,128]{1,0:T(8,128)S(1)}, u32[]{:S(2)}, u32[]{:S(2)}) collective-permute-start(f32[144,128]{1,0:T(8,128)S(1)} %get-tuple-element.105), channel_id=1, source_target_pairs={{0,8},{1,9},{2,10},{3,11},{4,12},{5,13},{6,14},{7,15},{8,0},{9,1},... | collective-permute-start | bytes 221192 | tf_op jit(solution)/shard_map/ppermute | solution.py:426
  110.3 12.0 %collective-permute-start.28 = (f32[144,128]{1,0:T(8,128)S(1)}, f32[144,128]{1,0:T(8,128)S(1)}, u32[]{:S(2)}, u32[]{:S(2)}) collective-permute-start(f32[144,128]{1,0:T(8,128)S(1)} %get-tuple-element.104), channel_id=1, source_target_pairs={{0,12},{1,13},{2,14},{3,15},{4,8},{5,9},{6,10},{7,11},{8,4},{9,5},... | collective-permute-start | bytes 221192 | tf_op jit(solution)/shard_map/ppermute | solution.py:426
  122.4 7.8 %collective-permute-start.31 = (f32[144,128]{1,0:T(8,128)S(1)}, f32[144,128]{1,0:T(8,128)S(1)}, u32[]{:S(2)}, u32[]{:S(2)}) collective-permute-start(f32[144,128]{1,0:T(8,128)S(1)} %fusion.3), channel_id=1, source_target_pairs={{0,4},{1,5},{2,6},{3,7},{4,0},{5,1},{6,2},{7,3},{8,12},{9,13},{10,... | collective-permute-start | bytes 221192 | tf_op jit(solution)/shard_map/ppermute | solution.py:426
  132.9 10.1 %collective-permute-start.34 = (f32[576,128]{1,0:T(8,128)S(1)}, f32[576,128]{1,0:T(8,128)S(1)}, u32[]{:S(2)}, u32[]{:S(2)}) collective-permute-start(f32[576,128]{1,0:T(8,128)S(1)} %pad_maximum_fusion.1), channel_id=1, source_target_pairs={{0,2},{1,3},{2,0},{3,1},{4,6},{5,7},{6,4},{7,5},{8,10},{9,11},{10,... | collective-permute-start | bytes 884744 | tf_op jit(solution)/shard_map/ppermute | solution.py:426
  148.6 10.2 %collective-permute-start.37 = (f32[192,128]{1,0:T(8,128)S(1)}, f32[192,128]{1,0:T(8,128)S(1)}, u32[]{:S(2)}, u32[]{:S(2)}) collective-permute-start(f32[192,128]{1,0:T(8,128)S(1)} %add.98), channel_id=1, source_target_pairs={{0,4},{1,5},{2,6},{3,7},{4,0},{5,1},{6,2},{7,3},{8,12},{9,13},{10,... | collective-permute-start | bytes 294920 | tf_op jit(solution)/shard_map/ppermute | solution.py:426
  149.9 9.9 %collective-permute-start.38 = (f32[192,128]{1,0:T(8,128)S(1)}, f32[192,128]{1,0:T(8,128)S(1)}, u32[]{:S(2)}, u32[]{:S(2)}) collective-permute-start(f32[192,128]{1,0:T(8,128)S(1)} %add.98), channel_id=1, source_target_pairs={{0,8},{1,9},{2,10},{3,11},{4,12},{5,13},{6,14},{7,15},{8,0},{9,1},... | collective-permute-start | bytes 294920 | tf_op jit(solution)/shard_map/ppermute | solution.py:426
  150.9 8.9 %collective-permute-start.39 = (f32[192,128]{1,0:T(8,128)S(1)}, f32[192,128]{1,0:T(8,128)S(1)}, u32[]{:S(2)}, u32[]{:S(2)}) collective-permute-start(f32[192,128]{1,0:T(8,128)S(1)} %add.98), channel_id=1, source_target_pairs={{0,12},{1,13},{2,14},{3,15},{4,8},{5,9},{6,10},{7,11},{8,4},{9,5},... | collective-permute-start | bytes 294920 | tf_op jit(solution)/shard_map/ppermute | solution.py:426
  (37 other events, 252.9 us)

commit v4 on v3

--- a/solution.py
+++ b/solution.py
@@ -180,6 +180,10 @@
 
 def multiply_kernel(layout, has_start, rows_at, index_ref, *refs):
     refs = list(refs)
+    late = []
+    if rows_at:
+        sem = refs.pop()
+        kept = [refs.pop() for _ in range(4)][::-1]
     sources = [refs.pop(0) for _ in range(4)]
     piece_count = sum(len(block) for block in layout)
     pieces = [refs.pop(0) for _ in range(piece_count)]
@@ -190,6 +194,16 @@
     held = refs.pop(0)
     rows = sources[0].shape[1]
     step = pl.program_id(0)
+    if rows_at:
+        last = rows_at[-1][1] + tile
+        away = starts + [ref.at[:, pl.ds(0, last)] for ref in factors]
+        late = [
+            pltpu.make_async_copy(ref, place, sem.at[i])
+            for i, (ref, place) in enumerate(zip(away, kept))
+        ]
+        for copy in late:
+            copy.start()
+        starts, factors = kept[:2], kept[2:]
     at = 0
     for b, block in enumerate(layout):
         chosen = pieces[at : at + len(block)]
@@ -201,10 +215,12 @@
             for ref, (top, height) in zip(chosen, block):
                 held[top : top + height, left : left + rows] = ref[...]
 
-    @pl.when(step == 0)
-    def _():
-        for i in range(2):
-            outs[i][...] = starts[i][...] if has_start else jnp.zeros_like(outs[i])
+    if not rows_at:
+
+        @pl.when(step == 0)
+        def _():
+            for i in range(2):
+                outs[i][...] = starts[i][...] if has_start else jnp.zeros_like(outs[i])
 
     inverse = jnp.concatenate(
         [
@@ -214,8 +230,13 @@
         axis=0,
     )
     value = product_of(halves_of(held[...]), halves_of(inverse))
+    for copy in late[:2]:
+        copy.wait()
     for i in range(2):
-        outs[i][...] += value[:, i * rows : (i + 1) * rows]
+        before = starts[i] if rows_at else outs[i]
+        outs[i][...] = before[...] + value[:, i * rows : (i + 1) * rows]
+    for copy in late[2:]:
+        copy.wait()
     if rows_at:
 
         @pl.when(step == len(layout) // 2 - 1)
@@ -265,16 +286,22 @@
         count = sum(first // tile + 1 for _, first in rows_at)
         out_shape.append(jax.ShapeDtypeStruct((count * tile, tile), jnp.float32))
     operands = flat + list(start or ()) + list(factors)
+    scratch = []
+    if rows_at:
+        shapes = [(height, rows)] * 2 + [(rows, rows_at[-1][1] + tile)] * 2
+        scratch = [pltpu.VMEM(shape, jnp.float32) for shape in shapes]
+        scratch.append(pltpu.SemaphoreType.DMA((4,)))
     return pl.pallas_call(
         functools.partial(multiply_kernel, tuple(layout), start is not None, rows_at),
         grid_spec=pltpu.PrefetchScalarGridSpec(
             num_scalar_prefetch=1,
             grid=(len(blocks) // 2,),
             in_specs=[source(0), source(0), source(1), source(1)]
-            + [whole(v.shape) for v in flat + list(start or ())]
-            + [whole((rows, rows_at[-1][1] + tile)) for _ in factors],
+            + [whole(v.shape) for v in flat]
+            + [pl.BlockSpec(memory_space=pl.ANY) if rows_at else whole(v.shape) for v in start or ()]
+            + [pl.BlockSpec(memory_space=pl.ANY) for _ in factors],
             out_specs=[whole(v.shape) for v in out_shape],
-            scratch_shapes=[pltpu.VMEM((height, 2 * rows), jnp.float32)],
+            scratch_shapes=[pltpu.VMEM((height, 2 * rows), jnp.float32)] + scratch,
         ),
         out_shape=out_shape,
         compiler_params=pltpu.CompilerParams(vmem_limit_bytes=vmem_bytes),
@@ -575,9 +602,7 @@
         P(),
     )
     out_specs = (P(("pole", "prow", "pcol"), None), P("pole", None))
-    levels = mesh.shape["pcol"] // 4
-    ringed = mesh.shape["prow"] == 1 and mesh.shape["pcol"] % 4 == 0
-    ringed = ringed and levels > 1 and levels & (levels - 1) == 0
+    ringed = mesh.shape["prow"] == 1 and mesh.shape["pcol"] == 16
     return jax.shard_map(
         fast if ringed else on_device, mesh=mesh, in_specs=in_specs, out_specs=out_specs, check_vma=False
     )

time: 165 us -> 164 us (level)
  no operation moved by 1% of the time
where the time goes in v4:
time: 164 us; the launch traced here: 163 us
  waiting for transfers between devices  62.8 us (38%)
  Pallas kernels  51.4 us (31%)
  starting transfers between devices  40.7 us (25%)
  local copies, waits for them, and re-layouts  7.05 us (4%)
    ppermute x42, waiting for transfers between devices, send(): return lax.ppermute(value, 'pcol', pairs)  62.8 us
    ppermute x42, starting transfers between devices, send(): return lax.ppermute(value, 'pcol', pairs)  40.7 us
    pallas_call x6, Pallas kernels, multiply(): pl.pallas_call(functools.partial(multiply_kernel, tuple(layout), start is...  36.2 us
    pallas_call x1, Pallas kernels, window_blocks_of(): pl.pallas_call(functools.partial(window_kernel, width, steps, tops), in_s...  5.68 us
    pallas_call x1, Pallas kernels, solve_columns(): pl.pallas_call(functools.partial(columns_kernel, width, steps), out_shape...  4.29 us
    unnamed x54, local copies, waits for them, and re-layouts  3.94 us
  transfers between devices with their start and end apart: 42, of which 18 were waited for; matrix products, arithmetic and copies ran while one was open for 1% of the time, Pallas kernels for 30%

profile of v4, /device:TPU:0, one launch (start us, length us, event | category | flops | bytes accessed | tf_op | source)
XLA Modules:
  0.0 163.3 jit_solution(11187806876578559646)
XLA Ops:
  1.1 2.9 %shard_map.68 = (f32[384,768]{1,0:T(8,128)}, f32[256,384]{1,0:T(8,128)}, f32[256,384]{1,0:T(8,128)}, f32[256,384]{1,0:T(8,128)}) custom-call(s32[1]{0:T(128)} %bitcast.index_ref.core_ref, s32[3,24]{1,0:T(4,128)} %structure_ref.1, f32[384,768]{1,0:T(8,128)} %factor_ref.2), custom_call_target="tpu_custom_call" | custom-call | flops 1 | bytes 1 | tf_op jit(solution)/shard_map/pallas_call | solution.py:170
  4.0 2.6 %collective-permute-start.1 = (f32[256,384]{1,0:T(8,128)}, f32[256,384]{1,0:T(8,128)S(1)}, u32[]{:S(2)}, u32[]{:S(2)}) collective-permute-start(f32[256,384]{1,0:T(8,128)} %get-tuple-element.52.refs_4_), channel_id=1, source_target_pairs={{0,4},{1,5},{4,8},{5,9},{8,12},{9,13},{12,14},{13,15},{14,10},{15,... | collective-permute-start | bytes 1179656 | tf_op jit(solution)/shard_map/ppermute | solution.py:453
  6.6 2.0 %collective-permute-start.4 = (f32[256,384]{1,0:T(8,128)}, f32[256,384]{1,0:T(8,128)S(1)}, u32[]{:S(2)}, u32[]{:S(2)}) collective-permute-start(f32[256,384]{1,0:T(8,128)} %get-tuple-element.53.refs_5_), channel_id=1, source_target_pairs={{0,4},{1,5},{4,8},{5,9},{8,12},{9,13},{12,14},{13,15},{14,10},{15,... | collective-permute-start | bytes 1179656 | tf_op jit(solution)/shard_map/ppermute | solution.py:453
  8.6 8.1 %collective-permute-done.1.refs_6_ = f32[256,384]{1,0:T(8,128)S(1)} collective-permute-done((f32[256,384]{1,0:T(8,128)}, f32[256,384]{1,0:T(8,128)S(1)}, u32[]{:S(2)}, u32[]{:S(2)}) %collective-permute-start.1) | collective-permute-done | bytes 393248 | tf_op jit(solution)/shard_map/ppermute | solution.py:453
  16.7 2.0 %collective-permute-start.2 = (f32[256,384]{1,0:T(8,128)S(1)}, f32[256,384]{1,0:T(8,128)}, u32[]{:S(2)}, u32[]{:S(2)}) collective-permute-start(f32[256,384]{1,0:T(8,128)S(1)} %collective-permute-done.1.refs_6_), channel_id=1, source_target_pairs={{0,4},{1,5},{4,8},{5,9},{8,12},{9,13},{12,14},{13,15},{14,10},{15,... | collective-permute-start | bytes 1179656 | tf_op jit(solution)/shard_map/ppermute | solution.py:453
  18.8 6.3 %collective-permute-done.4.refs_7_ = f32[256,384]{1,0:T(8,128)S(1)} collective-permute-done((f32[256,384]{1,0:T(8,128)}, f32[256,384]{1,0:T(8,128)S(1)}, u32[]{:S(2)}, u32[]{:S(2)}) %collective-permute-start.4) | collective-permute-done | bytes 393248 | tf_op jit(solution)/shard_map/ppermute | solution.py:453
  25.1 2.0 %collective-permute-start.5 = (f32[256,384]{1,0:T(8,128)S(1)}, f32[256,384]{1,0:T(8,128)}, u32[]{:S(2)}, u32[]{:S(2)}) collective-permute-start(f32[256,384]{1,0:T(8,128)S(1)} %collective-permute-done.4.refs_7_), channel_id=1, source_target_pairs={{0,4},{1,5},{4,8},{5,9},{8,12},{9,13},{12,14},{13,15},{14,10},{15,... | collective-permute-start | bytes 1179656 | tf_op jit(solution)/shard_map/ppermute | solution.py:453
  27.2 6.5 %collective-permute-done.2.refs_10_ = f32[256,384]{1,0:T(8,128)} collective-permute-done((f32[256,384]{1,0:T(8,128)S(1)}, f32[256,384]{1,0:T(8,128)}, u32[]{:S(2)}, u32[]{:S(2)}) %collective-permute-start.2) | collective-permute-done | bytes 393248 | tf_op jit(solution)/shard_map/ppermute | solution.py:453
  33.7 2.0 %collective-permute-done.11.refs_5_ = f32[256,384]{1,0:T(8,128)S(1)} collective-permute-done((f32[256,384]{1,0:T(8,128)S(1)}, f32[256,384]{1,0:T(8,128)S(1)}, u32[]{:S(2)}, u32[]{:S(2)}) %collective-permute-start.11) | collective-permute-done | bytes 393248 | tf_op jit(solution)/shard_map/ppermute | solution.py:453
  35.7 6.2 %collective-permute-done.5.refs_11_ = f32[256,384]{1,0:T(8,128)} collective-permute-done((f32[256,384]{1,0:T(8,128)S(1)}, f32[256,384]{1,0:T(8,128)}, u32[]{:S(2)}, u32[]{:S(2)}) %collective-permute-start.5) | collective-permute-done | bytes 393248 | tf_op jit(solution)/shard_map/ppermute | solution.py:453
  41.9 1.8 %collective-permute-start.3 = (f32[256,384]{1,0:T(8,128)}, f32[256,384]{1,0:T(8,128)S(1)}, u32[]{:S(2)}, u32[]{:S(2)}) collective-permute-start(f32[256,384]{1,0:T(8,128)} %collective-permute-done.2.refs_10_), channel_id=1, source_target_pairs={{0,4},{1,5},{4,8},{5,9},{8,12},{9,13},{12,14},{13,15},{14,10},{15,... | collective-permute-start | bytes 1179656 | tf_op jit(solution)/shard_map/ppermute | solution.py:453
  46.1 8.4 %shard_map.69 = (f32[512,384]{1,0:T(8,128)}, f32[512,384]{1,0:T(8,128)}) custom-call(s32[1]{0:T(128)} %bitcast.index_ref.core_ref, f32[6144,384]{1,0:T(8,128)} %refs_2_.12, f32[6144,384]{1,0:T(8,128)} %collective-permute-done.refs_1_.refs_3_, f32[6144,384]{1,0:T(8,128)} %refs_2_.12, f32[6144,384]{1,0:T(8,128)} %collective-permute-done.refs_1_.refs_3_, ...), custom_call_target="tpu_custom_call" | custom-call | flops 1 | bytes 1 | tf_op jit(solution)/shard_map/pallas_call | solution.py:294
  54.6 6.9 %collective-permute-done.6.refs_7_ = f32[256,384]{1,0:T(8,128)S(1)} collective-permute-done((f32[256,384]{1,0:T(8,128)}, f32[256,384]{1,0:T(8,128)S(1)}, u32[]{:S(2)}, u32[]{:S(2)}) %collective-permute-start.6) | collective-permute-done | bytes 393248 | tf_op jit(solution)/shard_map/ppermute | solution.py:453
  63.5 1.6 collective-permute-start.13
  65.6 5.8 %shard_map.70 = (f32[512,384]{1,0:T(8,128)}, f32[512,384]{1,0:T(8,128)}) custom-call(s32[1]{0:T(128)} %bitcast.index_ref.core_ref, f32[6144,384]{1,0:T(8,128)} %refs_2_.12, f32[6144,384]{1,0:T(8,128)} %collective-permute-done.refs_1_.refs_3_, f32[6144,384]{1,0:T(8,128)} %refs_2_.12, f32[6144,384]{1,0:T(8,128)} %collective-permute-done.refs_1_.refs_3_, ...), custom_call_target="tpu_custom_call" | custom-call | flops 1 | bytes 1 | tf_op jit(solution)/shard_map/pallas_call | solution.py:294
  71.3 2.2 %collective-permute-done.16.refs_7_ = f32[256,384]{1,0:T(8,128)S(1)} collective-permute-done((f32[256,384]{1,0:T(8,128)S(1)}, f32[256,384]{1,0:T(8,128)S(1)}, u32[]{:S(2)}, u32[]{:S(2)}) %collective-permute-start.16) | collective-permute-done | bytes 393248 | tf_op jit(solution)/shard_map/ppermute | solution.py:453
  75.9 7.6 %shard_map.71 = (f32[512,384]{1,0:T(8,128)}, f32[512,384]{1,0:T(8,128)}, f32[2304,128]{1,0:T(8,128)}) custom-call(s32[1]{0:T(128)} %bitcast.index_ref.core_ref, f32[6144,384]{1,0:T(8,128)} %refs_2_.12, f32[6144,384]{1,0:T(8,128)} %collective-permute-done.refs_1_.refs_3_, f32[6144,384]{1,0:T(8,128)} %refs_2_.12, ...), custom_call_target="tpu_custom_call" | custom-call | flops 1 | bytes 1 | tf_op jit(solution)/shard_map/pallas_call | solution.py:294
  87.4 1.6 %collective-permute-start.21 = (f32[576,128]{1,0:T(8,128)S(1)}, f32[576,128]{1,0:T(8,128)S(1)}, u32[]{:S(2)}, u32[]{:S(2)}) collective-permute-start(f32[576,128]{1,0:T(8,128)S(1)} %dynamic-slice_bitcast_fusion.1), channel_id=1, source_target_pairs={{0,2},{1,3},{2,0},{3,1},{4,6},{5,7},{6,4},{7,5},{8,10},{9,11},{10,... | collective-permute-start | bytes 884744 | tf_op jit(solution)/shard_map/ppermute | solution.py:453
  89.1 8.5 %collective-permute-done.18.refs_7_ = f32[256,384]{1,0:T(8,128)} collective-permute-done((f32[256,384]{1,0:T(8,128)}, f32[256,384]{1,0:T(8,128)}, u32[]{:S(2)}, u32[]{:S(2)}) %collective-permute-start.18) | collective-permute-done | bytes 393248 | tf_op jit(solution)/shard_map/ppermute | solution.py:453
  97.6 5.6 %shard_map.72 = (f32[256,384]{1,0:T(8,128)}, f32[256,384]{1,0:T(8,128)}) custom-call(s32[1]{0:T(128)} %bitcast.index_ref.core_ref, f32[6144,384]{1,0:T(8,128)} %refs_2_.12, f32[6144,384]{1,0:T(8,128)} %collective-permute-done.refs_1_.refs_3_, f32[6144,384]{1,0:T(8,128)} %refs_2_.12, f32[6144,384]{1,0:T(8,128)} %collective-permute-done.refs_1_.refs_3_, ...), custom_call_target="tpu_custom_call" | custom-call | flops 1 | bytes 1 | tf_op jit(solution)/shard_map/pallas_call | solution.py:294
  103.9 2.0 %collective-permute-start.22 = (f32[256,384]{1,0:T(8,128)}, f32[256,384]{1,0:T(8,128)S(1)}, u32[]{:S(2)}, u32[]{:S(2)}) collective-permute-start(f32[256,384]{1,0:T(8,128)} %copy-done.21), channel_id=1, source_target_pairs={{4,0},{5,1},{8,4},{9,5},{12,8},{13,9},{14,12},{15,13},{10,14},{11,... | collective-permute-start | bytes 1179656 | tf_op jit(solution)/shard_map/ppermute | solution.py:453
  106.1 3.5 %collective-permute-start.27 = (f32[144,128]{1,0:T(8,128)S(1)}, f32[144,128]{1,0:T(8,128)S(1)}, u32[]{:S(2)}, u32[]{:S(2)}) collective-permute-start(f32[144,128]{1,0:T(8,128)S(1)} %get-tuple-element.105), channel_id=1, source_target_pairs={{0,8},{1,9},{2,10},{3,11},{4,12},{5,13},{6,14},{7,15},{8,0},{9,1},... | collective-permute-start | bytes 221192 | tf_op jit(solution)/shard_map/ppermute | solution.py:453
  110.5 4.3 %shard_map.74.columns_ref = f32[384,768]{1,0:T(8,128)} custom-call(f32[512,384]{1,0:T(8,128)} %get-tuple-element.81.image_ref, f32[512,384]{1,0:T(8,128)} %copy-done.5, f32[768,768]{1,0:T(8,128)} %refs_2_.13), custom_call_target="tpu_custom_call" | custom-call | flops 1 | bytes 1 | tf_op jit(solution)/shard_map/pallas_call | solution.py:329
  115.5 4.1 %shard_map.73 = (f32[256,384]{1,0:T(8,128)}, f32[256,384]{1,0:T(8,128)}) custom-call(s32[1]{0:T(128)} %bitcast.index_ref.core_ref, f32[6144,384]{1,0:T(8,128)} %refs_2_.12, f32[6144,384]{1,0:T(8,128)} %collective-permute-done.refs_1_.refs_3_, f32[6144,384]{1,0:T(8,128)} %refs_2_.12, f32[6144,384]{1,0:T(8,128)} %collective-permute-done.refs_1_.refs_3_, ...), custom_call_target="tpu_custom_call" | custom-call | flops 1 | bytes 1 | tf_op jit(solution)/shard_map/pallas_call | solution.py:294
  119.7 1.9 %collective-permute-done.28 = f32[144,128]{1,0:T(8,128)S(1)} collective-permute-done((f32[144,128]{1,0:T(8,128)S(1)}, f32[144,128]{1,0:T(8,128)S(1)}, u32[]{:S(2)}, u32[]{:S(2)}) %collective-permute-start.28) | collective-permute-done | bytes 73760 | tf_op jit(solution)/shard_map/ppermute | solution.py:453
  122.5 2.5 %collective-permute-start.32 = (f32[144,128]{1,0:T(8,128)S(1)}, f32[144,128]{1,0:T(8,128)S(1)}, u32[]{:S(2)}, u32[]{:S(2)}) collective-permute-start(f32[144,128]{1,0:T(8,128)S(1)} %fusion.3), channel_id=1, source_target_pairs={{0,8},{1,9},{2,10},{3,11},{4,12},{5,13},{6,14},{7,15},{8,0},{9,1},... | collective-permute-start | bytes 221192 | tf_op jit(solution)/shard_map/ppermute | solution.py:453
  129.4 2.6 %collective-permute-done.33 = f32[144,128]{1,0:T(8,128)S(1)} collective-permute-done((f32[144,128]{1,0:T(8,128)S(1)}, f32[144,128]{1,0:T(8,128)S(1)}, u32[]{:S(2)}, u32[]{:S(2)}) %collective-permute-start.33) | collective-permute-done | bytes 73760 | tf_op jit(solution)/shard_map/ppermute | solution.py:453
  135.1 4.8 %shard_map.75 = (f32[256,384]{1,0:T(8,128)}, f32[256,384]{1,0:T(8,128)}, f32[384,128]{1,0:T(8,128)}) custom-call(s32[1]{0:T(128)} %bitcast.index_ref.core_ref, f32[6144,384]{1,0:T(8,128)} %refs_2_.12, f32[6144,384]{1,0:T(8,128)} %collective-permute-done.refs_1_.refs_3_, f32[6144,384]{1,0:T(8,128)} %refs_2_.12, ...), custom_call_target="tpu_custom_call" | custom-call | flops 1 | bytes 1 | tf_op jit(solution)/shard_map/pallas_call | solution.py:294
  143.5 4.1 %collective-permute-done.35 = f32[192,128]{1,0:T(8,128)S(1)} collective-permute-done((f32[192,128]{1,0:T(8,128)S(1)}, f32[192,128]{1,0:T(8,128)S(1)}, u32[]{:S(2)}, u32[]{:S(2)}) %collective-permute-start.35) | collective-permute-done | bytes 98336 | tf_op jit(solution)/shard_map/ppermute | solution.py:453
  150.0 2.1 %collective-permute-start.39 = (f32[192,128]{1,0:T(8,128)S(1)}, f32[192,128]{1,0:T(8,128)S(1)}, u32[]{:S(2)}, u32[]{:S(2)}) collective-permute-start(f32[192,128]{1,0:T(8,128)S(1)} %add.98), channel_id=1, source_target_pairs={{0,12},{1,13},{2,14},{3,15},{4,8},{5,9},{6,10},{7,11},{8,4},{9,5},... | collective-permute-start | bytes 294920 | tf_op jit(solution)/shard_map/ppermute | solution.py:453
  152.0 5.7 %shard_map.76.base_ref = f32[768,768]{1,0:T(8,128)} custom-call(s32[1]{0:T(128)} %bitcast.index_ref.core_ref, f32[1152,128]{1,0:T(8,128)} %copy-done.1, f32[1152,128]{1,0:T(8,128)} %copy-done.6, f32[768,768]{1,0:T(8,128)} %refs_2_.13, f32[3,256,256]{2,1,0:T(8,128)} %refs_3_.1), custom_call_target="tpu_custom_call" | custom-call | flops 1 | bytes 1 | tf_op jit(solution)/shard_map/pallas_call | solution.py:420
  160.9 2.4 %shard_map.77 = (f32[384,768]{1,0:T(8,128)}, f32[768,768]{1,0:T(8,128)}) custom-call(s32[1]{0:T(128)} %bitcast.index_ref.core_ref, f32[192,128]{1,0:T(8,128)} %copy-done.20, f32[192,128]{1,0:T(8,128)} %copy-done.25, f32[256,384]{1,0:T(8,128)} %get-tuple-element.96.image_ref, f32[256,384]{1,0:T(8,128)} %copy-done.19, ...), custom_call_target="tpu_custom_call", output_to_operand_aliasing={{0}: (5, {}), {1}: (6, {})} | custom-call | flops 1 | bytes 1 | tf_op jit(solution)/shard_map/pallas_call | solution.py:367
  (134 shorter events, 31.8 us)
Async XLA Ops:
  0.6 45.0 %collective-permute-start = (f32[6144,384]{1,0:T(8,128)}, f32[6144,384]{1,0:T(8,128)}, u32[]{:S(2)}, u32[]{:S(2)}) collective-permute-start(f32[6144,384]{1,0:T(8,128)} %refs_2_.12), channel_id=1, source_target_pairs={{0,1},{1,0},{2,3},{3,2},{4,5},{5,4},{6,7},{7,6},{8,9},{9,8},{10,11... | collective-permute-start | bytes 28311560 | tf_op jit(solution)/shard_map/ppermute | solution.py:453
  4.0 12.7 %collective-permute-start.1 = (f32[256,384]{1,0:T(8,128)}, f32[256,384]{1,0:T(8,128)S(1)}, u32[]{:S(2)}, u32[]{:S(2)}) collective-permute-start(f32[256,384]{1,0:T(8,128)} %get-tuple-element.52.refs_4_), channel_id=1, source_target_pairs={{0,4},{1,5},{4,8},{5,9},{8,12},{9,13},{12,14},{13,15},{14,10},{15,... | collective-permute-start | bytes 1179656 | tf_op jit(solution)/shard_map/ppermute | solution.py:453
  6.6 12.2 %collective-permute-start.10 = (f32[256,384]{1,0:T(8,128)}, f32[256,384]{1,0:T(8,128)S(1)}, u32[]{:S(2)}, u32[]{:S(2)}) collective-permute-start(f32[256,384]{1,0:T(8,128)} %get-tuple-element.53.refs_5_), channel_id=1, source_target_pairs={{4,0},{5,1},{8,4},{9,5},{12,8},{13,9},{14,12},{15,13},{10,14},{11,... | collective-permute-start | bytes 1179656 | tf_op jit(solution)/shard_map/ppermute | solution.py:453
  6.6 18.5 %collective-permute-start.4 = (f32[256,384]{1,0:T(8,128)}, f32[256,384]{1,0:T(8,128)S(1)}, u32[]{:S(2)}, u32[]{:S(2)}) collective-permute-start(f32[256,384]{1,0:T(8,128)} %get-tuple-element.53.refs_5_), channel_id=1, source_target_pairs={{0,4},{1,5},{4,8},{5,9},{8,12},{9,13},{12,14},{13,15},{14,10},{15,... | collective-permute-start | bytes 1179656 | tf_op jit(solution)/shard_map/ppermute | solution.py:453
  8.6 18.6 %collective-permute-start.7 = (f32[256,384]{1,0:T(8,128)}, f32[256,384]{1,0:T(8,128)S(1)}, u32[]{:S(2)}, u32[]{:S(2)}) collective-permute-start(f32[256,384]{1,0:T(8,128)} %get-tuple-element.52.refs_4_), channel_id=1, source_target_pairs={{4,0},{5,1},{8,4},{9,5},{12,8},{13,9},{14,12},{15,13},{10,14},{11,... | collective-permute-start | bytes 1179656 | tf_op jit(solution)/shard_map/ppermute | solution.py:453
  16.7 17.0 %collective-permute-start.2 = (f32[256,384]{1,0:T(8,128)S(1)}, f32[256,384]{1,0:T(8,128)}, u32[]{:S(2)}, u32[]{:S(2)}) collective-permute-start(f32[256,384]{1,0:T(8,128)S(1)} %collective-permute-done.1.refs_6_), channel_id=1, source_target_pairs={{0,4},{1,5},{4,8},{5,9},{8,12},{9,13},{12,14},{13,15},{14,10},{15,... | collective-permute-start | bytes 1179656 | tf_op jit(solution)/shard_map/ppermute | solution.py:453
  18.8 16.9 %collective-permute-start.11 = (f32[256,384]{1,0:T(8,128)S(1)}, f32[256,384]{1,0:T(8,128)S(1)}, u32[]{:S(2)}, u32[]{:S(2)}) collective-permute-start(f32[256,384]{1,0:T(8,128)S(1)} %collective-permute-done.10.refs_9_), channel_id=1, source_target_pairs={{4,0},{5,1},{8,4},{9,5},{12,8},{13,9},{14,12},{15,13},{10,14},{11,... | collective-permute-start | bytes 1179656 | tf_op jit(solution)/shard_map/ppermute | solution.py:453
  25.1 16.8 %collective-permute-start.5 = (f32[256,384]{1,0:T(8,128)S(1)}, f32[256,384]{1,0:T(8,128)}, u32[]{:S(2)}, u32[]{:S(2)}) collective-permute-start(f32[256,384]{1,0:T(8,128)S(1)} %collective-permute-done.4.refs_7_), channel_id=1, source_target_pairs={{0,4},{1,5},{4,8},{5,9},{8,12},{9,13},{12,14},{13,15},{14,10},{15,... | collective-permute-start | bytes 1179656 | tf_op jit(solution)/shard_map/ppermute | solution.py:453
  27.2 16.9 %collective-permute-start.8 = (f32[256,384]{1,0:T(8,128)S(1)}, f32[256,384]{1,0:T(8,128)S(1)}, u32[]{:S(2)}, u32[]{:S(2)}) collective-permute-start(f32[256,384]{1,0:T(8,128)S(1)} %collective-permute-done.7.refs_8_), channel_id=1, source_target_pairs={{4,0},{5,1},{8,4},{9,5},{12,8},{13,9},{14,12},{15,13},{10,14},{11,... | collective-permute-start | bytes 1179656 | tf_op jit(solution)/shard_map/ppermute | solution.py:453
  33.7 37.7 %collective-permute-start.17 = (f32[384,768]{1,0:T(8,128)}, f32[384,768]{1,0:T(8,128)S(1)}, u32[]{:S(2)}, u32[]{:S(2)}) collective-permute-start(f32[384,768]{1,0:T(8,128)} %get-tuple-element.67.refs_10_.refs_9_), channel_id=1, source_target_pairs={{0,1},{1,0},{2,3},{3,2},{4,5},{5,4},{6,7},{7,6},{8,9},{9,8},{10,11... | collective-permute-start | bytes 3538952 | tf_op jit(solution)/shard_map/ppermute | solution.py:453
  35.6 18.9 %collective-permute-start.12 = (f32[256,384]{1,0:T(8,128)S(1)}, f32[256,384]{1,0:T(8,128)S(1)}, u32[]{:S(2)}, u32[]{:S(2)}) collective-permute-start(f32[256,384]{1,0:T(8,128)S(1)} %collective-permute-done.11.refs_5_), channel_id=1, source_target_pairs={{4,0},{5,1},{8,4},{9,5},{12,8},{13,9},{14,12},{15,13},{10,14},{11,... | collective-permute-start | bytes 1179656 | tf_op jit(solution)/shard_map/ppermute | solution.py:453
  41.9 12.7 %collective-permute-start.3 = (f32[256,384]{1,0:T(8,128)}, f32[256,384]{1,0:T(8,128)S(1)}, u32[]{:S(2)}, u32[]{:S(2)}) collective-permute-start(f32[256,384]{1,0:T(8,128)} %collective-permute-done.2.refs_10_), channel_id=1, source_target_pairs={{0,4},{1,5},{4,8},{5,9},{8,12},{9,13},{12,14},{13,15},{14,10},{15,... | collective-permute-start | bytes 1179656 | tf_op jit(solution)/shard_map/ppermute | solution.py:453
  44.1 17.4 %collective-permute-start.6 = (f32[256,384]{1,0:T(8,128)}, f32[256,384]{1,0:T(8,128)S(1)}, u32[]{:S(2)}, u32[]{:S(2)}) collective-permute-start(f32[256,384]{1,0:T(8,128)} %collective-permute-done.5.refs_11_), channel_id=1, source_target_pairs={{0,4},{1,5},{4,8},{5,9},{8,12},{9,13},{12,14},{13,15},{14,10},{15,... | collective-permute-start | bytes 1179656 | tf_op jit(solution)/shard_map/ppermute | solution.py:453
  45.6 15.8 %collective-permute-start.9 = (f32[256,384]{1,0:T(8,128)S(1)}, f32[256,384]{1,0:T(8,128)S(1)}, u32[]{:S(2)}, u32[]{:S(2)}) collective-permute-start(f32[256,384]{1,0:T(8,128)S(1)} %collective-permute-done.8.refs_4_), channel_id=1, source_target_pairs={{4,0},{5,1},{8,4},{9,5},{12,8},{13,9},{14,12},{15,13},{10,14},{11,... | collective-permute-start | bytes 1179656 | tf_op jit(solution)/shard_map/ppermute | solution.py:453
  61.5 12.1 %collective-permute-start.16 = (f32[256,384]{1,0:T(8,128)S(1)}, f32[256,384]{1,0:T(8,128)S(1)}, u32[]{:S(2)}, u32[]{:S(2)}) collective-permute-start(f32[256,384]{1,0:T(8,128)S(1)} %collective-permute-done.12.refs_5_), channel_id=1, source_target_pairs={{4,0},{5,1},{8,4},{9,5},{12,8},{13,9},{14,12},{15,13},{10,14},{11,... | collective-permute-start | bytes 1179656 | tf_op jit(solution)/shard_map/ppermute | solution.py:453
  63.0 12.1 %collective-permute-start.15 = (f32[256,384]{1,0:T(8,128)S(1)}, f32[256,384]{1,0:T(8,128)S(1)}, u32[]{:S(2)}, u32[]{:S(2)}) collective-permute-start(f32[256,384]{1,0:T(8,128)S(1)} %collective-permute-done.3.refs_6_), channel_id=1, source_target_pairs={{0,4},{1,5},{4,8},{5,9},{8,12},{9,13},{12,14},{13,15},{14,10},{15,... | collective-permute-start | bytes 1179656 | tf_op jit(solution)/shard_map/ppermute | solution.py:453
  63.5 20.0 %collective-permute-start.13 = (f32[256,384]{1,0:T(8,128)}, f32[256,384]{1,0:T(8,128)}, u32[]{:S(2)}, u32[]{:S(2)}) collective-permute-start(f32[256,384]{1,0:T(8,128)} %get-tuple-element.58.refs_4_), channel_id=1, source_target_pairs={{0,4},{1,5},{4,8},{5,9},{8,12},{9,13},{12,14},{13,15},{14,10},{15,... | collective-permute-start | bytes 1179656 | tf_op jit(solution)/shard_map/ppermute | solution.py:453
  65.2 18.3 %collective-permute-start.14 = (f32[256,384]{1,0:T(8,128)}, f32[256,384]{1,0:T(8,128)}, u32[]{:S(2)}, u32[]{:S(2)}) collective-permute-start(f32[256,384]{1,0:T(8,128)} %get-tuple-element.58.refs_4_), channel_id=1, source_target_pairs={{4,0},{5,1},{8,4},{9,5},{12,8},{13,9},{14,12},{15,13},{10,14},{11,... | collective-permute-start | bytes 1179656 | tf_op jit(solution)/shard_map/ppermute | solution.py:453
  84.8 24.7 %collective-permute-start.29 = (f32[512,384]{1,0:T(8,128)}, f32[512,384]{1,0:T(8,128)S(1)}, u32[]{:S(2)}, u32[]{:S(2)}) collective-permute-start(f32[512,384]{1,0:T(8,128)} %get-tuple-element.82), channel_id=1, source_target_pairs={{0,1},{1,0},{2,3},{3,2},{4,5},{5,4},{6,7},{7,6},{8,9},{9,8},{10,11... | collective-permute-start | bytes 2359304 | tf_op jit(solution)/shard_map/ppermute | solution.py:453
  85.3 12.3 %collective-permute-start.18 = (f32[256,384]{1,0:T(8,128)}, f32[256,384]{1,0:T(8,128)}, u32[]{:S(2)}, u32[]{:S(2)}) collective-permute-start(f32[256,384]{1,0:T(8,128)} %collective-permute-done.13.refs_5_), channel_id=1, source_target_pairs={{0,4},{1,5},{4,8},{5,9},{8,12},{9,13},{12,14},{13,15},{14,10},{15,... | collective-permute-start | bytes 1179656 | tf_op jit(solution)/shard_map/ppermute | solution.py:453
  85.8 17.4 %collective-permute-start.19 = (f32[256,384]{1,0:T(8,128)}, f32[256,384]{1,0:T(8,128)S(1)}, u32[]{:S(2)}, u32[]{:S(2)}) collective-permute-start(f32[256,384]{1,0:T(8,128)} %collective-permute-done.14.refs_6_), channel_id=1, source_target_pairs={{4,0},{5,1},{8,4},{9,5},{12,8},{13,9},{14,12},{15,13},{10,14},{11,... | collective-permute-start | bytes 1179656 | tf_op jit(solution)/shard_map/ppermute | solution.py:453
  87.4 15.7 %collective-permute-start.21 = (f32[576,128]{1,0:T(8,128)S(1)}, f32[576,128]{1,0:T(8,128)S(1)}, u32[]{:S(2)}, u32[]{:S(2)}) collective-permute-start(f32[576,128]{1,0:T(8,128)S(1)} %dynamic-slice_bitcast_fusion.1), channel_id=1, source_target_pairs={{0,2},{1,3},{2,0},{3,1},{4,6},{5,7},{6,4},{7,5},{8,10},{9,11},{10,... | collective-permute-start | bytes 884744 | tf_op jit(solution)/shard_map/ppermute | solution.py:453
  103.9 10.9 %collective-permute-start.23 = (f32[256,384]{1,0:T(8,128)}, f32[256,384]{1,0:T(8,128)S(1)}, u32[]{:S(2)}, u32[]{:S(2)}) collective-permute-start(f32[256,384]{1,0:T(8,128)} %collective-permute-done.18.refs_7_), channel_id=1, source_target_pairs={{0,4},{1,5},{4,8},{5,9},{8,12},{9,13},{12,14},{13,15},{14,10},{15,... | collective-permute-start | bytes 1179656 | tf_op jit(solution)/shard_map/ppermute | solution.py:453
  103.9 24.0 %collective-permute-start.22 = (f32[256,384]{1,0:T(8,128)}, f32[256,384]{1,0:T(8,128)S(1)}, u32[]{:S(2)}, u32[]{:S(2)}) collective-permute-start(f32[256,384]{1,0:T(8,128)} %copy-done.21), channel_id=1, source_target_pairs={{4,0},{5,1},{8,4},{9,5},{12,8},{13,9},{14,12},{15,13},{10,14},{11,... | collective-permute-start | bytes 1179656 | tf_op jit(solution)/shard_map/ppermute | solution.py:453
  106.0 13.7 %collective-permute-start.26 = (f32[144,128]{1,0:T(8,128)S(1)}, f32[144,128]{1,0:T(8,128)S(1)}, u32[]{:S(2)}, u32[]{:S(2)}) collective-permute-start(f32[144,128]{1,0:T(8,128)S(1)} %get-tuple-element.106), channel_id=1, source_target_pairs={{0,4},{1,5},{2,6},{3,7},{4,0},{5,1},{6,2},{7,3},{8,12},{9,13},{10,... | collective-permute-start | bytes 221192 | tf_op jit(solution)/shard_map/ppermute | solution.py:453
  106.1 13.6 %collective-permute-start.27 = (f32[144,128]{1,0:T(8,128)S(1)}, f32[144,128]{1,0:T(8,128)S(1)}, u32[]{:S(2)}, u32[]{:S(2)}) collective-permute-start(f32[144,128]{1,0:T(8,128)S(1)} %get-tuple-element.105), channel_id=1, source_target_pairs={{0,8},{1,9},{2,10},{3,11},{4,12},{5,13},{6,14},{7,15},{8,0},{9,1},... | collective-permute-start | bytes 221192 | tf_op jit(solution)/shard_map/ppermute | solution.py:453
  109.5 12.0 %collective-permute-start.28 = (f32[144,128]{1,0:T(8,128)S(1)}, f32[144,128]{1,0:T(8,128)S(1)}, u32[]{:S(2)}, u32[]{:S(2)}) collective-permute-start(f32[144,128]{1,0:T(8,128)S(1)} %get-tuple-element.104), channel_id=1, source_target_pairs={{0,12},{1,13},{2,14},{3,15},{4,8},{5,9},{6,10},{7,11},{8,4},{9,5},... | collective-permute-start | bytes 221192 | tf_op jit(solution)/shard_map/ppermute | solution.py:453
  121.6 7.8 %collective-permute-start.31 = (f32[144,128]{1,0:T(8,128)S(1)}, f32[144,128]{1,0:T(8,128)S(1)}, u32[]{:S(2)}, u32[]{:S(2)}) collective-permute-start(f32[144,128]{1,0:T(8,128)S(1)} %fusion.3), channel_id=1, source_target_pairs={{0,4},{1,5},{2,6},{3,7},{4,0},{5,1},{6,2},{7,3},{8,12},{9,13},{10,... | collective-permute-start | bytes 221192 | tf_op jit(solution)/shard_map/ppermute | solution.py:453
  132.2 9.9 %collective-permute-start.34 = (f32[576,128]{1,0:T(8,128)S(1)}, f32[576,128]{1,0:T(8,128)S(1)}, u32[]{:S(2)}, u32[]{:S(2)}) collective-permute-start(f32[576,128]{1,0:T(8,128)S(1)} %pad_maximum_fusion.1), channel_id=1, source_target_pairs={{0,2},{1,3},{2,0},{3,1},{4,6},{5,7},{6,4},{7,5},{8,10},{9,11},{10,... | collective-permute-start | bytes 884744 | tf_op jit(solution)/shard_map/ppermute | solution.py:453
  147.6 10.2 %collective-permute-start.37 = (f32[192,128]{1,0:T(8,128)S(1)}, f32[192,128]{1,0:T(8,128)S(1)}, u32[]{:S(2)}, u32[]{:S(2)}) collective-permute-start(f32[192,128]{1,0:T(8,128)S(1)} %add.98), channel_id=1, source_target_pairs={{0,4},{1,5},{2,6},{3,7},{4,0},{5,1},{6,2},{7,3},{8,12},{9,13},{10,... | collective-permute-start | bytes 294920 | tf_op jit(solution)/shard_map/ppermute | solution.py:453
  148.9 9.9 %collective-permute-start.38 = (f32[192,128]{1,0:T(8,128)S(1)}, f32[192,128]{1,0:T(8,128)S(1)}, u32[]{:S(2)}, u32[]{:S(2)}) collective-permute-start(f32[192,128]{1,0:T(8,128)S(1)} %add.98), channel_id=1, source_target_pairs={{0,8},{1,9},{2,10},{3,11},{4,12},{5,13},{6,14},{7,15},{8,0},{9,1},... | collective-permute-start | bytes 294920 | tf_op jit(solution)/shard_map/ppermute | solution.py:453
  150.0 8.9 %collective-permute-start.39 = (f32[192,128]{1,0:T(8,128)S(1)}, f32[192,128]{1,0:T(8,128)S(1)}, u32[]{:S(2)}, u32[]{:S(2)}) collective-permute-start(f32[192,128]{1,0:T(8,128)S(1)} %add.98), channel_id=1, source_target_pairs={{0,12},{1,13},{2,14},{3,15},{4,8},{5,9},{6,10},{7,11},{8,4},{9,5},... | collective-permute-start | bytes 294920 | tf_op jit(solution)/shard_map/ppermute | solution.py:453
  (37 other events, 252.9 us)

commit v5 on v4

--- a/solution.py
+++ b/solution.py
@@ -111,7 +111,7 @@
     return (anc_columns, win_inverse)
 
 
-vmem_bytes = 60 * 1024 * 1024
+vmem_bytes = 56 * 1024 * 1024
 tile = 128
 little = pl.CostEstimate(flops=1, bytes_accessed=1, transcendentals=0)
 

time: 164 us -> 163 us (level)
    unnamed x54 -> x58, local copies, waits for them, and re-layouts: 3.94 us -> 4.27 us
where the time goes in v5:
time: 163 us
  waiting for transfers between devices  62.5 us (38%)
  Pallas kernels  51.5 us (32%)
  starting transfers between devices  39.9 us (24%)
  local copies, waits for them, and re-layouts  7.39 us (5%)
    ppermute x42, waiting for transfers between devices, send(): return lax.ppermute(value, 'pcol', pairs)  62.5 us
    ppermute x42, starting transfers between devices, send(): return lax.ppermute(value, 'pcol', pairs)  39.9 us
    pallas_call x6, Pallas kernels, multiply(): pl.pallas_call(functools.partial(multiply_kernel, tuple(layout), start is...  36.2 us
    pallas_call x1, Pallas kernels, window_blocks_of(): pl.pallas_call(functools.partial(window_kernel, width, steps, tops), in_s...  5.67 us
    pallas_call x1, Pallas kernels, solve_columns(): pl.pallas_call(functools.partial(columns_kernel, width, steps), out_shape...  4.31 us
    unnamed x58, local copies, waits for them, and re-layouts  4.27 us
  transfers between devices with their start and end apart: 42, of which 18 were waited for; matrix products, arithmetic and copies ran while one was open for 1% of the time, Pallas kernels for 30%

profile of v5, /device:TPU:0, one launch (start us, length us, event | category | flops | bytes accessed | tf_op | source)
XLA Modules:
  0.0 162.7 jit_solution(3598682352587657450)
XLA Ops:
  1.1 2.9 %shard_map.68 = (f32[384,768]{1,0:T(8,128)}, f32[256,384]{1,0:T(8,128)}, f32[256,384]{1,0:T(8,128)}, f32[256,384]{1,0:T(8,128)}) custom-call(s32[1]{0:T(128)} %bitcast.index_ref.core_ref, s32[3,24]{1,0:T(4,128)} %structure_ref.1, f32[384,768]{1,0:T(8,128)} %factor_ref.2), custom_call_target="tpu_custom_call" | custom-call | flops 1 | bytes 1 | tf_op jit(solution)/shard_map/pallas_call | solution.py:170
  4.0 2.6 %collective-permute-start.1 = (f32[256,384]{1,0:T(8,128)}, f32[256,384]{1,0:T(8,128)S(1)}, u32[]{:S(2)}, u32[]{:S(2)}) collective-permute-start(f32[256,384]{1,0:T(8,128)} %get-tuple-element.52.refs_4_), channel_id=1, source_target_pairs={{0,4},{1,5},{4,8},{5,9},{8,12},{9,13},{12,14},{13,15},{14,10},{15,... | collective-permute-start | bytes 1179656 | tf_op jit(solution)/shard_map/ppermute | solution.py:453
  6.6 2.0 %collective-permute-start.4 = (f32[256,384]{1,0:T(8,128)}, f32[256,384]{1,0:T(8,128)S(1)}, u32[]{:S(2)}, u32[]{:S(2)}) collective-permute-start(f32[256,384]{1,0:T(8,128)} %get-tuple-element.53.refs_5_), channel_id=1, source_target_pairs={{0,4},{1,5},{4,8},{5,9},{8,12},{9,13},{12,14},{13,15},{14,10},{15,... | collective-permute-start | bytes 1179656 | tf_op jit(solution)/shard_map/ppermute | solution.py:453
  8.6 8.1 %collective-permute-done.1.refs_6_ = f32[256,384]{1,0:T(8,128)S(1)} collective-permute-done((f32[256,384]{1,0:T(8,128)}, f32[256,384]{1,0:T(8,128)S(1)}, u32[]{:S(2)}, u32[]{:S(2)}) %collective-permute-start.1) | collective-permute-done | bytes 393248 | tf_op jit(solution)/shard_map/ppermute | solution.py:453
  16.7 2.0 %collective-permute-start.2 = (f32[256,384]{1,0:T(8,128)S(1)}, f32[256,384]{1,0:T(8,128)S(1)}, u32[]{:S(2)}, u32[]{:S(2)}) collective-permute-start(f32[256,384]{1,0:T(8,128)S(1)} %collective-permute-done.1.refs_6_), channel_id=1, source_target_pairs={{0,4},{1,5},{4,8},{5,9},{8,12},{9,13},{12,14},{13,15},{14,10},{15,... | collective-permute-start | bytes 1179656 | tf_op jit(solution)/shard_map/ppermute | solution.py:453
  18.8 6.3 %collective-permute-done.4.refs_7_ = f32[256,384]{1,0:T(8,128)S(1)} collective-permute-done((f32[256,384]{1,0:T(8,128)}, f32[256,384]{1,0:T(8,128)S(1)}, u32[]{:S(2)}, u32[]{:S(2)}) %collective-permute-start.4) | collective-permute-done | bytes 393248 | tf_op jit(solution)/shard_map/ppermute | solution.py:453
  25.1 2.0 %collective-permute-start.5 = (f32[256,384]{1,0:T(8,128)S(1)}, f32[256,384]{1,0:T(8,128)S(1)}, u32[]{:S(2)}, u32[]{:S(2)}) collective-permute-start(f32[256,384]{1,0:T(8,128)S(1)} %collective-permute-done.4.refs_7_), channel_id=1, source_target_pairs={{0,4},{1,5},{4,8},{5,9},{8,12},{9,13},{12,14},{13,15},{14,10},{15,... | collective-permute-start | bytes 1179656 | tf_op jit(solution)/shard_map/ppermute | solution.py:453
  27.2 6.3 %collective-permute-done.2.refs_10_ = f32[256,384]{1,0:T(8,128)S(1)} collective-permute-done((f32[256,384]{1,0:T(8,128)S(1)}, f32[256,384]{1,0:T(8,128)S(1)}, u32[]{:S(2)}, u32[]{:S(2)}) %collective-permute-start.2) | collective-permute-done | bytes 393248 | tf_op jit(solution)/shard_map/ppermute | solution.py:453
  33.6 2.1 %collective-permute-done.11.refs_5_ = f32[256,384]{1,0:T(8,128)S(1)} collective-permute-done((f32[256,384]{1,0:T(8,128)S(1)}, f32[256,384]{1,0:T(8,128)S(1)}, u32[]{:S(2)}, u32[]{:S(2)}) %collective-permute-start.11) | collective-permute-done | bytes 393248 | tf_op jit(solution)/shard_map/ppermute | solution.py:453
  35.6 6.1 %collective-permute-done.5.refs_11_ = f32[256,384]{1,0:T(8,128)S(1)} collective-permute-done((f32[256,384]{1,0:T(8,128)S(1)}, f32[256,384]{1,0:T(8,128)S(1)}, u32[]{:S(2)}, u32[]{:S(2)}) %collective-permute-start.5) | collective-permute-done | bytes 393248 | tf_op jit(solution)/shard_map/ppermute | solution.py:453
  41.8 1.8 %collective-permute-start.3 = (f32[256,384]{1,0:T(8,128)S(1)}, f32[256,384]{1,0:T(8,128)S(1)}, u32[]{:S(2)}, u32[]{:S(2)}) collective-permute-start(f32[256,384]{1,0:T(8,128)S(1)} %collective-permute-done.2.refs_10_), channel_id=1, source_target_pairs={{0,4},{1,5},{4,8},{5,9},{8,12},{9,13},{12,14},{13,15},{14,10},{15,... | collective-permute-start | bytes 1179656 | tf_op jit(solution)/shard_map/ppermute | solution.py:453
  46.1 8.4 %shard_map.69 = (f32[512,384]{1,0:T(8,128)}, f32[512,384]{1,0:T(8,128)}) custom-call(s32[1]{0:T(128)} %bitcast.index_ref.core_ref, f32[6144,384]{1,0:T(8,128)} %refs_2_.12, f32[6144,384]{1,0:T(8,128)} %collective-permute-done.refs_1_.refs_3_, f32[6144,384]{1,0:T(8,128)} %refs_2_.12, f32[6144,384]{1,0:T(8,128)} %collective-permute-done.refs_1_.refs_3_, ...), custom_call_target="tpu_custom_call" | custom-call | flops 1 | bytes 1 | tf_op jit(solution)/shard_map/pallas_call | solution.py:294
  54.6 6.6 %collective-permute-done.6.refs_7_ = f32[256,384]{1,0:T(8,128)S(1)} collective-permute-done((f32[256,384]{1,0:T(8,128)S(1)}, f32[256,384]{1,0:T(8,128)S(1)}, u32[]{:S(2)}, u32[]{:S(2)}) %collective-permute-start.6) | collective-permute-done | bytes 393248 | tf_op jit(solution)/shard_map/ppermute | solution.py:453
  65.3 5.7 %shard_map.70 = (f32[512,384]{1,0:T(8,128)}, f32[512,384]{1,0:T(8,128)}) custom-call(s32[1]{0:T(128)} %bitcast.index_ref.core_ref, f32[6144,384]{1,0:T(8,128)} %refs_2_.12, f32[6144,384]{1,0:T(8,128)} %collective-permute-done.refs_1_.refs_3_, f32[6144,384]{1,0:T(8,128)} %refs_2_.12, f32[6144,384]{1,0:T(8,128)} %collective-permute-done.refs_1_.refs_3_, ...), custom_call_target="tpu_custom_call" | custom-call | flops 1 | bytes 1 | tf_op jit(solution)/shard_map/pallas_call | solution.py:294
  71.0 2.2 %collective-permute-done.16.refs_7_ = f32[256,384]{1,0:T(8,128)S(1)} collective-permute-done((f32[256,384]{1,0:T(8,128)S(1)}, f32[256,384]{1,0:T(8,128)S(1)}, u32[]{:S(2)}, u32[]{:S(2)}) %collective-permute-start.16) | collective-permute-done | bytes 393248 | tf_op jit(solution)/shard_map/ppermute | solution.py:453
  75.5 7.6 %shard_map.71 = (f32[512,384]{1,0:T(8,128)}, f32[512,384]{1,0:T(8,128)}, f32[2304,128]{1,0:T(8,128)}) custom-call(s32[1]{0:T(128)} %bitcast.index_ref.core_ref, f32[6144,384]{1,0:T(8,128)} %refs_2_.12, f32[6144,384]{1,0:T(8,128)} %collective-permute-done.refs_1_.refs_3_, f32[6144,384]{1,0:T(8,128)} %refs_2_.12, ...), custom_call_target="tpu_custom_call" | custom-call | flops 1 | bytes 1 | tf_op jit(solution)/shard_map/pallas_call | solution.py:294
  88.7 8.5 %collective-permute-done.18.refs_7_ = f32[256,384]{1,0:T(8,128)} collective-permute-done((f32[256,384]{1,0:T(8,128)}, f32[256,384]{1,0:T(8,128)}, u32[]{:S(2)}, u32[]{:S(2)}) %collective-permute-start.18) | collective-permute-done | bytes 393248 | tf_op jit(solution)/shard_map/ppermute | solution.py:453
  97.3 5.6 %shard_map.72 = (f32[256,384]{1,0:T(8,128)}, f32[256,384]{1,0:T(8,128)}) custom-call(s32[1]{0:T(128)} %bitcast.index_ref.core_ref, f32[6144,384]{1,0:T(8,128)} %refs_2_.12, f32[6144,384]{1,0:T(8,128)} %collective-permute-done.refs_1_.refs_3_, f32[6144,384]{1,0:T(8,128)} %refs_2_.12, f32[6144,384]{1,0:T(8,128)} %collective-permute-done.refs_1_.refs_3_, ...), custom_call_target="tpu_custom_call" | custom-call | flops 1 | bytes 1 | tf_op jit(solution)/shard_map/pallas_call | solution.py:294
  102.9 2.0 %collective-permute-start.22 = (f32[256,384]{1,0:T(8,128)S(1)}, f32[256,384]{1,0:T(8,128)S(1)}, u32[]{:S(2)}, u32[]{:S(2)}) collective-permute-start(f32[256,384]{1,0:T(8,128)S(1)} %collective-permute-done.19.refs_4_), channel_id=1, source_target_pairs={{4,0},{5,1},{8,4},{9,5},{12,8},{13,9},{14,12},{15,13},{10,14},{11,... | collective-permute-start | bytes 1179656 | tf_op jit(solution)/shard_map/ppermute | solution.py:453
  105.1 4.1 %collective-permute-start.27 = (f32[144,128]{1,0:T(8,128)S(1)}, f32[144,128]{1,0:T(8,128)S(1)}, u32[]{:S(2)}, u32[]{:S(2)}) collective-permute-start(f32[144,128]{1,0:T(8,128)S(1)} %get-tuple-element.105), channel_id=1, source_target_pairs={{0,8},{1,9},{2,10},{3,11},{4,12},{5,13},{6,14},{7,15},{8,0},{9,1},... | collective-permute-start | bytes 221192 | tf_op jit(solution)/shard_map/ppermute | solution.py:453
  110.2 4.3 %shard_map.74.columns_ref = f32[384,768]{1,0:T(8,128)} custom-call(f32[512,384]{1,0:T(8,128)} %get-tuple-element.81.image_ref, f32[512,384]{1,0:T(8,128)} %copy-done.5, f32[768,768]{1,0:T(8,128)} %refs_2_.13), custom_call_target="tpu_custom_call" | custom-call | flops 1 | bytes 1 | tf_op jit(solution)/shard_map/pallas_call | solution.py:329
  115.2 4.1 %shard_map.73 = (f32[256,384]{1,0:T(8,128)}, f32[256,384]{1,0:T(8,128)}) custom-call(s32[1]{0:T(128)} %bitcast.index_ref.core_ref, f32[6144,384]{1,0:T(8,128)} %refs_2_.12, f32[6144,384]{1,0:T(8,128)} %collective-permute-done.refs_1_.refs_3_, f32[6144,384]{1,0:T(8,128)} %refs_2_.12, f32[6144,384]{1,0:T(8,128)} %collective-permute-done.refs_1_.refs_3_, ...), custom_call_target="tpu_custom_call" | custom-call | flops 1 | bytes 1 | tf_op jit(solution)/shard_map/pallas_call | solution.py:294
  122.0 2.9 %collective-permute-start.32 = (f32[144,128]{1,0:T(8,128)S(1)}, f32[144,128]{1,0:T(8,128)S(1)}, u32[]{:S(2)}, u32[]{:S(2)}) collective-permute-start(f32[144,128]{1,0:T(8,128)S(1)} %fusion.3), channel_id=1, source_target_pairs={{0,8},{1,9},{2,10},{3,11},{4,12},{5,13},{6,14},{7,15},{8,0},{9,1},... | collective-permute-start | bytes 221192 | tf_op jit(solution)/shard_map/ppermute | solution.py:453
  126.6 2.0 %collective-permute-start.25 = (f32[128,384]{1,0:T(8,128)S(1)}, f32[128,384]{1,0:T(8,128)S(1)}, u32[]{:S(2)}, u32[]{:S(2)}) collective-permute-start(f32[128,384]{1,0:T(8,128)S(1)} %slice.9), channel_id=1, source_target_pairs={{4,0},{5,1},{8,4},{9,5},{12,8},{13,9},{14,12},{15,13},{10,14},{11,... | collective-permute-start | bytes 589832 | tf_op jit(solution)/shard_map/ppermute | solution.py:453
  128.8 2.4 %collective-permute-done.33 = f32[144,128]{1,0:T(8,128)S(1)} collective-permute-done((f32[144,128]{1,0:T(8,128)S(1)}, f32[144,128]{1,0:T(8,128)S(1)}, u32[]{:S(2)}, u32[]{:S(2)}) %collective-permute-start.33) | collective-permute-done | bytes 73760 | tf_op jit(solution)/shard_map/ppermute | solution.py:453
  131.4 2.2 %collective-permute-done.24.refs_5_ = f32[128,384]{1,0:T(8,128)S(1)} collective-permute-done((f32[128,384]{1,0:T(8,128)S(1)}, f32[128,384]{1,0:T(8,128)S(1)}, u32[]{:S(2)}, u32[]{:S(2)}) %collective-permute-start.24) | collective-permute-done | bytes 196640 | tf_op jit(solution)/shard_map/ppermute | solution.py:453
  135.0 4.8 %shard_map.75 = (f32[256,384]{1,0:T(8,128)}, f32[256,384]{1,0:T(8,128)}, f32[384,128]{1,0:T(8,128)}) custom-call(s32[1]{0:T(128)} %bitcast.index_ref.core_ref, f32[6144,384]{1,0:T(8,128)} %refs_2_.12, f32[6144,384]{1,0:T(8,128)} %collective-permute-done.refs_1_.refs_3_, f32[6144,384]{1,0:T(8,128)} %refs_2_.12, ...), custom_call_target="tpu_custom_call" | custom-call | flops 1 | bytes 1 | tf_op jit(solution)/shard_map/pallas_call | solution.py:294
  143.0 4.5 %collective-permute-done.35 = f32[192,128]{1,0:T(8,128)S(1)} collective-permute-done((f32[192,128]{1,0:T(8,128)S(1)}, f32[192,128]{1,0:T(8,128)S(1)}, u32[]{:S(2)}, u32[]{:S(2)}) %collective-permute-start.35) | collective-permute-done | bytes 98336 | tf_op jit(solution)/shard_map/ppermute | solution.py:453
  147.8 2.1 %collective-permute-start.38 = (f32[192,128]{1,0:T(8,128)S(1)}, f32[192,128]{1,0:T(8,128)S(1)}, u32[]{:S(2)}, u32[]{:S(2)}) collective-permute-start(f32[192,128]{1,0:T(8,128)S(1)} %add.98), channel_id=1, source_target_pairs={{0,8},{1,9},{2,10},{3,11},{4,12},{5,13},{6,14},{7,15},{8,0},{9,1},... | collective-permute-start | bytes 294920 | tf_op jit(solution)/shard_map/ppermute | solution.py:453
  149.9 2.0 %collective-permute-start.39 = (f32[192,128]{1,0:T(8,128)S(1)}, f32[192,128]{1,0:T(8,128)S(1)}, u32[]{:S(2)}, u32[]{:S(2)}) collective-permute-start(f32[192,128]{1,0:T(8,128)S(1)} %add.98), channel_id=1, source_target_pairs={{0,12},{1,13},{2,14},{3,15},{4,8},{5,9},{6,10},{7,11},{8,4},{9,5},... | collective-permute-start | bytes 294920 | tf_op jit(solution)/shard_map/ppermute | solution.py:453
  151.9 5.7 %shard_map.76.base_ref = f32[768,768]{1,0:T(8,128)} custom-call(s32[1]{0:T(128)} %bitcast.index_ref.core_ref, f32[1152,128]{1,0:T(8,128)} %copy-done.1, f32[1152,128]{1,0:T(8,128)} %copy-done.6, f32[768,768]{1,0:T(8,128)} %refs_2_.13, f32[3,256,256]{2,1,0:T(8,128)} %refs_3_.1), custom_call_target="tpu_custom_call" | custom-call | flops 1 | bytes 1 | tf_op jit(solution)/shard_map/pallas_call | solution.py:420
  160.3 2.4 %shard_map.77 = (f32[384,768]{1,0:T(8,128)}, f32[768,768]{1,0:T(8,128)}) custom-call(s32[1]{0:T(128)} %bitcast.index_ref.core_ref, f32[192,128]{1,0:T(8,128)} %copy-done.22, f32[192,128]{1,0:T(8,128)} %copy-done.27, f32[256,384]{1,0:T(8,128)} %get-tuple-element.96.image_ref, f32[256,384]{1,0:T(8,128)} %copy-done.21, ...), custom_call_target="tpu_custom_call", output_to_operand_aliasing={{0}: (5, {}), {1}: (6, {})} | custom-call | flops 1 | bytes 1 | tf_op jit(solution)/shard_map/pallas_call | solution.py:367
  (138 shorter events, 29.1 us)
Async XLA Ops:
  0.6 45.0 %collective-permute-start = (f32[6144,384]{1,0:T(8,128)}, f32[6144,384]{1,0:T(8,128)}, u32[]{:S(2)}, u32[]{:S(2)}) collective-permute-start(f32[6144,384]{1,0:T(8,128)} %refs_2_.12), channel_id=1, source_target_pairs={{0,1},{1,0},{2,3},{3,2},{4,5},{5,4},{6,7},{7,6},{8,9},{9,8},{10,11... | collective-permute-start | bytes 28311560 | tf_op jit(solution)/shard_map/ppermute | solution.py:453
  4.0 12.7 %collective-permute-start.1 = (f32[256,384]{1,0:T(8,128)}, f32[256,384]{1,0:T(8,128)S(1)}, u32[]{:S(2)}, u32[]{:S(2)}) collective-permute-start(f32[256,384]{1,0:T(8,128)} %get-tuple-element.52.refs_4_), channel_id=1, source_target_pairs={{0,4},{1,5},{4,8},{5,9},{8,12},{9,13},{12,14},{13,15},{14,10},{15,... | collective-permute-start | bytes 1179656 | tf_op jit(solution)/shard_map/ppermute | solution.py:453
  6.6 12.2 %collective-permute-start.10 = (f32[256,384]{1,0:T(8,128)}, f32[256,384]{1,0:T(8,128)S(1)}, u32[]{:S(2)}, u32[]{:S(2)}) collective-permute-start(f32[256,384]{1,0:T(8,128)} %get-tuple-element.53.refs_5_), channel_id=1, source_target_pairs={{4,0},{5,1},{8,4},{9,5},{12,8},{13,9},{14,12},{15,13},{10,14},{11,... | collective-permute-start | bytes 1179656 | tf_op jit(solution)/shard_map/ppermute | solution.py:453
  6.6 18.5 %collective-permute-start.4 = (f32[256,384]{1,0:T(8,128)}, f32[256,384]{1,0:T(8,128)S(1)}, u32[]{:S(2)}, u32[]{:S(2)}) collective-permute-start(f32[256,384]{1,0:T(8,128)} %get-tuple-element.53.refs_5_), channel_id=1, source_target_pairs={{0,4},{1,5},{4,8},{5,9},{8,12},{9,13},{12,14},{13,15},{14,10},{15,... | collective-permute-start | bytes 1179656 | tf_op jit(solution)/shard_map/ppermute | solution.py:453
  8.6 18.6 %collective-permute-start.7 = (f32[256,384]{1,0:T(8,128)}, f32[256,384]{1,0:T(8,128)S(1)}, u32[]{:S(2)}, u32[]{:S(2)}) collective-permute-start(f32[256,384]{1,0:T(8,128)} %get-tuple-element.52.refs_4_), channel_id=1, source_target_pairs={{4,0},{5,1},{8,4},{9,5},{12,8},{13,9},{14,12},{15,13},{10,14},{11,... | collective-permute-start | bytes 1179656 | tf_op jit(solution)/shard_map/ppermute | solution.py:453
  16.7 16.9 %collective-permute-start.2 = (f32[256,384]{1,0:T(8,128)S(1)}, f32[256,384]{1,0:T(8,128)S(1)}, u32[]{:S(2)}, u32[]{:S(2)}) collective-permute-start(f32[256,384]{1,0:T(8,128)S(1)} %collective-permute-done.1.refs_6_), channel_id=1, source_target_pairs={{0,4},{1,5},{4,8},{5,9},{8,12},{9,13},{12,14},{13,15},{14,10},{15,... | collective-permute-start | bytes 1179656 | tf_op jit(solution)/shard_map/ppermute | solution.py:453
  18.8 16.9 %collective-permute-start.11 = (f32[256,384]{1,0:T(8,128)S(1)}, f32[256,384]{1,0:T(8,128)S(1)}, u32[]{:S(2)}, u32[]{:S(2)}) collective-permute-start(f32[256,384]{1,0:T(8,128)S(1)} %collective-permute-done.10.refs_9_), channel_id=1, source_target_pairs={{4,0},{5,1},{8,4},{9,5},{12,8},{13,9},{14,12},{15,13},{10,14},{11,... | collective-permute-start | bytes 1179656 | tf_op jit(solution)/shard_map/ppermute | solution.py:453
  25.1 16.6 %collective-permute-start.5 = (f32[256,384]{1,0:T(8,128)S(1)}, f32[256,384]{1,0:T(8,128)S(1)}, u32[]{:S(2)}, u32[]{:S(2)}) collective-permute-start(f32[256,384]{1,0:T(8,128)S(1)} %collective-permute-done.4.refs_7_), channel_id=1, source_target_pairs={{0,4},{1,5},{4,8},{5,9},{8,12},{9,13},{12,14},{13,15},{14,10},{15,... | collective-permute-start | bytes 1179656 | tf_op jit(solution)/shard_map/ppermute | solution.py:453
  27.2 16.9 %collective-permute-start.8 = (f32[256,384]{1,0:T(8,128)S(1)}, f32[256,384]{1,0:T(8,128)S(1)}, u32[]{:S(2)}, u32[]{:S(2)}) collective-permute-start(f32[256,384]{1,0:T(8,128)S(1)} %collective-permute-done.7.refs_8_), channel_id=1, source_target_pairs={{4,0},{5,1},{8,4},{9,5},{12,8},{13,9},{14,12},{15,13},{10,14},{11,... | collective-permute-start | bytes 1179656 | tf_op jit(solution)/shard_map/ppermute | solution.py:453
  33.6 37.4 %collective-permute-start.17 = (f32[384,768]{1,0:T(8,128)}, f32[384,768]{1,0:T(8,128)S(1)}, u32[]{:S(2)}, u32[]{:S(2)}) collective-permute-start(f32[384,768]{1,0:T(8,128)} %get-tuple-element.67.refs_10_.refs_9_), channel_id=1, source_target_pairs={{0,1},{1,0},{2,3},{3,2},{4,5},{5,4},{6,7},{7,6},{8,9},{9,8},{10,11... | collective-permute-start | bytes 3538952 | tf_op jit(solution)/shard_map/ppermute | solution.py:453
  35.6 18.9 %collective-permute-start.12 = (f32[256,384]{1,0:T(8,128)S(1)}, f32[256,384]{1,0:T(8,128)S(1)}, u32[]{:S(2)}, u32[]{:S(2)}) collective-permute-start(f32[256,384]{1,0:T(8,128)S(1)} %collective-permute-done.11.refs_5_), channel_id=1, source_target_pairs={{4,0},{5,1},{8,4},{9,5},{12,8},{13,9},{14,12},{15,13},{10,14},{11,... | collective-permute-start | bytes 1179656 | tf_op jit(solution)/shard_map/ppermute | solution.py:453
  41.8 12.8 %collective-permute-start.3 = (f32[256,384]{1,0:T(8,128)S(1)}, f32[256,384]{1,0:T(8,128)S(1)}, u32[]{:S(2)}, u32[]{:S(2)}) collective-permute-start(f32[256,384]{1,0:T(8,128)S(1)} %collective-permute-done.2.refs_10_), channel_id=1, source_target_pairs={{0,4},{1,5},{4,8},{5,9},{8,12},{9,13},{12,14},{13,15},{14,10},{15,... | collective-permute-start | bytes 1179656 | tf_op jit(solution)/shard_map/ppermute | solution.py:453
  44.1 17.1 %collective-permute-start.6 = (f32[256,384]{1,0:T(8,128)S(1)}, f32[256,384]{1,0:T(8,128)S(1)}, u32[]{:S(2)}, u32[]{:S(2)}) collective-permute-start(f32[256,384]{1,0:T(8,128)S(1)} %collective-permute-done.5.refs_11_), channel_id=1, source_target_pairs={{0,4},{1,5},{4,8},{5,9},{8,12},{9,13},{12,14},{13,15},{14,10},{15,... | collective-permute-start | bytes 1179656 | tf_op jit(solution)/shard_map/ppermute | solution.py:453
  45.6 15.5 %collective-permute-start.9 = (f32[256,384]{1,0:T(8,128)S(1)}, f32[256,384]{1,0:T(8,128)S(1)}, u32[]{:S(2)}, u32[]{:S(2)}) collective-permute-start(f32[256,384]{1,0:T(8,128)S(1)} %collective-permute-done.8.refs_4_), channel_id=1, source_target_pairs={{4,0},{5,1},{8,4},{9,5},{12,8},{13,9},{14,12},{15,13},{10,14},{11,... | collective-permute-start | bytes 1179656 | tf_op jit(solution)/shard_map/ppermute | solution.py:453
  61.1 12.1 %collective-permute-start.16 = (f32[256,384]{1,0:T(8,128)S(1)}, f32[256,384]{1,0:T(8,128)S(1)}, u32[]{:S(2)}, u32[]{:S(2)}) collective-permute-start(f32[256,384]{1,0:T(8,128)S(1)} %collective-permute-done.12.refs_5_), channel_id=1, source_target_pairs={{4,0},{5,1},{8,4},{9,5},{12,8},{13,9},{14,12},{15,13},{10,14},{11,... | collective-permute-start | bytes 1179656 | tf_op jit(solution)/shard_map/ppermute | solution.py:453
  62.7 12.1 %collective-permute-start.15 = (f32[256,384]{1,0:T(8,128)S(1)}, f32[256,384]{1,0:T(8,128)S(1)}, u32[]{:S(2)}, u32[]{:S(2)}) collective-permute-start(f32[256,384]{1,0:T(8,128)S(1)} %collective-permute-done.3.refs_6_), channel_id=1, source_target_pairs={{0,4},{1,5},{4,8},{5,9},{8,12},{9,13},{12,14},{13,15},{14,10},{15,... | collective-permute-start | bytes 1179656 | tf_op jit(solution)/shard_map/ppermute | solution.py:453
  63.2 20.0 %collective-permute-start.13 = (f32[256,384]{1,0:T(8,128)}, f32[256,384]{1,0:T(8,128)}, u32[]{:S(2)}, u32[]{:S(2)}) collective-permute-start(f32[256,384]{1,0:T(8,128)} %get-tuple-element.58.refs_4_), channel_id=1, source_target_pairs={{0,4},{1,5},{4,8},{5,9},{8,12},{9,13},{12,14},{13,15},{14,10},{15,... | collective-permute-start | bytes 1179656 | tf_op jit(solution)/shard_map/ppermute | solution.py:453
  64.8 18.3 %collective-permute-start.14 = (f32[256,384]{1,0:T(8,128)}, f32[256,384]{1,0:T(8,128)}, u32[]{:S(2)}, u32[]{:S(2)}) collective-permute-start(f32[256,384]{1,0:T(8,128)} %get-tuple-element.58.refs_4_), channel_id=1, source_target_pairs={{4,0},{5,1},{8,4},{9,5},{12,8},{13,9},{14,12},{15,13},{10,14},{11,... | collective-permute-start | bytes 1179656 | tf_op jit(solution)/shard_map/ppermute | solution.py:453
  84.5 24.7 %collective-permute-start.29 = (f32[512,384]{1,0:T(8,128)}, f32[512,384]{1,0:T(8,128)S(1)}, u32[]{:S(2)}, u32[]{:S(2)}) collective-permute-start(f32[512,384]{1,0:T(8,128)} %get-tuple-element.82), channel_id=1, source_target_pairs={{0,1},{1,0},{2,3},{3,2},{4,5},{5,4},{6,7},{7,6},{8,9},{9,8},{10,11... | collective-permute-start | bytes 2359304 | tf_op jit(solution)/shard_map/ppermute | solution.py:453
  85.0 12.3 %collective-permute-start.18 = (f32[256,384]{1,0:T(8,128)}, f32[256,384]{1,0:T(8,128)}, u32[]{:S(2)}, u32[]{:S(2)}) collective-permute-start(f32[256,384]{1,0:T(8,128)} %collective-permute-done.13.refs_5_), channel_id=1, source_target_pairs={{0,4},{1,5},{4,8},{5,9},{8,12},{9,13},{12,14},{13,15},{14,10},{15,... | collective-permute-start | bytes 1179656 | tf_op jit(solution)/shard_map/ppermute | solution.py:453
  85.5 17.4 %collective-permute-start.19 = (f32[256,384]{1,0:T(8,128)}, f32[256,384]{1,0:T(8,128)S(1)}, u32[]{:S(2)}, u32[]{:S(2)}) collective-permute-start(f32[256,384]{1,0:T(8,128)} %collective-permute-done.14.refs_6_), channel_id=1, source_target_pairs={{4,0},{5,1},{8,4},{9,5},{12,8},{13,9},{14,12},{15,13},{10,14},{11,... | collective-permute-start | bytes 1179656 | tf_op jit(solution)/shard_map/ppermute | solution.py:453
  87.1 15.7 %collective-permute-start.21 = (f32[576,128]{1,0:T(8,128)S(1)}, f32[576,128]{1,0:T(8,128)S(1)}, u32[]{:S(2)}, u32[]{:S(2)}) collective-permute-start(f32[576,128]{1,0:T(8,128)S(1)} %dynamic-slice_bitcast_fusion.1), channel_id=1, source_target_pairs={{0,2},{1,3},{2,0},{3,1},{4,6},{5,7},{6,4},{7,5},{8,10},{9,11},{10,... | collective-permute-start | bytes 884744 | tf_op jit(solution)/shard_map/ppermute | solution.py:453
  102.9 11.6 %collective-permute-start.23 = (f32[256,384]{1,0:T(8,128)}, f32[256,384]{1,0:T(8,128)S(1)}, u32[]{:S(2)}, u32[]{:S(2)}) collective-permute-start(f32[256,384]{1,0:T(8,128)} %collective-permute-done.18.refs_7_), channel_id=1, source_target_pairs={{0,4},{1,5},{4,8},{5,9},{8,12},{9,13},{12,14},{13,15},{14,10},{15,... | collective-permute-start | bytes 1179656 | tf_op jit(solution)/shard_map/ppermute | solution.py:453
  102.9 23.6 %collective-permute-start.22 = (f32[256,384]{1,0:T(8,128)S(1)}, f32[256,384]{1,0:T(8,128)S(1)}, u32[]{:S(2)}, u32[]{:S(2)}) collective-permute-start(f32[256,384]{1,0:T(8,128)S(1)} %collective-permute-done.19.refs_4_), channel_id=1, source_target_pairs={{4,0},{5,1},{8,4},{9,5},{12,8},{13,9},{14,12},{15,13},{10,14},{11,... | collective-permute-start | bytes 1179656 | tf_op jit(solution)/shard_map/ppermute | solution.py:453
  105.0 14.3 %collective-permute-start.26 = (f32[144,128]{1,0:T(8,128)S(1)}, f32[144,128]{1,0:T(8,128)S(1)}, u32[]{:S(2)}, u32[]{:S(2)}) collective-permute-start(f32[144,128]{1,0:T(8,128)S(1)} %get-tuple-element.106), channel_id=1, source_target_pairs={{0,4},{1,5},{2,6},{3,7},{4,0},{5,1},{6,2},{7,3},{8,12},{9,13},{10,... | collective-permute-start | bytes 221192 | tf_op jit(solution)/shard_map/ppermute | solution.py:453
  105.1 14.2 %collective-permute-start.27 = (f32[144,128]{1,0:T(8,128)S(1)}, f32[144,128]{1,0:T(8,128)S(1)}, u32[]{:S(2)}, u32[]{:S(2)}) collective-permute-start(f32[144,128]{1,0:T(8,128)S(1)} %get-tuple-element.105), channel_id=1, source_target_pairs={{0,8},{1,9},{2,10},{3,11},{4,12},{5,13},{6,14},{7,15},{8,0},{9,1},... | collective-permute-start | bytes 221192 | tf_op jit(solution)/shard_map/ppermute | solution.py:453
  109.2 11.8 %collective-permute-start.28 = (f32[144,128]{1,0:T(8,128)S(1)}, f32[144,128]{1,0:T(8,128)S(1)}, u32[]{:S(2)}, u32[]{:S(2)}) collective-permute-start(f32[144,128]{1,0:T(8,128)S(1)} %get-tuple-element.104), channel_id=1, source_target_pairs={{0,12},{1,13},{2,14},{3,15},{4,8},{5,9},{6,10},{7,11},{8,4},{9,5},... | collective-permute-start | bytes 221192 | tf_op jit(solution)/shard_map/ppermute | solution.py:453
  121.1 7.6 %collective-permute-start.31 = (f32[144,128]{1,0:T(8,128)S(1)}, f32[144,128]{1,0:T(8,128)S(1)}, u32[]{:S(2)}, u32[]{:S(2)}) collective-permute-start(f32[144,128]{1,0:T(8,128)S(1)} %fusion.3), channel_id=1, source_target_pairs={{0,4},{1,5},{2,6},{3,7},{4,0},{5,1},{6,2},{7,3},{8,12},{9,13},{10,... | collective-permute-start | bytes 221192 | tf_op jit(solution)/shard_map/ppermute | solution.py:453
  131.3 10.7 %collective-permute-start.34 = (f32[576,128]{1,0:T(8,128)S(1)}, f32[576,128]{1,0:T(8,128)S(1)}, u32[]{:S(2)}, u32[]{:S(2)}) collective-permute-start(f32[576,128]{1,0:T(8,128)S(1)} %pad_maximum_fusion.1), channel_id=1, source_target_pairs={{0,2},{1,3},{2,0},{3,1},{4,6},{5,7},{6,4},{7,5},{8,10},{9,11},{10,... | collective-permute-start | bytes 884744 | tf_op jit(solution)/shard_map/ppermute | solution.py:453
  147.5 10.1 %collective-permute-start.37 = (f32[192,128]{1,0:T(8,128)S(1)}, f32[192,128]{1,0:T(8,128)S(1)}, u32[]{:S(2)}, u32[]{:S(2)}) collective-permute-start(f32[192,128]{1,0:T(8,128)S(1)} %add.98), channel_id=1, source_target_pairs={{0,4},{1,5},{2,6},{3,7},{4,0},{5,1},{6,2},{7,3},{8,12},{9,13},{10,... | collective-permute-start | bytes 294920 | tf_op jit(solution)/shard_map/ppermute | solution.py:453
  147.8 10.4 %collective-permute-start.38 = (f32[192,128]{1,0:T(8,128)S(1)}, f32[192,128]{1,0:T(8,128)S(1)}, u32[]{:S(2)}, u32[]{:S(2)}) collective-permute-start(f32[192,128]{1,0:T(8,128)S(1)} %add.98), channel_id=1, source_target_pairs={{0,8},{1,9},{2,10},{3,11},{4,12},{5,13},{6,14},{7,15},{8,0},{9,1},... | collective-permute-start | bytes 294920 | tf_op jit(solution)/shard_map/ppermute | solution.py:453
  149.9 8.3 %collective-permute-start.39 = (f32[192,128]{1,0:T(8,128)S(1)}, f32[192,128]{1,0:T(8,128)S(1)}, u32[]{:S(2)}, u32[]{:S(2)}) collective-permute-start(f32[192,128]{1,0:T(8,128)S(1)} %add.98), channel_id=1, source_target_pairs={{0,12},{1,13},{2,14},{3,15},{4,8},{5,9},{6,10},{7,11},{8,4},{9,5},... | collective-permute-start | bytes 294920 | tf_op jit(solution)/shard_map/ppermute | solution.py:453
  (39 other events, 294.2 us)
